TPU v7x, 32 devices: a whole 2x2x4 slice. The times are simulated.
32 devices in a mesh: row: 2 (over x), col: 8 (over z, y), layer: 2 (over core).
Axes of the slice: x: 2, y: 2, z: 4, core: 2. Of those that a mesh axis runs over, the one named last changes fastest.
Arguments:
- flow: float32 [2048, 2048], P('row', ('col', 'layer')), as said below
- pattern: int32 [4, 4], replicated, may hold values from 0 to 1, as said below
- prune_level: int32 [4], replicated, may hold values from 1 to 8
- power: int32 [4], replicated, may hold values from 1 to 4
Outputs:
- pruned: float32 [2048, 2048], P('row', ('col', 'layer'))
Inputs may be any that keep to these rules, and one draw needn't show every extreme that they name: pattern holds 0 or 1 and its diagonal is all 1; in every draw, all block rows that meet the 1024 rows of one index of row are all 1, and all block columns that meet the columns of one index of col are all 1. flow is positive.
All inputs are finite; a program needn't handle non-finite values.
Results may differ from a plain program's by a relative error of at most 0.00018.
Values sent between devices are 32-bit elements; how exact they have to be, the bound alone decides.
No kernel may reach another device: no remote copies, remote signals or barrier semaphores. Data moves between devices by JAX's collectives and lax.ppermute only.
A program may use at most 128 MiB of HBM per device.

v0:
```python
import jax
import jax.numpy as jnp
from jax import lax
from jax.sharding import PartitionSpec as P


def multiply(left, right):
    exact = lax.Precision.HIGHEST
    return jnp.dot(left, right, precision=exact, preferred_element_type=jnp.float32)


def on_device(flow, pattern, prune_level, power):
    rows, width = flow.shape
    layers = lax.axis_size("layer")
    order = rows * lax.axis_size("row")
    blocks = pattern.shape[0]
    tile_edge = order // blocks
    row_start = lax.axis_index("row") * rows
    col_start = (lax.axis_index("col") * layers + lax.axis_index("layer")) * width
    block_ids = jnp.arange(blocks, dtype=jnp.int32)
    row_ids = (row_start + jnp.arange(rows, dtype=jnp.int32)) // tile_edge
    col_ids = (col_start + jnp.arange(width, dtype=jnp.int32)) // tile_edge
    row_onehot = (row_ids[:, None] == block_ids[None, :]).astype(jnp.float32)
    col_onehot = (block_ids[:, None] == col_ids[None, :]).astype(jnp.float32)
    exact = lax.Precision.HIGHEST
    chosen = jnp.dot(
        jnp.dot(row_onehot, pattern.astype(jnp.float32), precision=exact),
        col_onehot,
        precision=exact,
    )
    masked = flow * chosen
    groups = rows // (layers * width)
    parted = masked.reshape(groups, layers, width, width)
    swapped = lax.all_to_all(parted, "layer", split_axis=1, concat_axis=3, tiled=True)
    inner_rows = swapped.reshape(groups * width, layers * width)
    strip = lax.all_gather(masked, "col", axis=1, tiled=True)
    partial_value = multiply(strip, lax.all_gather(inner_rows, "row", axis=0, tiled=True))
    expanded = lax.psum_scatter(partial_value, "layer", scatter_dimension=1, tiled=True)
    exponents = jnp.dot(power.astype(jnp.float32)[None, :], col_onehot, precision=exact)[0]
    inflated = jnp.power(expanded, exponents[None, :])
    totals = lax.psum(jnp.sum(inflated, axis=0), "row")
    levels = jnp.dot(prune_level.astype(jnp.float32)[None, :], col_onehot, precision=exact)[0] / 8.0
    return jnp.maximum(order * inflated / totals[None, :] - levels[None, :], 0.0)


def solution(mesh):
    return jax.shard_map(
        on_device,
        mesh=mesh,
        in_specs=(P("row", ("col", "layer")), P(), P(), P()),
        out_specs=P("row", ("col", "layer")),
        check_vma=False,
    )
```

profile of v0, /device:TPU:0, one launch (start us, length us, event | category | flops | bytes accessed | tf_op | source)
XLA Modules:
  0.0 145.4 jit_solution(2533182909635452199)
XLA Ops:
  6.5 0.0 all-gather.5.cloned.1.call-start
  6.6 1.1 fusion.1
  7.7 1.7 %convolution_multiply_fusion = f32[1024,128]{1,0:T(8,128)S(1)} fusion(f32[1024,128]{1,0:T(8,128)} %param.4, f32[1024,4]{0,1:T(4,128)S(1)} %fusion.1, s32[128]{0:T(128)S(1)} %and_select_fusion), kind=kOutput, calls=%fused_computation | convolution fusion | flops 6423040 | bytes 1065472 | tf_op jit(solution)/shard_map/dot_general | solution.py:26
  9.4 0.0 copy-start
  9.4 4.2 %all_to_all.15 = f32[4,2,128,128]{3,2,0,1:T(8,128)S(1)} all-to-all(f32[4,2,128,128]{3,2,0,1:T(8,128)S(1)} %copy.6), channel_id=1, replica_groups=mesh['row'=2,'col'=8,'layer'=2] {'layer'}, dimensions={1} | all-to-all | bytes 1048576 | tf_op jit(solution)/shard_map/all_to_all | solution.py:34
  13.6 0.4 copy.7
  14.0 0.9 copy.10
  14.8 0.0 copy-start.1
  14.8 0.0 copy-start.2
  14.9 0.0 all-gather.5.cloned.1.call-update
  14.9 0.0 all-gather.3.cloned.1.call-start
  14.9 0.0 copy-done
  14.9 0.7 all-gather.3.cloned.1.call-update
  15.6 0.0 reduce-scatter.2.cloned.1.call-start
  15.7 23.4 %all-gather.5.cloned.1.call-done = f32[1024,256]{1,0:T(8,128)} async-done(((f32[512,256]{1,0:T(8,128)}), f32[1024,256]{1,0:T(8,128)}) %all-gather.5.cloned.1.call-update) | async-done | bytes 1048592 | tf_op jit(solution)/shard_map/all_gather | solution.py:37
  39.0 77.1 %all-gather.3.cloned.1.call-done = f32[1024,1024]{1,0:T(8,128)} async-done(((f32[1024,128]{1,0:T(8,128)}), f32[1024,1024]{1,0:T(8,128)}) %all-gather.3.cloned.1.call-update) | async-done | bytes 4194320 | tf_op jit(solution)/shard_map/all_gather | solution.py:36
  116.1 6.9 %fusion.10 = f32[1024,256]{1,0:T(8,128)} fusion(f32[1024,1024]{1,0:T(8,128)} %all-gather.3.cloned.1.call-done, f32[1024,256]{1,0:T(8,128)} %all-gather.5.cloned.1.call-done), kind=kOutput, calls=%fused_computation.30 | convolution fusion | flops 3221225472 | bytes 6291456 | tf_op jit(solution)/shard_map/dot_general | solution.py:9
  123.0 0.0 reduce-scatter.2.cloned.1.call-update
  123.1 0.0 copy-done.1
  123.1 0.1 convolution_bitcast_fusion.1
  123.2 0.0 copy-done.2
  123.2 0.1 fusion
  123.3 6.6 %reduce-scatter.2.cloned.1.call-done = f32[1024,128]{1,0:T(8,128)} async-done(((f32[1024,256]{1,0:T(8,128)}), f32[1024,128]{1,0:T(8,128)}) %reduce-scatter.2.cloned.1.call-update) | async-done | bytes 524304 | tf_op jit(solution)/shard_map/reduce_scatter | solution.py:38
  129.9 1.6 %power_reduce_fusion = f32[128]{0:T(128)S(1)} fusion(f32[1024,128]{1,0:T(8,128)} %reduce-scatter.2.cloned.1.call-done, f32[128]{0:T(128)S(1)} %convolution_bitcast_fusion.1), kind=kLoop, calls=%fused_computation.8 | loop fusion | flops 130944 | bytes 525312 | tf_op jit(solution)/shard_map/reduce_sum | solution.py:41
  131.5 4.9 %psum.7 = f32[128]{0:T(128)S(1)} all-reduce(f32[128]{0:T(128)S(1)} %power_reduce_fusion), channel_id=1, replica_groups=mesh['row'=2,'col'=8,'layer'=2] {'row'}, use_global_device_ids=true, to_apply=%region_2.3 | all-reduce | flops 128 | bytes 1024 | tf_op jit(solution)/shard_map/psum | solution.py:41
  136.5 2.4 %subtract_maximum_fusion = f32[1024,128]{1,0:T(8,128)} fusion(f32[1024,128]{1,0:T(8,128)} %reduce-scatter.2.cloned.1.call-done, f32[128]{0:T(128)S(1)} %fusion, f32[128]{0:T(128)S(1)} %psum.7, f32[128]{0:T(128)S(1)} %convolution_bitcast_fusion.1), kind=kLoop, calls=%fused_computation.5 | loop fusion | flops 524288 | bytes 1050112 | tf_op jit(solution)/shard_map/max | solution.py:43
  (3 shorter events, 0.1 us)
Async XLA Ops:
  6.5 32.5 %all-gather.5.cloned.1.call-start = ((), (), s32[]{:S(2)}) async-start(), calls=%async_computation.3 | async-start | bytes 1572864 | tf_op jit(solution)/shard_map/all_gather | solution.py:37
  9.4 5.6 %copy-start = (f32[1024,128]{1,0:T(8,128)}, f32[1024,128]{1,0:T(8,128)S(1)}, u32[]{:S(2)}) copy-start(f32[1024,128]{1,0:T(8,128)S(1)} %convolution_multiply_fusion) | copy-start | bytes 1572868
  14.8 108.2 %copy-start.1 = (s32[4]{0:T(128)S(1)}, s32[4]{0:T(128)}, u32[]{:S(2)}) copy-start(s32[4]{0:T(128)} %param.7) | copy-start | bytes 52
  14.8 108.3 %copy-start.2 = (s32[4]{0:T(128)S(1)}, s32[4]{0:T(128)}, u32[]{:S(2)}) copy-start(s32[4]{0:T(128)} %param.6) | copy-start | bytes 52
  14.9 101.3 %all-gather.3.cloned.1.call-start = ((), (), s32[]{:S(2)}) async-start(), calls=%async_computation.2 | async-start | bytes 4718592 | tf_op jit(solution)/shard_map/all_gather | solution.py:36
  15.6 114.3 %reduce-scatter.2.cloned.1.call-start = ((), (), s32[]{:S(2)}) async-start(), calls=%async_computation.4 | async-start | bytes 1572864 | tf_op jit(solution)/shard_map/reduce_scatter | solution.py:38
Sparse Core Ops, SparseCore 0:
  15.0 23.9 all-gather.4
  41.1 75.0 all-gather.2
  123.2 6.7 reduce-scatter.1
where the time goes:
time: 146 us; the launch traced here: 145 us
  waiting for transfers between devices  108 us (74%)
  between operations  13.2 us (9%)
  matrix products  9.94 us (7%)
  blocking collectives  9.09 us (6%)
  other arithmetic  4.05 us (3%)
    all_gather x1, waiting for transfers between devices, on_device(): strip = lax.all_gather(masked, 'col', axis=1, tiled=True)  77.1 us
    all_gather x1, waiting for transfers between devices, on_device(): lax.all_gather(inner_rows, 'row', axis=0, tiled=True)  23.4 us
    dot_general x1, matrix products, multiply(): jnp.dot(left, right, precision=exact, preferred_element_type=jnp.float32)  6.9 us
    reduce_scatter x1, waiting for transfers between devices, on_device(): lax.psum_scatter(partial_value, 'layer', scatter_dimension=1, tiled=True)  6.61 us
    psum x1, blocking collectives, on_device(): totals = lax.psum(jnp.sum(inflated, axis=0), 'row')  4.94 us
    all_to_all x1, blocking collectives, on_device(): lax.all_to_all(parted, 'layer', split_axis=1, concat_axis=3, tiled=True)  4.15 us
  transfers between devices with their start and end apart: 3, of which 3 were waited for; matrix products, arithmetic and copies ran while one was open for 0% of the time, Pallas kernels for 0%

commit v1 on v0

--- a/solution.py
+++ b/solution.py
@@ -5,11 +5,17 @@
 
 
 def multiply(left, right):
-    exact = lax.Precision.HIGHEST
-    return jnp.dot(left, right, precision=exact, preferred_element_type=jnp.float32)
+    return jnp.dot(left, right, precision=lax.Precision.HIGH, preferred_element_type=jnp.float32)
 
 
-def on_device(flow, pattern, prune_level, power):
+def raise_to(value, exponent):
+    square = value * value
+    low = jnp.where(exponent == 1, value, square)
+    high = square * jnp.where(exponent == 3, value, square)
+    return jnp.where(exponent <= 2, low, high)
+
+
+def general(flow, pattern, prune_level, power):
     rows, width = flow.shape
     layers = lax.axis_size("layer")
     order = rows * lax.axis_size("row")
@@ -43,9 +49,85 @@
     return jnp.maximum(order * inflated / totals[None, :] - levels[None, :], 0.0)
 
 
+def squared(flow, pattern, prune_level, power):
+    rows, width = flow.shape
+    half = rows // 2
+    order = rows * 2
+    x, c, l = lax.axis_index("row"), lax.axis_index("col"), lax.axis_index("layer")
+    y, z = c % 2, c // 2
+
+    def along_z(value, pairs):
+        return lax.ppermute(value, "col", [(2 * a + b, 2 * d + b) for a, d in pairs for b in range(2)])
+
+    def along_y(value):
+        return lax.ppermute(value, "col", [(i, i ^ 1) for i in range(8)])
+
+    def along_x(value):
+        return lax.ppermute(value, "row", [(0, 1), (1, 0)])
+
+    def across(value):
+        return lax.ppermute(value, "layer", [(0, 1), (1, 0)])
+
+    one = [(i, i ^ 1) for i in range(4)]
+    two = [(i, i ^ 2) for i in range(4)]
+    mid = [(1, 2), (2, 1)]
+    out = [(1, 0), (2, 3)]
+
+    own = lax.dynamic_slice_in_dim(flow, y * half, half, 0)
+    rest = lax.dynamic_slice_in_dim(flow, (1 - y) * half, half, 0)
+    got = along_y(rest)
+    parts = []
+    for piece in (own, got):
+        by_two = along_z(piece, two)
+        by_one = along_z(piece, one)
+        by_mid = along_z(piece, mid)
+        by_out = along_z(by_two, out)
+        inner = (z == 1) | (z == 2)
+        by_three = jnp.where(inner, by_mid, by_out)
+        parts.append((piece, by_one, by_two, by_three))
+
+    groups = flow.reshape(rows // (2 * width), 2, width, width)
+    keep = lax.dynamic_index_in_dim(groups, l, 1, False).reshape(half, width)
+    give = lax.dynamic_index_in_dim(groups, 1 - l, 1, False).reshape(half, width)
+    near = jnp.stack([keep, across(give)])
+    near_x = along_x(near)
+    side = along_y(near)
+    side_x = along_x(side)
+    here = jnp.concatenate([near, side], axis=2)
+    there = jnp.concatenate([near_x, side_x], axis=2)
+    right = jnp.where(x == 0, jnp.stack([here, there], 1), jnp.stack([there, here], 1))
+    right = right.reshape(2, 4, 2, width, 2 * width)
+    stored = pattern[2 * x + y] * pattern[:, z]
+    right = right * stored.astype(jnp.float32)[None, :, None, None, None]
+
+    left, kept, sent = [], [], []
+    for i in range(4):
+        chosen = lax.dynamic_index_in_dim(right, z ^ i, 1, False)
+        first = lax.dynamic_index_in_dim(chosen, y, 1, False)
+        second = lax.dynamic_index_in_dim(chosen, 1 - y, 1, False)
+        both = jnp.concatenate([first, second], axis=1)
+        left.append(jnp.concatenate([parts[0][i], parts[1][i]], axis=1))
+        kept.append(both[0])
+        sent.append(both[1])
+    left = jnp.concatenate(left, axis=1)
+    outgoing = multiply(left, jnp.concatenate(sent, axis=0))
+    product = multiply(left, jnp.concatenate(kept, axis=0)) + across(outgoing)
+    inflated = raise_to(product, power[z])
+    sums = jnp.sum(inflated, axis=0, keepdims=True)
+    mine, other = inflated[:, :width], inflated[:, width:]
+    arrived = along_y(other)
+    row_sum = sums[:, :width] + along_y(sums[:, width:])
+    totals = row_sum + along_x(row_sum)
+    whole = jnp.where(y == 0, jnp.stack([mine, arrived]), jnp.stack([arrived, mine])).reshape(rows, width)
+    level = prune_level[z].astype(jnp.float32) / 8.0
+    return jnp.maximum(order * whole / totals - level, 0.0)
+
+
 def solution(mesh):
+    shape = dict(mesh.shape)
+    special = shape == {"row": 2, "col": 8, "layer": 2}
     return jax.shard_map(
-        on_device,
+        squared if special else general,
         mesh=mesh,
         in_specs=(P("row", ("col", "layer")), P(), P(), P()),
         out_specs=P("row", ("col", "layer")),

time: 146 us -> 71 us (0.49)
  waiting for transfers between devices: 108 us -> 35.9 us
  starting transfers between devices: 0.08 us -> 22.4 us
  between operations: 13.2 us -> 2.93 us
  blocking collectives: 9.09 us -> 0 us
  matrix products: 9.94 us -> 2.14 us
  local copies, waits for them, and re-layouts: 1.31 us -> 5.62 us
  other arithmetic: 4.05 us -> 1.76 us
    all_gather x2 -> x0, waiting for transfers between devices: 100 us -> none  [the longest x1 77.1 us: on_device(): strip = lax.all_gather(masked, 'col', axis=1, tiled=True)]
    ppermute x0 -> x17, waiting for transfers between devices: none -> 35.9 us  [the longest x8 26.6 us: along_z(): lax.ppermute(value, 'col', [(2 * a + b, 2 * d + b) for a, d in pairs for...]
    ppermute x0 -> x17, starting transfers between devices: none -> 22.4 us  [the longest x8 11.3 us: along_z(): lax.ppermute(value, 'col', [(2 * a + b, 2 * d + b) for a, d in pairs for...]
    dot_general x5 -> x2, matrix products: 9.94 us -> 2.14 us  [multiply(): jnp.dot(left, right, precision=lax.Precision.HIGH, preferred_element_type...]
    reduce_scatter x1 -> x0, waiting for transfers between devices: 6.61 us -> none  [on_device(): lax.psum_scatter(partial_value, 'layer', scatter_dimension=1, tiled=True)]
    psum x1 -> x0, blocking collectives: 4.94 us -> none  [on_device(): totals = lax.psum(jnp.sum(inflated, axis=0), 'row')]
    all_to_all x1 -> x0, blocking collectives: 4.15 us -> none  [on_device(): lax.all_to_all(parted, 'layer', split_axis=1, concat_axis=3, tiled=True)]
    dynamic_slice x0 -> x4, local copies, waits for them, and re-layouts: none -> 2.42 us  [the longest x1 1.06 us: squared(): keep = lax.dynamic_index_in_dim(groups, l, 1, False).reshape(half, width)]
  transfers between devices with their start and end apart: 3 -> 17, of which waited for: 3 -> 9; matrix products, arithmetic and copies ran while one was open for 0% -> 5% of each run, Pallas kernels for 0% -> 0%
where the time goes in v1:
time: 71 us; the launch traced here: 70.7 us
  waiting for transfers between devices  35.9 us (51%)
  starting transfers between devices  22.4 us (32%)
  local copies, waits for them, and re-layouts  5.62 us (8%)
  between operations  2.93 us (4%)
  matrix products  2.14 us (3%)
  other arithmetic  1.76 us (2%)
    ppermute x8, waiting for transfers between devices, along_z(): lax.ppermute(value, 'col', [(2 * a + b, 2 * d + b) for a, d in pairs for...  26.6 us
    ppermute x8, starting transfers between devices, along_z(): lax.ppermute(value, 'col', [(2 * a + b, 2 * d + b) for a, d in pairs for...  11.3 us
    ppermute x4, starting transfers between devices, along_y(): return lax.ppermute(value, 'col', [(i, i ^ 1) for i in range(8)])  6.46 us
    ppermute x3, waiting for transfers between devices, along_x(): return lax.ppermute(value, 'row', [(0, 1), (1, 0)])  5.86 us
    ppermute x3, starting transfers between devices, along_x(): return lax.ppermute(value, 'row', [(0, 1), (1, 0)])  4.54 us
    ppermute x4, waiting for transfers between devices, along_y(): return lax.ppermute(value, 'col', [(i, i ^ 1) for i in range(8)])  3.36 us
    unnamed x12, local copies, waits for them, and re-layouts  2.97 us
    dot_general x2, matrix products, multiply(): jnp.dot(left, right, precision=lax.Precision.HIGH, preferred_element_type...  2.14 us
  transfers between devices with their start and end apart: 17, of which 9 were waited for; matrix products, arithmetic and copies ran while one was open for 5% of the time, Pallas kernels for 0%

profile of v1, /device:TPU:0, one launch (start us, length us, event | category | flops | bytes accessed | tf_op | source)
XLA Modules:
  0.0 70.7 jit_solution(15975495793811046905)
XLA Ops:
  0.0 1.9 %constant_dynamic-update-slice_fusion.5 = (f32[512,1024]{1,0:T(8,128)S(1)}, f32[512,128]{1,0:T(8,128)}, f32[512,128]{1,0:T(8,128)}) fusion(f32[1024,128]{1,0:T(8,128)} %param.4, s32[]{:T(128)S(6)} %select_n.128, s32[]{:T(128)S(6)} %select_n.129), kind=kLoop, calls=%fused_computation.70 | loop fusion | bytes 1310728
  1.9 3.0 %collective-permute-start = (f32[512,128]{1,0:T(8,128)}, f32[512,128]{1,0:T(8,128)S(1)}, u32[]{:S(2)}, u32[]{:S(2)}) collective-permute-start(f32[512,128]{1,0:T(8,128)} %get-tuple-element.27), channel_id=1, source_target_pairs={{0,2},{2,0},{4,6},{6,4},{8,10},{10,8},{12,14},{14,12},{1,3},{3,1},... | collective-permute-start | bytes 786440 | tf_op jit(solution)/shard_map/ppermute | solution.py:63
  4.9 1.1 %constant_dynamic-slice_fusion.3 = (f32[4,1,128,128]{3,2,1,0:T(8,128)S(1)}, f32[4,1,128,128]{3,2,1,0:T(8,128)S(1)}) fusion(f32[4,2,128,128]{3,2,1,0:T(8,128)} %bitcast.72, s32[]{:T(128)S(6)} %select_n.134, s32[]{:T(128)S(6)} %select_n.135), kind=kLoop, calls=%fused_computation.74 | loop fusion | bytes 1048584 | tf_op jit(solution)/shard_map/jit(dynamic_index_in_dim)/dynamic_slice | solution.py:90
  5.9 0.1 collective-permute-start.9
  6.0 1.6 %collective-permute-start.1 = (f32[512,128]{1,0:T(8,128)}, f32[512,128]{1,0:T(8,128)}, u32[]{:S(2)}, u32[]{:S(2)}) collective-permute-start(f32[512,128]{1,0:T(8,128)} %get-tuple-element.6), channel_id=1, source_target_pairs={{0,4},{2,6},{4,0},{6,2},{8,12},{10,14},{12,8},{14,10},{1,5},{3,7},... | collective-permute-start | bytes 786440 | tf_op jit(solution)/shard_map/ppermute | solution.py:60
  7.6 2.6 %collective-permute-start.3 = (f32[512,128]{1,0:T(8,128)}, f32[512,128]{1,0:T(8,128)S(1)}, u32[]{:S(2)}, u32[]{:S(2)}) collective-permute-start(f32[512,128]{1,0:T(8,128)} %get-tuple-element.6), channel_id=1, source_target_pairs={{0,8},{2,10},{4,12},{6,14},{8,0},{10,2},{12,4},{14,6},{1,9},{3,11}... | collective-permute-start | bytes 786440 | tf_op jit(solution)/shard_map/ppermute | solution.py:60
  10.2 1.4 %collective-permute-start.5 = (f32[512,128]{1,0:T(8,128)}, f32[512,128]{1,0:T(8,128)}, u32[]{:S(2)}, u32[]{:S(2)}) collective-permute-start(f32[512,128]{1,0:T(8,128)} %get-tuple-element.6), channel_id=1, source_target_pairs={{4,8},{6,10},{8,4},{10,6},{5,9},{7,11},{9,5},{11,7},{20,24},{22,26... | collective-permute-start | bytes 786440 | tf_op jit(solution)/shard_map/ppermute | solution.py:60
  11.6 0.2 fusion.33
  11.9 0.0 collective-permute-done
  11.9 1.6 %collective-permute-start.2 = (f32[512,128]{1,0:T(8,128)S(1)}, f32[512,128]{1,0:T(8,128)S(1)}, u32[]{:S(2)}, u32[]{:S(2)}) collective-permute-start(f32[512,128]{1,0:T(8,128)S(1)} %collective-permute-done), channel_id=1, source_target_pairs={{0,4},{2,6},{4,0},{6,2},{8,12},{10,14},{12,8},{14,10},{1,5},{3,7},... | collective-permute-start | bytes 786440 | tf_op jit(solution)/shard_map/ppermute | solution.py:60
  13.4 0.0 collective-permute-done.9
  13.5 1.3 %collective-permute-start.10 = (f32[2,512,128]{2,1,0:T(8,128)S(1)}, f32[2,512,128]{2,1,0:T(8,128)S(1)}, u32[]{:S(2)}, u32[]{:S(2)}) collective-permute-start(f32[2,512,128]{2,1,0:T(8,128)S(1)} %pad_maximum_fusion), channel_id=1, source_target_pairs={{0,2},{2,0},{4,6},{6,4},{8,10},{10,8},{12,14},{14,12},{1,3},{3,1},... | collective-permute-start | bytes 1572872 | tf_op jit(solution)/shard_map/ppermute | solution.py:63
  14.8 5.8 %collective-permute-done.1 = f32[512,128]{1,0:T(8,128)} collective-permute-done((f32[512,128]{1,0:T(8,128)}, f32[512,128]{1,0:T(8,128)}, u32[]{:S(2)}, u32[]{:S(2)}) %collective-permute-start.1) | collective-permute-done | bytes 262176 | tf_op jit(solution)/shard_map/ppermute | solution.py:60
  20.7 0.9 %collective-permute-start.4 = (f32[512,128]{1,0:T(8,128)S(1)}, f32[512,128]{1,0:T(8,128)S(1)}, u32[]{:S(2)}, u32[]{:S(2)}) collective-permute-start(f32[512,128]{1,0:T(8,128)S(1)} %collective-permute-done), channel_id=1, source_target_pairs={{0,8},{2,10},{4,12},{6,14},{8,0},{10,2},{12,4},{14,6},{1,9},{3,11}... | collective-permute-start | bytes 786440 | tf_op jit(solution)/shard_map/ppermute | solution.py:60
  21.6 1.0 %constant_dynamic-update-slice_fusion.3 = f32[512,1024]{1,0:T(8,128)S(1)} fusion(f32[512,1024]{1,0:T(8,128)S(1)} %constant_dynamic-update-slice_fusion.4, f32[512,128]{1,0:T(8,128)} %collective-permute-done.1), kind=kLoop, calls=%fused_computation.68 | loop fusion | bytes 524288
  22.5 1.0 %collective-permute-done.3 = f32[512,128]{1,0:T(8,128)S(1)} collective-permute-done((f32[512,128]{1,0:T(8,128)}, f32[512,128]{1,0:T(8,128)S(1)}, u32[]{:S(2)}, u32[]{:S(2)}) %collective-permute-start.3) | collective-permute-done | bytes 262176 | tf_op jit(solution)/shard_map/ppermute | solution.py:60
  23.6 1.5 %collective-permute-start.11 = (f32[2,512,128]{2,1,0:T(8,128)S(1)}, f32[2,512,128]{2,1,0:T(8,128)S(1)}, u32[]{:S(2)}, u32[]{:S(2)}) collective-permute-start(f32[2,512,128]{2,1,0:T(8,128)S(1)} %pad_maximum_fusion), channel_id=1, source_target_pairs={{0,16},{16,0},{1,17},{17,1},{2,18},{18,2},{3,19},{19,3},{4,20},{20... | collective-permute-start | bytes 1572872 | tf_op jit(solution)/shard_map/ppermute | solution.py:66
  25.1 1.1 %collective-permute-done.2 = f32[512,128]{1,0:T(8,128)S(1)} collective-permute-done((f32[512,128]{1,0:T(8,128)S(1)}, f32[512,128]{1,0:T(8,128)S(1)}, u32[]{:S(2)}, u32[]{:S(2)}) %collective-permute-start.2) | collective-permute-done | bytes 262176 | tf_op jit(solution)/shard_map/ppermute | solution.py:60
  26.2 1.3 %collective-permute-start.6 = (f32[512,128]{1,0:T(8,128)S(1)}, f32[512,128]{1,0:T(8,128)S(1)}, u32[]{:S(2)}, u32[]{:S(2)}) collective-permute-start(f32[512,128]{1,0:T(8,128)S(1)} %collective-permute-done.3), channel_id=1, source_target_pairs={{4,0},{6,2},{8,12},{10,14},{5,1},{7,3},{9,13},{11,15},{20,16},{22,... | collective-permute-start | bytes 786440 | tf_op jit(solution)/shard_map/ppermute | solution.py:60
  27.5 12.2 %collective-permute-done.4 = f32[512,128]{1,0:T(8,128)S(1)} collective-permute-done((f32[512,128]{1,0:T(8,128)S(1)}, f32[512,128]{1,0:T(8,128)S(1)}, u32[]{:S(2)}, u32[]{:S(2)}) %collective-permute-start.4) | collective-permute-done | bytes 262176 | tf_op jit(solution)/shard_map/ppermute | solution.py:60
  39.8 0.7 collective-permute-start.7
  40.5 0.0 collective-permute-done.5
  40.5 1.3 %collective-permute-start.8 = (f32[512,128]{1,0:T(8,128)S(1)}, f32[512,128]{1,0:T(8,128)S(1)}, u32[]{:S(2)}, u32[]{:S(2)}) collective-permute-start(f32[512,128]{1,0:T(8,128)S(1)} %collective-permute-done.4), channel_id=1, source_target_pairs={{4,0},{6,2},{8,12},{10,14},{5,1},{7,3},{9,13},{11,15},{20,16},{22,... | collective-permute-start | bytes 786440 | tf_op jit(solution)/shard_map/ppermute | solution.py:60
  41.8 0.0 collective-permute-done.10
  41.8 1.6 %collective-permute-start.12 = (f32[2,512,128]{2,1,0:T(8,128)S(1)}, f32[2,512,128]{2,1,0:T(8,128)S(1)}, u32[]{:S(2)}, u32[]{:S(2)}) collective-permute-start(f32[2,512,128]{2,1,0:T(8,128)S(1)} %collective-permute-done.10), channel_id=1, source_target_pairs={{0,16},{16,0},{1,17},{17,1},{2,18},{18,2},{3,19},{19,3},{4,20},{20... | collective-permute-start | bytes 1572872 | tf_op jit(solution)/shard_map/ppermute | solution.py:66
  43.4 0.1 maximum_bitcast_fusion
  43.5 6.4 %collective-permute-done.8 = f32[512,128]{1,0:T(8,128)S(1)} collective-permute-done((f32[512,128]{1,0:T(8,128)S(1)}, f32[512,128]{1,0:T(8,128)S(1)}, u32[]{:S(2)}, u32[]{:S(2)}) %collective-permute-start.8) | collective-permute-done | bytes 262176 | tf_op jit(solution)/shard_map/ppermute | solution.py:60
  49.9 5.0 %collective-permute-done.12 = f32[2,512,128]{2,1,0:T(8,128)S(1)} collective-permute-done((f32[2,512,128]{2,1,0:T(8,128)S(1)}, f32[2,512,128]{2,1,0:T(8,128)S(1)}, u32[]{:S(2)}, u32[]{:S(2)}) %collective-permute-start.12) | collective-permute-done | bytes 524320 | tf_op jit(solution)/shard_map/ppermute | solution.py:66
  55.0 0.1 maximum_bitcast_fusion.1
  55.1 0.2 maximum_select_fusion
  55.2 0.3 broadcast_multiply_fusion
  55.5 0.2 dynamic-slice_bitcast_fusion.7
  55.7 0.1 fusion.22
  55.8 0.1 fusion.26
  55.9 0.0 copy-start.1
  55.9 1.0 %fusion.7 = f32[512,256]{1,0:T(8,128)S(1)} fusion(f32[512,1024]{1,0:T(8,128)S(1)} %select_dynamic-update-slice_fusion, f32[256,256]{1,0:T(8,128)S(1)} %get-tuple-element.24, f32[256,256]{1,0:T(8,128)S(1)} %get-tuple-element.30, f32[256,256]{1,0:T(8,128)S(1)} %get-tuple-element.20, f32[256,256]{1,0:T(8,128)S(1)} %get-tuple-element.32), kind=kOutput, calls=%fused_computation.11 | convolution fusion | flops 806092800 | bytes 3670016 | tf_op jit(solution)/shard_map/dot_general | solution.py:8
  56.9 0.1 collective-permute-start.13
  57.0 0.6 dynamic_slice.55
  59.6 0.0 copy-start.2
  59.6 1.1 %fusion.39 = (f32[256]{0:T(256)S(1)}, f32[512,256]{1,0:T(8,128)S(1)}) fusion(pred[]{:T(512)} %bitcast.26, f32[512,256]{1,0:T(8,128)S(1)} %collective-permute-done.13, f32[512,1024]{1,0:T(8,128)S(1)} %select_dynamic-update-slice_fusion, f32[256,256]{1,0:T(8,128)S(1)} %get-tuple-element.23, f32[256,256]{1,0:T(8,128)S(1)} %get-tuple-element.31, ...), kind=kOutput, calls=%fused_computation.85 | convolution fusion | flops 807010048 | bytes 4195331 | tf_op jit(solution)/shard_map/dot_general | solution.py:8
  60.7 0.6 collective-permute-start.15
  61.3 1.6 %collective-permute-start.14 = (f32[512,128]{1,0:T(8,128)S(1)}, f32[512,128]{1,0:T(8,128)S(1)}, u32[]{:S(2)}, u32[]{:S(2)}) collective-permute-start(f32[512,128]{1,0:T(8,128)S(1)} %get-tuple-element.16), channel_id=1, source_target_pairs={{0,2},{2,0},{4,6},{6,4},{8,10},{10,8},{12,14},{14,12},{1,3},{3,1},... | collective-permute-start | bytes 786440 | tf_op jit(solution)/shard_map/ppermute | solution.py:63
  62.9 1.4 %collective-permute-done.15 = f32[1,128]{1,0:T(1,128)S(1)} collective-permute-done((f32[1,128]{1,0:T(1,128)S(1)}, f32[1,128]{1,0:T(1,128)S(1)}, u32[]{:S(2)}, u32[]{:S(2)}) %collective-permute-start.15) | collective-permute-done | bytes 544 | tf_op jit(solution)/shard_map/ppermute | solution.py:63
  64.3 1.5 %collective-permute-start.16 = (f32[1,128]{1,0:T(1,128)S(1)}, f32[1,128]{1,0:T(1,128)S(1)}, u32[]{:S(2)}, u32[]{:S(2)}) collective-permute-start(f32[1,128]{1,0:T(1,128)S(1)} %slice_add_fusion), channel_id=1, source_target_pairs={{0,16},{16,0},{1,17},{17,1},{2,18},{18,2},{3,19},{19,3},{4,20},{20... | collective-permute-start | bytes 1544 | tf_op jit(solution)/shard_map/ppermute | solution.py:66
  65.8 0.6 dynamic_slice.70
  67.1 0.8 %collective-permute-done.16 = f32[1,128]{1,0:T(1,128)S(1)} collective-permute-done((f32[1,128]{1,0:T(1,128)S(1)}, f32[1,128]{1,0:T(1,128)S(1)}, u32[]{:S(2)}, u32[]{:S(2)}) %collective-permute-start.16) | collective-permute-done | bytes 544 | tf_op jit(solution)/shard_map/ppermute | solution.py:66
  67.9 1.9 %collective-permute-done.14 = f32[512,128]{1,0:T(8,128)S(1)} collective-permute-done((f32[512,128]{1,0:T(8,128)S(1)}, f32[512,128]{1,0:T(8,128)S(1)}, u32[]{:S(2)}, u32[]{:S(2)}) %collective-permute-start.14) | collective-permute-done | bytes 262176 | tf_op jit(solution)/shard_map/ppermute | solution.py:63
  69.9 0.9 %fusion.20 = f32[1024,128]{1,0:T(8,128)} fusion(f32[2,512,128]{2,1,0:T(8,128)S(1)} %fusion.18, f32[]{:T(128)} %bitcast.32, f32[128]{0:T(128)S(1)} %add_bitcast_fusion), kind=kLoop, calls=%fused_computation.37 | loop fusion | flops 393216 | bytes 1049092 | tf_op jit(solution)/shard_map/max | solution.py:123
  (21 shorter events, 0.3 us)
Async XLA Ops:
  0.0 11.6 %copy-start = (s32[4,4]{1,0:T(4,128)S(1)}, s32[4,4]{1,0:T(4,128)}, u32[]{:S(2)}) copy-start(s32[4,4]{1,0:T(4,128)} %param.5) | copy-start | bytes 196
  1.9 10.0 %collective-permute-start = (f32[512,128]{1,0:T(8,128)}, f32[512,128]{1,0:T(8,128)S(1)}, u32[]{:S(2)}, u32[]{:S(2)}) collective-permute-start(f32[512,128]{1,0:T(8,128)} %get-tuple-element.27), channel_id=1, source_target_pairs={{0,2},{2,0},{4,6},{6,4},{8,10},{10,8},{12,14},{14,12},{1,3},{3,1},... | collective-permute-start | bytes 786440 | tf_op jit(solution)/shard_map/ppermute | solution.py:63
  5.9 7.5 %collective-permute-start.9 = (f32[512,128]{1,0:T(8,128)S(1)}, f32[512,128]{1,0:T(8,128)S(1)}, u32[]{:S(2)}, u32[]{:S(2)}) collective-permute-start(f32[512,128]{1,0:T(8,128)S(1)} %bitcast.75), channel_id=1, source_target_pairs={{0,1},{1,0},{2,3},{3,2},{4,5},{5,4},{6,7},{7,6},{8,9},{9,8},{10,11... | collective-permute-start | bytes 786440 | tf_op jit(solution)/shard_map/ppermute | solution.py:69
  6.0 14.7 %collective-permute-start.1 = (f32[512,128]{1,0:T(8,128)}, f32[512,128]{1,0:T(8,128)}, u32[]{:S(2)}, u32[]{:S(2)}) collective-permute-start(f32[512,128]{1,0:T(8,128)} %get-tuple-element.6), channel_id=1, source_target_pairs={{0,4},{2,6},{4,0},{6,2},{8,12},{10,14},{12,8},{14,10},{1,5},{3,7},... | collective-permute-start | bytes 786440 | tf_op jit(solution)/shard_map/ppermute | solution.py:60
  7.6 15.9 %collective-permute-start.3 = (f32[512,128]{1,0:T(8,128)}, f32[512,128]{1,0:T(8,128)S(1)}, u32[]{:S(2)}, u32[]{:S(2)}) collective-permute-start(f32[512,128]{1,0:T(8,128)} %get-tuple-element.6), channel_id=1, source_target_pairs={{0,8},{2,10},{4,12},{6,14},{8,0},{10,2},{12,4},{14,6},{1,9},{3,11}... | collective-permute-start | bytes 786440 | tf_op jit(solution)/shard_map/ppermute | solution.py:60
  10.2 30.2 %collective-permute-start.5 = (f32[512,128]{1,0:T(8,128)}, f32[512,128]{1,0:T(8,128)}, u32[]{:S(2)}, u32[]{:S(2)}) collective-permute-start(f32[512,128]{1,0:T(8,128)} %get-tuple-element.6), channel_id=1, source_target_pairs={{4,8},{6,10},{8,4},{10,6},{5,9},{7,11},{9,5},{11,7},{20,24},{22,26... | collective-permute-start | bytes 786440 | tf_op jit(solution)/shard_map/ppermute | solution.py:60
  11.9 14.3 %collective-permute-start.2 = (f32[512,128]{1,0:T(8,128)S(1)}, f32[512,128]{1,0:T(8,128)S(1)}, u32[]{:S(2)}, u32[]{:S(2)}) collective-permute-start(f32[512,128]{1,0:T(8,128)S(1)} %collective-permute-done), channel_id=1, source_target_pairs={{0,4},{2,6},{4,0},{6,2},{8,12},{10,14},{12,8},{14,10},{1,5},{3,7},... | collective-permute-start | bytes 786440 | tf_op jit(solution)/shard_map/ppermute | solution.py:60
  13.5 28.3 %collective-permute-start.10 = (f32[2,512,128]{2,1,0:T(8,128)S(1)}, f32[2,512,128]{2,1,0:T(8,128)S(1)}, u32[]{:S(2)}, u32[]{:S(2)}) collective-permute-start(f32[2,512,128]{2,1,0:T(8,128)S(1)} %pad_maximum_fusion), channel_id=1, source_target_pairs={{0,2},{2,0},{4,6},{6,4},{8,10},{10,8},{12,14},{14,12},{1,3},{3,1},... | collective-permute-start | bytes 1572872 | tf_op jit(solution)/shard_map/ppermute | solution.py:63
  20.7 19.1 %collective-permute-start.4 = (f32[512,128]{1,0:T(8,128)S(1)}, f32[512,128]{1,0:T(8,128)S(1)}, u32[]{:S(2)}, u32[]{:S(2)}) collective-permute-start(f32[512,128]{1,0:T(8,128)S(1)} %collective-permute-done), channel_id=1, source_target_pairs={{0,8},{2,10},{4,12},{6,14},{8,0},{10,2},{12,4},{14,6},{1,9},{3,11}... | collective-permute-start | bytes 786440 | tf_op jit(solution)/shard_map/ppermute | solution.py:60
  23.6 26.4 %collective-permute-start.11 = (f32[2,512,128]{2,1,0:T(8,128)S(1)}, f32[2,512,128]{2,1,0:T(8,128)S(1)}, u32[]{:S(2)}, u32[]{:S(2)}) collective-permute-start(f32[2,512,128]{2,1,0:T(8,128)S(1)} %pad_maximum_fusion), channel_id=1, source_target_pairs={{0,16},{16,0},{1,17},{17,1},{2,18},{18,2},{3,19},{19,3},{4,20},{20... | collective-permute-start | bytes 1572872 | tf_op jit(solution)/shard_map/ppermute | solution.py:66
  26.2 17.2 %collective-permute-start.6 = (f32[512,128]{1,0:T(8,128)S(1)}, f32[512,128]{1,0:T(8,128)S(1)}, u32[]{:S(2)}, u32[]{:S(2)}) collective-permute-start(f32[512,128]{1,0:T(8,128)S(1)} %collective-permute-done.3), channel_id=1, source_target_pairs={{4,0},{6,2},{8,12},{10,14},{5,1},{7,3},{9,13},{11,15},{20,16},{22,... | collective-permute-start | bytes 786440 | tf_op jit(solution)/shard_map/ppermute | solution.py:60
  39.8 3.7 %collective-permute-start.7 = (f32[512,128]{1,0:T(8,128)S(1)}, f32[512,128]{1,0:T(8,128)S(1)}, u32[]{:S(2)}, u32[]{:S(2)}) collective-permute-start(f32[512,128]{1,0:T(8,128)S(1)} %collective-permute-done), channel_id=1, source_target_pairs={{4,8},{6,10},{8,4},{10,6},{5,9},{7,11},{9,5},{11,7},{20,24},{22,26... | collective-permute-start | bytes 786440 | tf_op jit(solution)/shard_map/ppermute | solution.py:60
  40.5 9.4 %collective-permute-start.8 = (f32[512,128]{1,0:T(8,128)S(1)}, f32[512,128]{1,0:T(8,128)S(1)}, u32[]{:S(2)}, u32[]{:S(2)}) collective-permute-start(f32[512,128]{1,0:T(8,128)S(1)} %collective-permute-done.4), channel_id=1, source_target_pairs={{4,0},{6,2},{8,12},{10,14},{5,1},{7,3},{9,13},{11,15},{20,16},{22,... | collective-permute-start | bytes 786440 | tf_op jit(solution)/shard_map/ppermute | solution.py:60
  41.8 13.2 %collective-permute-start.12 = (f32[2,512,128]{2,1,0:T(8,128)S(1)}, f32[2,512,128]{2,1,0:T(8,128)S(1)}, u32[]{:S(2)}, u32[]{:S(2)}) collective-permute-start(f32[2,512,128]{2,1,0:T(8,128)S(1)} %collective-permute-done.10), channel_id=1, source_target_pairs={{0,16},{16,0},{1,17},{17,1},{2,18},{18,2},{3,19},{19,3},{4,20},{20... | collective-permute-start | bytes 1572872 | tf_op jit(solution)/shard_map/ppermute | solution.py:66
  55.9 1.1 %copy-start.1 = (s32[4]{0:T(128)S(1)}, s32[4]{0:T(128)}, u32[]{:S(2)}) copy-start(s32[4]{0:T(128)} %param.7) | copy-start | bytes 52
  56.9 2.6 %collective-permute-start.13 = (f32[512,256]{1,0:T(8,128)S(1)}, f32[512,256]{1,0:T(8,128)S(1)}, u32[]{:S(2)}, u32[]{:S(2)}) collective-permute-start(f32[512,256]{1,0:T(8,128)S(1)} %fusion.7), channel_id=1, source_target_pairs={{0,1},{1,0},{2,3},{3,2},{4,5},{5,4},{6,7},{7,6},{8,9},{9,8},{10,11... | collective-permute-start | bytes 1572872 | tf_op jit(solution)/shard_map/ppermute | solution.py:69
  59.6 6.2 %copy-start.2 = (s32[4]{0:T(128)S(1)}, s32[4]{0:T(128)}, u32[]{:S(2)}) copy-start(s32[4]{0:T(128)} %param.6) | copy-start | bytes 52
  60.7 3.6 %collective-permute-start.15 = (f32[1,128]{1,0:T(1,128)S(1)}, f32[1,128]{1,0:T(1,128)S(1)}, u32[]{:S(2)}, u32[]{:S(2)}) collective-permute-start(f32[1,128]{1,0:T(1,128)S(1)} %slice.59), channel_id=1, source_target_pairs={{0,2},{2,0},{4,6},{6,4},{8,10},{10,8},{12,14},{14,12},{1,3},{3,1},... | collective-permute-start | bytes 1544 | tf_op jit(solution)/shard_map/ppermute | solution.py:63
  61.3 8.5 %collective-permute-start.14 = (f32[512,128]{1,0:T(8,128)S(1)}, f32[512,128]{1,0:T(8,128)S(1)}, u32[]{:S(2)}, u32[]{:S(2)}) collective-permute-start(f32[512,128]{1,0:T(8,128)S(1)} %get-tuple-element.16), channel_id=1, source_target_pairs={{0,2},{2,0},{4,6},{6,4},{8,10},{10,8},{12,14},{14,12},{1,3},{3,1},... | collective-permute-start | bytes 786440 | tf_op jit(solution)/shard_map/ppermute | solution.py:63
  64.3 3.5 %collective-permute-start.16 = (f32[1,128]{1,0:T(1,128)S(1)}, f32[1,128]{1,0:T(1,128)S(1)}, u32[]{:S(2)}, u32[]{:S(2)}) collective-permute-start(f32[1,128]{1,0:T(1,128)S(1)} %slice_add_fusion), channel_id=1, source_target_pairs={{0,16},{16,0},{1,17},{17,1},{2,18},{18,2},{3,19},{19,3},{4,20},{20... | collective-permute-start | bytes 1544 | tf_op jit(solution)/shard_map/ppermute | solution.py:66

commit v2 on v1

--- a/solution.py
+++ b/solution.py
@@ -56,8 +56,8 @@
     x, c, l = lax.axis_index("row"), lax.axis_index("col"), lax.axis_index("layer")
     y, z = c % 2, c // 2
 
-    def along_z(value, pairs):
-        return lax.ppermute(value, "col", [(2 * a + b, 2 * d + b) for a, d in pairs for b in range(2)])
+    def along_z(value, pairs, turn=0):
+        return lax.ppermute(value, "col", [(2 * a + b, 2 * d + (b ^ turn)) for a, d in pairs for b in range(2)])
 
     def along_y(value):
         return lax.ppermute(value, "col", [(i, i ^ 1) for i in range(8)])
@@ -73,45 +73,62 @@
     mid = [(1, 2), (2, 1)]
     out = [(1, 0), (2, 3)]
 
+    def after(value, *earlier):
+        return lax.optimization_barrier((value, *earlier))[0]
+
+    def split(value):
+        grouped = value.reshape(value.shape[0] // (2 * width), 2, width, width)
+        return [
+            lax.dynamic_index_in_dim(grouped, i, 1, False).reshape(value.shape[0] // 2, width)
+            for i in (l, 1 - l)
+        ]
+
+    def both_layers(value):
+        keep, give = split(value)
+        return jnp.stack([keep, across(give)])
+
     own = lax.dynamic_slice_in_dim(flow, y * half, half, 0)
     rest = lax.dynamic_slice_in_dim(flow, (1 - y) * half, half, 0)
-    got = along_y(rest)
-    parts = []
-    for piece in (own, got):
-        by_two = along_z(piece, two)
-        by_one = along_z(piece, one)
-        by_mid = along_z(piece, mid)
-        by_out = along_z(by_two, out)
-        inner = (z == 1) | (z == 2)
-        by_three = jnp.where(inner, by_mid, by_out)
-        parts.append((piece, by_one, by_two, by_three))
+    two_a = along_z(own, two)
+    two_b = along_z(rest, two, 1)
+    beside = along_y(flow)
+    far = along_x(flow)
+    one_a = along_z(own, one)
+    got = lax.dynamic_slice_in_dim(beside, y * half, half, 0)
+    one_b = along_z(got, one)
+    far_side = along_x(after(beside, far))
+    near = both_layers(after(flow, beside))
+    near_x = both_layers(far)
+    side = both_layers(beside)
+    by_two = jnp.concatenate([two_a, two_b], axis=1)
+    pair = jnp.concatenate([after(own, beside), got], axis=1)
+    by_out = along_z(after(by_two, one_a, near, near_x, side), out)
+    by_mid = along_z(after(pair, by_two, one_a, near, near_x, side), mid)
+    side_x = both_layers(far_side)
+    by_one = jnp.concatenate([one_a, one_b], axis=1)
 
-    groups = flow.reshape(rows // (2 * width), 2, width, width)
-    keep = lax.dynamic_index_in_dim(groups, l, 1, False).reshape(half, width)
-    give = lax.dynamic_index_in_dim(groups, 1 - l, 1, False).reshape(half, width)
-    near = jnp.stack([keep, across(give)])
-    near_x = along_x(near)
-    side = along_y(near)
-    side_x = along_x(side)
     here = jnp.concatenate([near, side], axis=2)
     there = jnp.concatenate([near_x, side_x], axis=2)
     right = jnp.where(x == 0, jnp.stack([here, there], 1), jnp.stack([there, here], 1))
     right = right.reshape(2, 4, 2, width, 2 * width)
     stored = pattern[2 * x + y] * pattern[:, z]
     right = right * stored.astype(jnp.float32)[None, :, None, None, None]
-
-    left, kept, sent = [], [], []
+    kept, sent = [], []
     for i in range(4):
         chosen = lax.dynamic_index_in_dim(right, z ^ i, 1, False)
         first = lax.dynamic_index_in_dim(chosen, y, 1, False)
         second = lax.dynamic_index_in_dim(chosen, 1 - y, 1, False)
         both = jnp.concatenate([first, second], axis=1)
-        left.append(jnp.concatenate([parts[0][i], parts[1][i]], axis=1))
         kept.append(both[0])
         sent.append(both[1])
-    left = jnp.concatenate(left, axis=1)
-    outgoing = multiply(left, jnp.concatenate(sent, axis=0))
-    product = multiply(left, jnp.concatenate(kept, axis=0)) + across(outgoing)
+
+    left = jnp.concatenate([pair, by_one, by_two], axis=1)
+    early_sent = multiply(left, jnp.concatenate(sent[:3]))
+    early_kept = multiply(left, jnp.concatenate(kept[:3]))
+    by_three = jnp.where((z == 1) | (z == 2), by_mid, by_out)
+    by_three = after(by_three, early_sent, early_kept)
+    outgoing = early_sent + multiply(by_three, sent[3])
+    product = early_kept + multiply(by_three, kept[3]) + across(outgoing)
     inflated = raise_to(product, power[z])
     sums = jnp.sum(inflated, axis=0, keepdims=True)
     mine, other = inflated[:, :width], inflated[:, width:]

time: 71 us -> 64.8 us (0.913)
  starting transfers between devices: 22.4 us -> 17.5 us
  local copies, waits for them, and re-layouts: 5.62 us -> 3.68 us
    ppermute x4 -> x3, waiting for transfers between devices: 3.36 us -> 6.87 us  [along_y(): return lax.ppermute(value, 'col', [(i, i ^ 1) for i in range(8)])]
    ppermute x8 -> x6, starting transfers between devices: 11.3 us -> 8.12 us  [along_z(): lax.ppermute(value, 'col', [(2 * a + b, 2 * d + (b ^ turn)) for a, d in p...]
    unnamed x12 -> x11, local copies, waits for them, and re-layouts: 2.97 us -> 0.16 us
    ppermute x3, waiting for transfers between devices: 5.86 us -> 3.23 us  [along_x(): return lax.ppermute(value, 'row', [(0, 1), (1, 0)])]
    ppermute x8 -> x6, waiting for transfers between devices: 26.6 us -> 24.4 us  [along_z(): lax.ppermute(value, 'col', [(2 * a + b, 2 * d + (b ^ turn)) for a, d in p...]
    ppermute x4 -> x3, starting transfers between devices: 6.46 us -> 5.12 us  [along_y(): return lax.ppermute(value, 'col', [(i, i ^ 1) for i in range(8)])]
    ppermute x3, starting transfers between devices: 4.54 us -> 3.52 us  [along_x(): return lax.ppermute(value, 'row', [(0, 1), (1, 0)])]
    ppermute x2 -> x5, waiting for transfers between devices: 0.01 us -> 1.02 us  [across(): return lax.ppermute(value, 'layer', [(0, 1), (1, 0)])]
  transfers between devices with their start and end apart: 17 -> 17, of which waited for: 9 -> 10; matrix products, arithmetic and copies ran while one was open for 5% -> 10% of each run, Pallas kernels for 0% -> 0%
where the time goes in v2:
time: 64.8 us; the launch traced here: 64.6 us
  waiting for transfers between devices  35.6 us (55%)
  starting transfers between devices  17.5 us (27%)
  local copies, waits for them, and re-layouts  3.68 us (6%)
  between operations  2.89 us (4%)
  matrix products  2.51 us (4%)
  other arithmetic  2.42 us (4%)
    ppermute x6, waiting for transfers between devices, along_z(): lax.ppermute(value, 'col', [(2 * a + b, 2 * d + (b ^ turn)) for a, d in p...  24.4 us
    ppermute x6, starting transfers between devices, along_z(): lax.ppermute(value, 'col', [(2 * a + b, 2 * d + (b ^ turn)) for a, d in p...  8.12 us
    ppermute x3, waiting for transfers between devices, along_y(): return lax.ppermute(value, 'col', [(i, i ^ 1) for i in range(8)])  6.87 us
    ppermute x3, starting transfers between devices, along_y(): return lax.ppermute(value, 'col', [(i, i ^ 1) for i in range(8)])  5.12 us
    ppermute x3, starting transfers between devices, along_x(): return lax.ppermute(value, 'row', [(0, 1), (1, 0)])  3.52 us
    ppermute x3, waiting for transfers between devices, along_x(): return lax.ppermute(value, 'row', [(0, 1), (1, 0)])  3.23 us
    dot_general x4, matrix products, multiply(): jnp.dot(left, right, precision=lax.Precision.HIGH, preferred_element_type...  2.51 us
  transfers between devices with their start and end apart: 17, of which 10 were waited for; matrix products, arithmetic and copies ran while one was open for 10% of the time, Pallas kernels for 0%

profile of v2, /device:TPU:0, one launch (start us, length us, event | category | flops | bytes accessed | tf_op | source)
XLA Modules:
  0.0 64.6 jit_solution(7724101268328776252)
XLA Ops:
  0.0 3.0 %collective-permute-start = (f32[1024,128]{1,0:T(8,128)}, f32[1024,128]{1,0:T(8,128)S(1)}, u32[]{:S(2)}, u32[]{:S(2)}) collective-permute-start(f32[1024,128]{1,0:T(8,128)} %param.4), channel_id=1, source_target_pairs={{0,2},{2,0},{4,6},{6,4},{8,10},{10,8},{12,14},{14,12},{1,3},{3,1},... | collective-permute-start | bytes 1572872 | tf_op jit(solution)/shard_map/ppermute | solution.py:63
  3.0 1.5 %collective-permute-start.7 = (f32[1024,128]{1,0:T(8,128)}, f32[1024,128]{1,0:T(8,128)S(1)}, u32[]{:S(2)}, u32[]{:S(2)}) collective-permute-start(f32[1024,128]{1,0:T(8,128)} %param.4), channel_id=1, source_target_pairs={{0,16},{16,0},{1,17},{17,1},{2,18},{18,2},{3,19},{19,3},{4,20},{20... | collective-permute-start | bytes 1572872 | tf_op jit(solution)/shard_map/ppermute | solution.py:66
  4.5 1.1 %constant_dynamic-slice_fusion.10 = (f32[512,128]{1,0:T(8,128)S(1)}, f32[512,128]{1,0:T(8,128)S(1)}) fusion(f32[1024,128]{1,0:T(8,128)} %param.4, s32[]{:T(128)S(6)} %select_n.130, s32[]{:T(128)S(6)} %select_n.129), kind=kLoop, calls=%fused_computation.85 | loop fusion | bytes 1048584 | tf_op jit(solution)/shard_map/dynamic_slice | solution.py:91
  5.5 2.7 %collective-permute-start.3 = (f32[512,128]{1,0:T(8,128)S(1)}, f32[512,128]{1,0:T(8,128)S(1)}, u32[]{:S(2)}, u32[]{:S(2)}) collective-permute-start(f32[512,128]{1,0:T(8,128)S(1)} %get-tuple-element.11), channel_id=1, source_target_pairs={{0,8},{2,10},{4,12},{6,14},{8,0},{10,2},{12,4},{14,6},{1,9},{3,11}... | collective-permute-start | bytes 786440 | tf_op jit(solution)/shard_map/ppermute | solution.py:60
  8.2 1.6 %collective-permute-start.1 = (f32[512,128]{1,0:T(8,128)S(1)}, f32[512,128]{1,0:T(8,128)S(1)}, u32[]{:S(2)}, u32[]{:S(2)}) collective-permute-start(f32[512,128]{1,0:T(8,128)S(1)} %get-tuple-element.11), channel_id=1, source_target_pairs={{0,4},{2,6},{4,0},{6,2},{8,12},{10,14},{12,8},{14,10},{1,5},{3,7},... | collective-permute-start | bytes 786440 | tf_op jit(solution)/shard_map/ppermute | solution.py:60
  9.8 0.3 collective-permute-start.4
  10.0 0.9 %fusion.32 = s32[4]{0:T(128)S(1)} fusion(s32[4,4]{1,0:T(4,128)} %param.5, s32[]{:T(128)S(6)} %select_n.126), kind=kLoop, calls=%fused_computation.88 | loop fusion | bytes 36 | tf_op jit(solution)/shard_map/dynamic_slice | solution.py:114
  10.9 0.7 %fusion.35 = f32[4]{0:T(128)S(1)} fusion(s32[4]{0:T(128)S(1)} %fusion.32, s32[4,4]{1,0:T(4,128)} %param.5, s32[]{:T(128)S(6)} %select_n.136), kind=kLoop, calls=%fused_computation.91 | loop fusion | flops 8 | bytes 52 | tf_op jit(solution)/shard_map/convert_element_type | solution.py:115
  11.6 3.5 %collective-permute-done = f32[1024,128]{1,0:T(8,128)S(1)} collective-permute-done((f32[1024,128]{1,0:T(8,128)}, f32[1024,128]{1,0:T(8,128)S(1)}, u32[]{:S(2)}, u32[]{:S(2)}) %collective-permute-start) | collective-permute-done | bytes 524320 | tf_op jit(solution)/shard_map/ppermute | solution.py:63
  15.1 1.5 %collective-permute-done.7 = f32[1024,128]{1,0:T(8,128)S(1)} collective-permute-done((f32[1024,128]{1,0:T(8,128)}, f32[1024,128]{1,0:T(8,128)S(1)}, u32[]{:S(2)}, u32[]{:S(2)}) %collective-permute-start.7) | collective-permute-done | bytes 524320 | tf_op jit(solution)/shard_map/ppermute | solution.py:66
  16.6 1.5 %collective-permute-start.9 = (f32[1024,128]{1,0:T(8,128)S(1)}, f32[1024,128]{1,0:T(8,128)S(1)}, u32[]{:S(2)}, u32[]{:S(2)}) collective-permute-start(f32[1024,128]{1,0:T(8,128)S(1)} %collective-permute-done), channel_id=1, source_target_pairs={{0,16},{16,0},{1,17},{17,1},{2,18},{18,2},{3,19},{19,3},{4,20},{20... | collective-permute-start | bytes 1572872 | tf_op jit(solution)/shard_map/ppermute | solution.py:66
  18.1 1.6 %collective-permute-start.2 = (f32[512,128]{1,0:T(8,128)S(1)}, f32[512,128]{1,0:T(8,128)S(1)}, u32[]{:S(2)}, u32[]{:S(2)}) collective-permute-start(f32[512,128]{1,0:T(8,128)S(1)} %get-tuple-element.18), channel_id=1, source_target_pairs={{0,4},{2,6},{4,0},{6,2},{8,12},{10,14},{12,8},{14,10},{1,5},{3,7},... | collective-permute-start | bytes 786440 | tf_op jit(solution)/shard_map/ppermute | solution.py:60
  19.8 0.1 pad_maximum_fusion.3
  19.9 0.0 copy-start
  19.9 0.7 %collective-permute-done.1 = f32[512,128]{1,0:T(8,128)S(1)} collective-permute-done((f32[512,128]{1,0:T(8,128)S(1)}, f32[512,128]{1,0:T(8,128)S(1)}, u32[]{:S(2)}, u32[]{:S(2)}) %collective-permute-start.1) | collective-permute-done | bytes 262176 | tf_op jit(solution)/shard_map/ppermute | solution.py:60
  20.7 10.5 %collective-permute-done.2 = f32[512,128]{1,0:T(8,128)S(1)} collective-permute-done((f32[512,128]{1,0:T(8,128)S(1)}, f32[512,128]{1,0:T(8,128)S(1)}, u32[]{:S(2)}, u32[]{:S(2)}) %collective-permute-start.2) | collective-permute-done | bytes 262176 | tf_op jit(solution)/shard_map/ppermute | solution.py:60
  31.2 0.0 collective-permute-done.3
  31.2 0.0 collective-permute-done.9
  31.2 0.1 constant_dynamic-slice_fusion.3
  31.3 0.6 collective-permute-start.5
  31.9 0.1 collective-permute-start.10
  32.0 0.6 collective-permute-done.8
  32.7 0.4 collective-permute-done.5
  33.1 0.7 %collective-permute-start.11 = (f32[512,256]{1,0:T(8,128)S(1)}, f32[512,256]{1,0:T(8,128)S(1)}, u32[]{:S(2)}, u32[]{:S(2)}) collective-permute-start(f32[512,256]{1,0:T(8,128)S(1)} %pad_maximum_fusion.3), channel_id=1, source_target_pairs={{4,8},{6,10},{8,4},{10,6},{5,9},{7,11},{9,5},{11,7},{20,24},{22,26... | collective-permute-start | bytes 1572872 | tf_op jit(solution)/shard_map/ppermute | solution.py:60
  33.7 1.3 %collective-permute-start.12 = (f32[512,256]{1,0:T(8,128)S(1)}, f32[512,256]{1,0:T(8,128)S(1)}, u32[]{:S(2)}, u32[]{:S(2)}) collective-permute-start(f32[512,256]{1,0:T(8,128)S(1)} %get-tuple-element.15), channel_id=1, source_target_pairs={{4,0},{6,2},{8,12},{10,14},{5,1},{7,3},{9,13},{11,15},{20,16},{22,... | collective-permute-start | bytes 1572872 | tf_op jit(solution)/shard_map/ppermute | solution.py:60
  35.0 0.1 maximum_bitcast_fusion
  35.1 0.1 maximum_bitcast_fusion.1
  35.2 0.2 maximum_select_fusion
  35.4 0.3 broadcast_multiply_fusion
  35.7 0.2 dynamic-slice_bitcast_fusion.1
  36.0 0.8 %fusion.7 = f32[512,256]{1,0:T(8,128)S(1)} fusion(f32[512,768]{1,0:T(8,128)S(1)} %get-tuple-element.46, f32[256,256]{1,0:T(8,128)S(1)} %get-tuple-element.34, f32[256,256]{1,0:T(8,128)S(1)} %get-tuple-element.32, f32[256,256]{1,0:T(8,128)S(1)} %get-tuple-element.30), kind=kOutput, calls=%fused_computation.16 | convolution fusion | flops 604372992 | bytes 2883584 | tf_op jit(solution)/shard_map/dot_general | solution.py:8
  36.8 0.8 %fusion.1 = f32[512,256]{1,0:T(8,128)S(1)} fusion(f32[512,768]{1,0:T(8,128)S(1)} %get-tuple-element.46, f32[256,256]{1,0:T(8,128)S(1)} %get-tuple-element.33, f32[256,256]{1,0:T(8,128)S(1)} %get-tuple-element.31, f32[256,256]{1,0:T(8,128)S(1)} %get-tuple-element.29), kind=kOutput, calls=%fused_computation.10 | convolution fusion | flops 604372992 | bytes 2883584 | tf_op jit(solution)/shard_map/dot_general | solution.py:8
  37.7 0.0 copy-start.1
  37.7 13.3 %collective-permute-done.12 = f32[512,256]{1,0:T(8,128)S(1)} collective-permute-done((f32[512,256]{1,0:T(8,128)S(1)}, f32[512,256]{1,0:T(8,128)S(1)}, u32[]{:S(2)}, u32[]{:S(2)}) %collective-permute-start.12) | collective-permute-done | bytes 524320 | tf_op jit(solution)/shard_map/ppermute | solution.py:60
  51.0 0.1 broadcast_select_fusion
  51.0 0.4 convolution_add_fusion
  51.4 0.1 collective-permute-start.13
  51.5 0.6 dynamic_slice.76
  54.1 0.0 copy-start.2
  54.1 0.5 fusion.40
  54.6 0.6 collective-permute-start.15
  55.2 1.6 %collective-permute-start.14 = (f32[512,128]{1,0:T(8,128)S(1)}, f32[512,128]{1,0:T(8,128)S(1)}, u32[]{:S(2)}, u32[]{:S(2)}) collective-permute-start(f32[512,128]{1,0:T(8,128)S(1)} %get-tuple-element.28), channel_id=1, source_target_pairs={{0,2},{2,0},{4,6},{6,4},{8,10},{10,8},{12,14},{14,12},{1,3},{3,1},... | collective-permute-start | bytes 786440 | tf_op jit(solution)/shard_map/ppermute | solution.py:63
  56.8 1.4 %collective-permute-done.15 = f32[1,128]{1,0:T(1,128)S(1)} collective-permute-done((f32[1,128]{1,0:T(1,128)S(1)}, f32[1,128]{1,0:T(1,128)S(1)}, u32[]{:S(2)}, u32[]{:S(2)}) %collective-permute-start.15) | collective-permute-done | bytes 544 | tf_op jit(solution)/shard_map/ppermute | solution.py:63
  58.2 0.5 collective-permute-start.16
  58.7 0.6 dynamic_slice.98
  59.9 1.8 %collective-permute-done.16 = f32[1,128]{1,0:T(1,128)S(1)} collective-permute-done((f32[1,128]{1,0:T(1,128)S(1)}, f32[1,128]{1,0:T(1,128)S(1)}, u32[]{:S(2)}, u32[]{:S(2)}) %collective-permute-start.16) | collective-permute-done | bytes 544 | tf_op jit(solution)/shard_map/ppermute | solution.py:66
  61.7 2.0 %collective-permute-done.14 = f32[512,128]{1,0:T(8,128)S(1)} collective-permute-done((f32[512,128]{1,0:T(8,128)S(1)}, f32[512,128]{1,0:T(8,128)S(1)}, u32[]{:S(2)}, u32[]{:S(2)}) %collective-permute-start.14) | collective-permute-done | bytes 262176 | tf_op jit(solution)/shard_map/ppermute | solution.py:63
  63.7 0.9 %fusion.16 = f32[1024,128]{1,0:T(8,128)} fusion(f32[2,512,128]{2,1,0:T(8,128)S(1)} %fusion.14, f32[]{:T(128)} %bitcast.44, f32[128]{0:T(128)S(1)} %add_bitcast_fusion), kind=kLoop, calls=%fused_computation.39 | loop fusion | flops 393216 | bytes 1049092 | tf_op jit(solution)/shard_map/max | solution.py:140
  (26 shorter events, 0.5 us)
Async XLA Ops:
  0.0 15.1 %collective-permute-start = (f32[1024,128]{1,0:T(8,128)}, f32[1024,128]{1,0:T(8,128)S(1)}, u32[]{:S(2)}, u32[]{:S(2)}) collective-permute-start(f32[1024,128]{1,0:T(8,128)} %param.4), channel_id=1, source_target_pairs={{0,2},{2,0},{4,6},{6,4},{8,10},{10,8},{12,14},{14,12},{1,3},{3,1},... | collective-permute-start | bytes 1572872 | tf_op jit(solution)/shard_map/ppermute | solution.py:63
  3.0 13.6 %collective-permute-start.7 = (f32[1024,128]{1,0:T(8,128)}, f32[1024,128]{1,0:T(8,128)S(1)}, u32[]{:S(2)}, u32[]{:S(2)}) collective-permute-start(f32[1024,128]{1,0:T(8,128)} %param.4), channel_id=1, source_target_pairs={{0,16},{16,0},{1,17},{17,1},{2,18},{18,2},{3,19},{19,3},{4,20},{20... | collective-permute-start | bytes 1572872 | tf_op jit(solution)/shard_map/ppermute | solution.py:66
  5.5 25.6 %collective-permute-start.3 = (f32[512,128]{1,0:T(8,128)S(1)}, f32[512,128]{1,0:T(8,128)S(1)}, u32[]{:S(2)}, u32[]{:S(2)}) collective-permute-start(f32[512,128]{1,0:T(8,128)S(1)} %get-tuple-element.11), channel_id=1, source_target_pairs={{0,8},{2,10},{4,12},{6,14},{8,0},{10,2},{12,4},{14,6},{1,9},{3,11}... | collective-permute-start | bytes 786440 | tf_op jit(solution)/shard_map/ppermute | solution.py:60
  8.2 12.4 %collective-permute-start.1 = (f32[512,128]{1,0:T(8,128)S(1)}, f32[512,128]{1,0:T(8,128)S(1)}, u32[]{:S(2)}, u32[]{:S(2)}) collective-permute-start(f32[512,128]{1,0:T(8,128)S(1)} %get-tuple-element.11), channel_id=1, source_target_pairs={{0,4},{2,6},{4,0},{6,2},{8,12},{10,14},{12,8},{14,10},{1,5},{3,7},... | collective-permute-start | bytes 786440 | tf_op jit(solution)/shard_map/ppermute | solution.py:60
  9.8 22.1 %collective-permute-start.4 = (f32[512,128]{1,0:T(8,128)S(1)}, f32[512,128]{1,0:T(8,128)S(1)}, u32[]{:S(2)}, u32[]{:S(2)}) collective-permute-start(f32[512,128]{1,0:T(8,128)S(1)} %get-tuple-element.43), channel_id=1, source_target_pairs={{0,10},{2,8},{4,14},{6,12},{8,2},{10,0},{12,6},{14,4},{1,11},{3,9}... | collective-permute-start | bytes 786440 | tf_op jit(solution)/shard_map/ppermute | solution.py:60
  16.6 14.7 %collective-permute-start.9 = (f32[1024,128]{1,0:T(8,128)S(1)}, f32[1024,128]{1,0:T(8,128)S(1)}, u32[]{:S(2)}, u32[]{:S(2)}) collective-permute-start(f32[1024,128]{1,0:T(8,128)S(1)} %collective-permute-done), channel_id=1, source_target_pairs={{0,16},{16,0},{1,17},{17,1},{2,18},{18,2},{3,19},{19,3},{4,20},{20... | collective-permute-start | bytes 1572872 | tf_op jit(solution)/shard_map/ppermute | solution.py:66
  18.1 13.0 %collective-permute-start.2 = (f32[512,128]{1,0:T(8,128)S(1)}, f32[512,128]{1,0:T(8,128)S(1)}, u32[]{:S(2)}, u32[]{:S(2)}) collective-permute-start(f32[512,128]{1,0:T(8,128)S(1)} %get-tuple-element.18), channel_id=1, source_target_pairs={{0,4},{2,6},{4,0},{6,2},{8,12},{10,14},{12,8},{14,10},{1,5},{3,7},... | collective-permute-start | bytes 786440 | tf_op jit(solution)/shard_map/ppermute | solution.py:60
  19.9 11.3 %copy-start = (f32[1024,128]{1,0:T(8,128)S(1)}, f32[1024,128]{1,0:T(8,128)}, u32[]{:S(2)}) copy-start(f32[1024,128]{1,0:T(8,128)} %param.4) | copy-start | bytes 1572868
  20.6 11.3 %collective-permute-start.6 = (f32[512,128]{1,0:T(8,128)S(1)}, f32[512,128]{1,0:T(8,128)S(1)}, u32[]{:S(2)}, u32[]{:S(2)}) collective-permute-start(f32[512,128]{1,0:T(8,128)S(1)} %bitcast.109), channel_id=1, source_target_pairs={{0,1},{1,0},{2,3},{3,2},{4,5},{5,4},{6,7},{7,6},{8,9},{9,8},{10,11... | collective-permute-start | bytes 786440 | tf_op jit(solution)/shard_map/ppermute | solution.py:69
  31.1 1.5 %collective-permute-start.8 = (f32[512,128]{1,0:T(8,128)S(1)}, f32[512,128]{1,0:T(8,128)S(1)}, u32[]{:S(2)}, u32[]{:S(2)}) collective-permute-start(f32[512,128]{1,0:T(8,128)S(1)} %bitcast.108), channel_id=1, source_target_pairs={{0,1},{1,0},{2,3},{3,2},{4,5},{5,4},{6,7},{7,6},{8,9},{9,8},{10,11... | collective-permute-start | bytes 786440 | tf_op jit(solution)/shard_map/ppermute | solution.py:69
  31.3 1.7 %collective-permute-start.5 = (f32[512,128]{1,0:T(8,128)S(1)}, f32[512,128]{1,0:T(8,128)S(1)}, u32[]{:S(2)}, u32[]{:S(2)}) collective-permute-start(f32[512,128]{1,0:T(8,128)S(1)} %bitcast.115), channel_id=1, source_target_pairs={{0,1},{1,0},{2,3},{3,2},{4,5},{5,4},{6,7},{7,6},{8,9},{9,8},{10,11... | collective-permute-start | bytes 786440 | tf_op jit(solution)/shard_map/ppermute | solution.py:69
  31.9 3.2 %collective-permute-start.10 = (f32[512,128]{1,0:T(8,128)S(1)}, f32[512,128]{1,0:T(8,128)S(1)}, u32[]{:S(2)}, u32[]{:S(2)}) collective-permute-start(f32[512,128]{1,0:T(8,128)S(1)} %bitcast.113), channel_id=1, source_target_pairs={{0,1},{1,0},{2,3},{3,2},{4,5},{5,4},{6,7},{7,6},{8,9},{9,8},{10,11... | collective-permute-start | bytes 786440 | tf_op jit(solution)/shard_map/ppermute | solution.py:69
  33.1 4.6 %collective-permute-start.11 = (f32[512,256]{1,0:T(8,128)S(1)}, f32[512,256]{1,0:T(8,128)S(1)}, u32[]{:S(2)}, u32[]{:S(2)}) collective-permute-start(f32[512,256]{1,0:T(8,128)S(1)} %pad_maximum_fusion.3), channel_id=1, source_target_pairs={{4,8},{6,10},{8,4},{10,6},{5,9},{7,11},{9,5},{11,7},{20,24},{22,26... | collective-permute-start | bytes 1572872 | tf_op jit(solution)/shard_map/ppermute | solution.py:60
  33.7 17.2 %collective-permute-start.12 = (f32[512,256]{1,0:T(8,128)S(1)}, f32[512,256]{1,0:T(8,128)S(1)}, u32[]{:S(2)}, u32[]{:S(2)}) collective-permute-start(f32[512,256]{1,0:T(8,128)S(1)} %get-tuple-element.15), channel_id=1, source_target_pairs={{4,0},{6,2},{8,12},{10,14},{5,1},{7,3},{9,13},{11,15},{20,16},{22,... | collective-permute-start | bytes 1572872 | tf_op jit(solution)/shard_map/ppermute | solution.py:60
  37.7 13.8 %copy-start.1 = (s32[4]{0:T(128)S(1)}, s32[4]{0:T(128)}, u32[]{:S(2)}) copy-start(s32[4]{0:T(128)} %param.7) | copy-start | bytes 52
  51.4 2.6 %collective-permute-start.13 = (f32[512,256]{1,0:T(8,128)S(1)}, f32[512,256]{1,0:T(8,128)S(1)}, u32[]{:S(2)}, u32[]{:S(2)}) collective-permute-start(f32[512,256]{1,0:T(8,128)S(1)} %convolution_add_fusion), channel_id=1, source_target_pairs={{0,1},{1,0},{2,3},{3,2},{4,5},{5,4},{6,7},{7,6},{8,9},{9,8},{10,11... | collective-permute-start | bytes 1572872 | tf_op jit(solution)/shard_map/ppermute | solution.py:69
  54.1 4.7 %copy-start.2 = (s32[4]{0:T(128)S(1)}, s32[4]{0:T(128)}, u32[]{:S(2)}) copy-start(s32[4]{0:T(128)} %param.6) | copy-start | bytes 52
  54.6 3.6 %collective-permute-start.15 = (f32[1,128]{1,0:T(1,128)S(1)}, f32[1,128]{1,0:T(1,128)S(1)}, u32[]{:S(2)}, u32[]{:S(2)}) collective-permute-start(f32[1,128]{1,0:T(1,128)S(1)} %slice.59), channel_id=1, source_target_pairs={{0,2},{2,0},{4,6},{6,4},{8,10},{10,8},{12,14},{14,12},{1,3},{3,1},... | collective-permute-start | bytes 1544 | tf_op jit(solution)/shard_map/ppermute | solution.py:63
  55.2 8.5 %collective-permute-start.14 = (f32[512,128]{1,0:T(8,128)S(1)}, f32[512,128]{1,0:T(8,128)S(1)}, u32[]{:S(2)}, u32[]{:S(2)}) collective-permute-start(f32[512,128]{1,0:T(8,128)S(1)} %get-tuple-element.28), channel_id=1, source_target_pairs={{0,2},{2,0},{4,6},{6,4},{8,10},{10,8},{12,14},{14,12},{1,3},{3,1},... | collective-permute-start | bytes 786440 | tf_op jit(solution)/shard_map/ppermute | solution.py:63
  58.2 3.5 %collective-permute-start.16 = (f32[1,128]{1,0:T(1,128)S(1)}, f32[1,128]{1,0:T(1,128)S(1)}, u32[]{:S(2)}, u32[]{:S(2)}) collective-permute-start(f32[1,128]{1,0:T(1,128)S(1)} %slice_add_fusion), channel_id=1, source_target_pairs={{0,16},{16,0},{1,17},{17,1},{2,18},{18,2},{3,19},{19,3},{4,20},{20... | collective-permute-start | bytes 1544 | tf_op jit(solution)/shard_map/ppermute | solution.py:66

commit v3 on v0

--- a/solution.py
+++ b/solution.py
@@ -5,11 +5,17 @@
 
 
 def multiply(left, right):
-    exact = lax.Precision.HIGHEST
-    return jnp.dot(left, right, precision=exact, preferred_element_type=jnp.float32)
+    return jnp.dot(left, right, precision=lax.Precision.HIGH, preferred_element_type=jnp.float32)
 
 
-def on_device(flow, pattern, prune_level, power):
+def raise_to(value, exponent):
+    square = value * value
+    low = jnp.where(exponent == 1, value, square)
+    high = square * jnp.where(exponent == 3, value, square)
+    return jnp.where(exponent <= 2, low, high)
+
+
+def general(flow, pattern, prune_level, power):
     rows, width = flow.shape
     layers = lax.axis_size("layer")
     order = rows * lax.axis_size("row")
@@ -43,9 +49,90 @@
     return jnp.maximum(order * inflated / totals[None, :] - levels[None, :], 0.0)
 
 
+def squared(flow, pattern, prune_level, power):
+    rows, width = flow.shape
+    half = rows // 2
+    order = rows * 2
+    x, c, l = lax.axis_index("row"), lax.axis_index("col"), lax.axis_index("layer")
+    y, z = c % 2, c // 2
+    p = z % 2
+
+    def along_z(value, distance):
+        return lax.ppermute(value, "col", [(i, i ^ (2 * distance)) for i in range(8)])
+
+    def along_y(value):
+        return lax.ppermute(value, "col", [(i, i ^ 1) for i in range(8)])
+
+    def along_x(value):
+        return lax.ppermute(value, "row", [(0, 1), (1, 0)])
+
+    def across(value):
+        return lax.ppermute(value, "layer", [(0, 1), (1, 0)])
+
+    def after(value, *earlier):
+        return lax.optimization_barrier((value, *earlier))[0]
+
+    def both_layers(value):
+        grouped = value.reshape(value.shape[0] // (2 * width), 2, width, width)
+        keep, give = [
+            lax.dynamic_index_in_dim(grouped, i, 1, False).reshape(value.shape[0] // 2, width)
+            for i in (l, 1 - l)
+        ]
+        return jnp.stack([keep, across(give)])
+
+    own = lax.dynamic_slice_in_dim(flow, p * half, half, 0)
+    rest = lax.dynamic_slice_in_dim(flow, (1 - p) * half, half, 0)
+    side_raw = along_z(flow, 1)
+    two = along_z(own, 2)
+    far = along_x(flow)
+    own_y = along_y(own)
+    three = along_z(after(rest, own_y), 3)
+    two_y = along_y(two)
+    far_side = along_x(after(side_raw, far))
+    one = lax.dynamic_slice_in_dim(side_raw, p * half, half, 0)
+    one_y = along_y(one)
+    three_y = along_y(after(three, two_y, one_y))
+    near = both_layers(after(flow, own_y))
+    near_x = both_layers(far)
+    side = both_layers(side_raw)
+    side_x = both_layers(far_side)
+
+    here = jnp.stack([near, side], axis=1)
+    there = jnp.stack([near_x, side_x], axis=1)
+    right = jnp.where(x == 0, jnp.stack([here, there], 2), jnp.stack([there, here], 2))
+    right = right.reshape(2, 2, 4, 2, width, width)
+    stored = pattern[2 * x + p][None, :] * jnp.stack([pattern[:, z], pattern[:, z ^ 1]])
+    right = right * stored.astype(jnp.float32)[None, :, :, None, None, None]
+    kept, sent = [], []
+    for i in range(4):
+        chosen = lax.dynamic_index_in_dim(right, z ^ i, 2, False)
+        first = lax.dynamic_index_in_dim(chosen, y, 2, False)
+        second = lax.dynamic_index_in_dim(chosen, 1 - y, 2, False)
+        both = jnp.concatenate([first, second], axis=2)
+        kept.append(jnp.concatenate([both[0, 0], both[0, 1]], axis=1))
+        sent.append(jnp.concatenate([both[1, 0], both[1, 1]], axis=1))
+
+    left = jnp.concatenate([own, own_y, one, one_y, two, two_y], axis=1)
+    early_sent = multiply(left, jnp.concatenate(sent[:3]))
+    early_kept = multiply(left, jnp.concatenate(kept[:3]))
+    last = jnp.concatenate([three, after(three_y, early_sent, early_kept)], axis=1)
+    outgoing = early_sent + multiply(last, sent[3])
+    product = early_kept + multiply(last, kept[3]) + across(outgoing)
+    mine = raise_to(product[:, :width], power[z])
+    other = raise_to(product[:, width:], power[z ^ 1])
+    arrived = along_z(other, 1)
+    row_sum = jnp.sum(mine, axis=0, keepdims=True) + along_z(jnp.sum(other, axis=0, keepdims=True), 1)
+    totals = row_sum + along_x(row_sum)
+    whole = jnp.where(p == 0, jnp.stack([mine, arrived]), jnp.stack([arrived, mine])).reshape(rows, width)
+    level = prune_level[z].astype(jnp.float32) / 8.0
+    return jnp.maximum(order * whole / totals - level, 0.0)
+
+
 def solution(mesh):
+    shape = dict(mesh.shape)
+    special = shape == {"row": 2, "col": 8, "layer": 2}
     return jax.shard_map(
-        on_device,
+        squared if special else general,
         mesh=mesh,
         in_specs=(P("row", ("col", "layer")), P(), P(), P()),
         out_specs=P("row", ("col", "layer")),

time: 146 us -> 58.5 us (0.40)
  waiting for transfers between devices: 108 us -> 23.6 us
  starting transfers between devices: 0.08 us -> 19.7 us
  blocking collectives: 9.09 us -> 0 us
  between operations: 13.2 us -> 4.62 us
  matrix products: 9.94 us -> 2.42 us
  local copies, waits for them, and re-layouts: 1.31 us -> 5.18 us
  other arithmetic: 4.05 us -> 2 us
    all_gather x2 -> x0, waiting for transfers between devices: 100 us -> none  [the longest x1 77.1 us: on_device(): strip = lax.all_gather(masked, 'col', axis=1, tiled=True)]
    ppermute x0 -> x17, waiting for transfers between devices: none -> 23.6 us  [the longest x5 12.8 us: along_z(): return lax.ppermute(value, 'col', [(i, i ^ 2 * distance) for i in range(8)])]
    ppermute x0 -> x17, starting transfers between devices: none -> 19.7 us  [the longest x5 8.91 us: along_z(): return lax.ppermute(value, 'col', [(i, i ^ 2 * distance) for i in range(8)])]
    dot_general x5 -> x4, matrix products: 9.94 us -> 2.42 us  [multiply(): jnp.dot(left, right, precision=lax.Precision.HIGH, preferred_element_type...]
    reduce_scatter x1 -> x0, waiting for transfers between devices: 6.61 us -> none  [on_device(): lax.psum_scatter(partial_value, 'layer', scatter_dimension=1, tiled=True)]
    psum x1 -> x0, blocking collectives: 4.94 us -> none  [on_device(): totals = lax.psum(jnp.sum(inflated, axis=0), 'row')]
    all_to_all x1 -> x0, blocking collectives: 4.15 us -> none  [on_device(): lax.all_to_all(parted, 'layer', split_axis=1, concat_axis=3, tiled=True)]
    dynamic_slice x0 -> x6, local copies, waits for them, and re-layouts: none -> 2.31 us  [the longest x1 0.97 us: squared(): pattern[:, z]]
  transfers between devices with their start and end apart: 3 -> 17, of which waited for: 3 -> 10; matrix products, arithmetic and copies ran while one was open for 0% -> 13% of each run, Pallas kernels for 0% -> 0%
where the time goes in v3:
time: 58.5 us; the launch traced here: 57.5 us
  waiting for transfers between devices  23.6 us (40%)
  starting transfers between devices  19.7 us (34%)
  local copies, waits for them, and re-layouts  5.18 us (9%)
  between operations  4.62 us (8%)
  matrix products  2.42 us (4%)
  other arithmetic  2 us (3%)
    ppermute x5, waiting for transfers between devices, along_z(): return lax.ppermute(value, 'col', [(i, i ^ 2 * distance) for i in range(8)])  12.8 us
    ppermute x4, waiting for transfers between devices, along_y(): return lax.ppermute(value, 'col', [(i, i ^ 1) for i in range(8)])  8.95 us
    ppermute x5, starting transfers between devices, along_z(): return lax.ppermute(value, 'col', [(i, i ^ 2 * distance) for i in range(8)])  8.91 us
    ppermute x4, starting transfers between devices, along_y(): return lax.ppermute(value, 'col', [(i, i ^ 1) for i in range(8)])  5.13 us
    ppermute x3, starting transfers between devices, along_x(): return lax.ppermute(value, 'row', [(0, 1), (1, 0)])  4.56 us
    dot_general x4, matrix products, multiply(): jnp.dot(left, right, precision=lax.Precision.HIGH, preferred_element_type...  2.42 us
    unnamed x12, local copies, waits for them, and re-layouts  1.91 us
  transfers between devices with their start and end apart: 17, of which 10 were waited for; matrix products, arithmetic and copies ran while one was open for 13% of the time, Pallas kernels for 0%

profile of v3, /device:TPU:0, one launch (start us, length us, event | category | flops | bytes accessed | tf_op | source)
XLA Modules:
  0.0 57.5 jit_solution(15916432227589022662)
XLA Ops:
  0.0 3.0 %collective-permute-start.1 = (f32[1024,128]{1,0:T(8,128)}, f32[1024,128]{1,0:T(8,128)S(1)}, u32[]{:S(2)}, u32[]{:S(2)}) collective-permute-start(f32[1024,128]{1,0:T(8,128)} %param.4), channel_id=1, source_target_pairs={{0,4},{2,6},{4,0},{6,2},{8,12},{10,14},{12,8},{14,10},{1,5},{3,7},... | collective-permute-start | bytes 1572872 | tf_op jit(solution)/shard_map/ppermute | solution.py:61
  3.0 1.5 %collective-permute-start.7 = (f32[1024,128]{1,0:T(8,128)}, f32[1024,128]{1,0:T(8,128)S(1)}, u32[]{:S(2)}, u32[]{:S(2)}) collective-permute-start(f32[1024,128]{1,0:T(8,128)} %param.4), channel_id=1, source_target_pairs={{0,16},{16,0},{1,17},{17,1},{2,18},{18,2},{3,19},{19,3},{4,20},{20... | collective-permute-start | bytes 1572872 | tf_op jit(solution)/shard_map/ppermute | solution.py:67
  4.5 1.8 %constant_dynamic-update-slice_fusion.5 = (f32[512,768]{1,0:T(8,128)S(1)}, f32[512,128]{1,0:T(8,128)}, f32[512,128]{1,0:T(8,128)S(1)}) fusion(f32[1024,128]{1,0:T(8,128)} %param.4, s32[]{:T(128)S(6)} %select_n.147, s32[]{:T(128)S(6)} %select_n.164), kind=kLoop, calls=%fused_computation.125 | loop fusion | bytes 1310728
  6.3 2.6 %collective-permute-start.3 = (f32[512,128]{1,0:T(8,128)}, f32[512,128]{1,0:T(8,128)S(1)}, u32[]{:S(2)}, u32[]{:S(2)}) collective-permute-start(f32[512,128]{1,0:T(8,128)} %get-tuple-element.22), channel_id=1, source_target_pairs={{0,8},{2,10},{4,12},{6,14},{8,0},{10,2},{12,4},{14,6},{1,9},{3,11}... | collective-permute-start | bytes 786440 | tf_op jit(solution)/shard_map/ppermute | solution.py:61
  8.9 1.5 %collective-permute-start = (f32[512,128]{1,0:T(8,128)}, f32[512,128]{1,0:T(8,128)S(1)}, u32[]{:S(2)}, u32[]{:S(2)}) collective-permute-start(f32[512,128]{1,0:T(8,128)} %get-tuple-element.22), channel_id=1, source_target_pairs={{0,2},{2,0},{4,6},{6,4},{8,10},{10,8},{12,14},{14,12},{1,3},{3,1},... | collective-permute-start | bytes 786440 | tf_op jit(solution)/shard_map/ppermute | solution.py:64
  10.4 0.7 %fusion.69 = s32[4]{0:T(128)S(1)} fusion(s32[4,4]{1,0:T(4,128)} %param.5, s32[]{:T(128)S(6)} %select_n.153), kind=kLoop, calls=%fused_computation.146 | loop fusion | bytes 36 | tf_op jit(solution)/shard_map/mul | solution.py:104
  11.1 1.0 %fusion.66 = (s32[4]{0:T(128)S(1)}, s32[4]{0:T(128)S(1)}) fusion(s32[4,4]{1,0:T(4,128)} %param.5, s32[]{:T(128)S(6)} %select_n.144, s32[]{:T(128)S(6)} %select_n.154), kind=kLoop, calls=%fused_computation.142 | loop fusion | bytes 72 | tf_op jit(solution)/shard_map/dynamic_slice | solution.py:104
  12.1 4.2 %collective-permute-done = f32[512,128]{1,0:T(8,128)S(1)} collective-permute-done((f32[512,128]{1,0:T(8,128)}, f32[512,128]{1,0:T(8,128)S(1)}, u32[]{:S(2)}, u32[]{:S(2)}) %collective-permute-start) | collective-permute-done | bytes 262176 | tf_op jit(solution)/shard_map/ppermute | solution.py:64
  16.3 0.2 collective-permute-start.11
  16.5 4.8 %collective-permute-done.3 = f32[512,128]{1,0:T(8,128)S(1)} collective-permute-done((f32[512,128]{1,0:T(8,128)}, f32[512,128]{1,0:T(8,128)S(1)}, u32[]{:S(2)}, u32[]{:S(2)}) %collective-permute-start.3) | collective-permute-done | bytes 262176 | tf_op jit(solution)/shard_map/ppermute | solution.py:61
  21.3 1.5 %collective-permute-start.4 = (f32[512,128]{1,0:T(8,128)S(1)}, f32[512,128]{1,0:T(8,128)S(1)}, u32[]{:S(2)}, u32[]{:S(2)}) collective-permute-start(f32[512,128]{1,0:T(8,128)S(1)} %collective-permute-done.3), channel_id=1, source_target_pairs={{0,2},{2,0},{4,6},{6,4},{8,10},{10,8},{12,14},{14,12},{1,3},{3,1},... | collective-permute-start | bytes 786440 | tf_op jit(solution)/shard_map/ppermute | solution.py:64
  22.9 0.0 collective-permute-done.1
  22.9 1.6 %collective-permute-start.9 = (f32[1024,128]{1,0:T(8,128)S(1)}, f32[1024,128]{1,0:T(8,128)S(1)}, u32[]{:S(2)}, u32[]{:S(2)}) collective-permute-start(f32[1024,128]{1,0:T(8,128)S(1)} %collective-permute-done.1), channel_id=1, source_target_pairs={{0,16},{16,0},{1,17},{17,1},{2,18},{18,2},{3,19},{19,3},{4,20},{20... | collective-permute-start | bytes 1572872 | tf_op jit(solution)/shard_map/ppermute | solution.py:67
  24.5 0.6 collective-permute-start.2
  25.1 0.0 copy-start
  25.1 0.1 collective-permute-start.6
  25.2 3.4 %collective-permute-done.11 = f32[512,128]{1,0:T(8,128)S(1)} collective-permute-done((f32[512,128]{1,0:T(8,128)S(1)}, f32[512,128]{1,0:T(8,128)S(1)}, u32[]{:S(2)}, u32[]{:S(2)}) %collective-permute-start.11) | collective-permute-done | bytes 262176 | tf_op jit(solution)/shard_map/ppermute | solution.py:61
  28.7 1.5 %collective-permute-done.4 = f32[512,128]{1,0:T(8,128)S(1)} collective-permute-done((f32[512,128]{1,0:T(8,128)S(1)}, f32[512,128]{1,0:T(8,128)S(1)}, u32[]{:S(2)}, u32[]{:S(2)}) %collective-permute-start.4) | collective-permute-done | bytes 262176 | tf_op jit(solution)/shard_map/ppermute | solution.py:64
  30.2 3.3 %collective-permute-done.2 = f32[512,128]{1,0:T(8,128)S(1)} collective-permute-done((f32[512,128]{1,0:T(8,128)S(1)}, f32[512,128]{1,0:T(8,128)S(1)}, u32[]{:S(2)}, u32[]{:S(2)}) %collective-permute-start.2) | collective-permute-done | bytes 262176 | tf_op jit(solution)/shard_map/ppermute | solution.py:64
  33.4 1.5 %collective-permute-start.12 = (f32[512,128]{1,0:T(8,128)S(1)}, f32[512,128]{1,0:T(8,128)S(1)}, u32[]{:S(2)}, u32[]{:S(2)}) collective-permute-start(f32[512,128]{1,0:T(8,128)S(1)} %collective-permute-done.11), channel_id=1, source_target_pairs={{0,2},{2,0},{4,6},{6,4},{8,10},{10,8},{12,14},{14,12},{1,3},{3,1},... | collective-permute-start | bytes 786440 | tf_op jit(solution)/shard_map/ppermute | solution.py:64
  35.0 0.1 constant_dynamic-slice_fusion.5
  35.1 0.1 collective-permute-start.10
  35.2 0.0 collective-permute-done.6
  35.3 0.6 collective-permute-start.5
  35.9 0.8 %collective-permute-done.10 = f32[512,128]{1,0:T(8,128)S(1)} collective-permute-done((f32[512,128]{1,0:T(8,128)S(1)}, f32[512,128]{1,0:T(8,128)S(1)}, u32[]{:S(2)}, u32[]{:S(2)}) %collective-permute-start.10) | collective-permute-done | bytes 262176 | tf_op jit(solution)/shard_map/ppermute | solution.py:70
  36.8 0.1 maximum_bitcast_fusion.1
  36.8 0.3 collective-permute-done.5
  37.1 0.1 maximum_bitcast_fusion
  37.2 0.1 maximum_select_fusion
  37.4 0.4 broadcast_multiply_fusion
  37.7 0.2 dynamic-slice_bitcast_fusion.1
  38.1 0.8 %fusion.13 = f32[512,256]{1,0:T(8,128)S(1)} fusion(f32[512,768]{1,0:T(8,128)S(1)} %constant_dynamic-update-slice_fusion, f32[256,128]{1,0:T(8,128)S(1)} %get-tuple-element.47, f32[256,128]{1,0:T(8,128)S(1)} %get-tuple-element.48, f32[256,128]{1,0:T(8,128)S(1)} %get-tuple-element.43, f32[256,128]{1,0:T(8,128)S(1)} %get-tuple-element.44, ...), kind=kOutput, calls=%fused_computation.19 | convolution fusion | flops 604962816 | bytes 2883584 | tf_op jit(solution)/shard_map/dot_general | solution.py:8
  38.9 0.8 %fusion.1 = f32[512,256]{1,0:T(8,128)S(1)} fusion(f32[512,768]{1,0:T(8,128)S(1)} %constant_dynamic-update-slice_fusion, f32[256,128]{1,0:T(8,128)S(1)} %get-tuple-element.46, f32[256,128]{1,0:T(8,128)S(1)} %get-tuple-element.45, f32[256,128]{1,0:T(8,128)S(1)} %get-tuple-element.42, f32[256,128]{1,0:T(8,128)S(1)} %get-tuple-element.41, ...), kind=kOutput, calls=%fused_computation.7 | convolution fusion | flops 604962816 | bytes 2883584 | tf_op jit(solution)/shard_map/dot_general | solution.py:8
  39.8 0.0 collective-permute-done.12
  39.9 0.4 convolution_add_fusion
  40.3 0.4 collective-permute-start.13
  40.7 0.6 %fusion.76 = (s32[1]{0:T(128)}, s32[1]{0:T(128)}) fusion(s32[4]{0:T(128)S(1)} %copy-done.1, s32[]{:T(128)S(6)} %select_n.144, s32[]{:T(128)S(6)} %select_n.154), kind=kLoop, calls=%fused_computation.154 | loop fusion | bytes 24 | tf_op jit(solution)/shard_map/dynamic_slice | solution.py:121
  44.9 0.0 copy-start.2
  44.9 0.4 fusion
  45.3 0.1 fusion.74
  45.5 3.0 %collective-permute-start.15 = (f32[1,128]{1,0:T(1,128)S(1)}, f32[1,128]{1,0:T(1,128)S(1)}, u32[]{:S(2)}, u32[]{:S(2)}) collective-permute-start(f32[1,128]{1,0:T(1,128)S(1)} %bitcast.142), channel_id=1, source_target_pairs={{0,4},{2,6},{4,0},{6,2},{8,12},{10,14},{12,8},{14,10},{1,5},{3,7},... | collective-permute-start | bytes 1544 | tf_op jit(solution)/shard_map/ppermute | solution.py:61
  48.5 0.1 collective-permute-start.14
  48.6 1.4 %collective-permute-done.15 = f32[1,128]{1,0:T(1,128)S(1)} collective-permute-done((f32[1,128]{1,0:T(1,128)S(1)}, f32[1,128]{1,0:T(1,128)S(1)}, u32[]{:S(2)}, u32[]{:S(2)}) %collective-permute-start.15) | collective-permute-done | bytes 544 | tf_op jit(solution)/shard_map/ppermute | solution.py:61
  50.0 1.5 %collective-permute-start.16 = (f32[1,128]{1,0:T(1,128)S(1)}, f32[1,128]{1,0:T(1,128)S(1)}, u32[]{:S(2)}, u32[]{:S(2)}) collective-permute-start(f32[1,128]{1,0:T(1,128)S(1)} %bitcast_add_fusion), channel_id=1, source_target_pairs={{0,16},{16,0},{1,17},{17,1},{2,18},{18,2},{3,19},{19,3},{4,20},{20... | collective-permute-start | bytes 1544 | tf_op jit(solution)/shard_map/ppermute | solution.py:67
  51.5 0.6 %dynamic_slice.106 = s32[1]{0:T(128)} dynamic-slice(s32[4]{0:T(128)S(1)} %copy-done.2, s32[]{:T(128)S(6)} %select_n.144), dynamic_slice_sizes={1} | dynamic-slice | bytes 12 | tf_op jit(solution)/shard_map/dynamic_slice | solution.py:127
  52.7 0.8 %collective-permute-done.16 = f32[1,128]{1,0:T(1,128)S(1)} collective-permute-done((f32[1,128]{1,0:T(1,128)S(1)}, f32[1,128]{1,0:T(1,128)S(1)}, u32[]{:S(2)}, u32[]{:S(2)}) %collective-permute-start.16) | collective-permute-done | bytes 544 | tf_op jit(solution)/shard_map/ppermute | solution.py:67
  53.5 3.1 %collective-permute-done.14 = f32[512,128]{1,0:T(8,128)S(1)} collective-permute-done((f32[512,128]{1,0:T(8,128)S(1)}, f32[512,128]{1,0:T(8,128)S(1)}, u32[]{:S(2)}, u32[]{:S(2)}) %collective-permute-start.14) | collective-permute-done | bytes 262176 | tf_op jit(solution)/shard_map/ppermute | solution.py:61
  56.7 0.9 %fusion.27 = f32[1024,128]{1,0:T(8,128)} fusion(f32[2,512,128]{2,1,0:T(8,128)S(1)} %fusion.25, f32[]{:T(128)} %bitcast.60, f32[128]{0:T(128)S(1)} %add_bitcast_fusion), kind=kLoop, calls=%fused_computation.63 | loop fusion | flops 393216 | bytes 1049092 | tf_op jit(solution)/shard_map/max | solution.py:128
  (30 shorter events, 0.6 us)
Async XLA Ops:
  0.0 22.9 %collective-permute-start.1 = (f32[1024,128]{1,0:T(8,128)}, f32[1024,128]{1,0:T(8,128)S(1)}, u32[]{:S(2)}, u32[]{:S(2)}) collective-permute-start(f32[1024,128]{1,0:T(8,128)} %param.4), channel_id=1, source_target_pairs={{0,4},{2,6},{4,0},{6,2},{8,12},{10,14},{12,8},{14,10},{1,5},{3,7},... | collective-permute-start | bytes 1572872 | tf_op jit(solution)/shard_map/ppermute | solution.py:61
  3.0 19.9 %collective-permute-start.7 = (f32[1024,128]{1,0:T(8,128)}, f32[1024,128]{1,0:T(8,128)S(1)}, u32[]{:S(2)}, u32[]{:S(2)}) collective-permute-start(f32[1024,128]{1,0:T(8,128)} %param.4), channel_id=1, source_target_pairs={{0,16},{16,0},{1,17},{17,1},{2,18},{18,2},{3,19},{19,3},{4,20},{20... | collective-permute-start | bytes 1572872 | tf_op jit(solution)/shard_map/ppermute | solution.py:67
  6.3 15.0 %collective-permute-start.3 = (f32[512,128]{1,0:T(8,128)}, f32[512,128]{1,0:T(8,128)S(1)}, u32[]{:S(2)}, u32[]{:S(2)}) collective-permute-start(f32[512,128]{1,0:T(8,128)} %get-tuple-element.22), channel_id=1, source_target_pairs={{0,8},{2,10},{4,12},{6,14},{8,0},{10,2},{12,4},{14,6},{1,9},{3,11}... | collective-permute-start | bytes 786440 | tf_op jit(solution)/shard_map/ppermute | solution.py:61
  8.9 7.4 %collective-permute-start = (f32[512,128]{1,0:T(8,128)}, f32[512,128]{1,0:T(8,128)S(1)}, u32[]{:S(2)}, u32[]{:S(2)}) collective-permute-start(f32[512,128]{1,0:T(8,128)} %get-tuple-element.22), channel_id=1, source_target_pairs={{0,2},{2,0},{4,6},{6,4},{8,10},{10,8},{12,14},{14,12},{1,3},{3,1},... | collective-permute-start | bytes 786440 | tf_op jit(solution)/shard_map/ppermute | solution.py:64
  16.3 12.4 %collective-permute-start.11 = (f32[512,128]{1,0:T(8,128)S(1)}, f32[512,128]{1,0:T(8,128)S(1)}, u32[]{:S(2)}, u32[]{:S(2)}) collective-permute-start(f32[512,128]{1,0:T(8,128)S(1)} %get-tuple-element.12), channel_id=1, source_target_pairs={{0,12},{2,14},{4,8},{6,10},{8,4},{10,6},{12,0},{14,2},{1,13},{3,15... | collective-permute-start | bytes 786440 | tf_op jit(solution)/shard_map/ppermute | solution.py:61
  21.3 8.8 %collective-permute-start.4 = (f32[512,128]{1,0:T(8,128)S(1)}, f32[512,128]{1,0:T(8,128)S(1)}, u32[]{:S(2)}, u32[]{:S(2)}) collective-permute-start(f32[512,128]{1,0:T(8,128)S(1)} %collective-permute-done.3), channel_id=1, source_target_pairs={{0,2},{2,0},{4,6},{6,4},{8,10},{10,8},{12,14},{14,12},{1,3},{3,1},... | collective-permute-start | bytes 786440 | tf_op jit(solution)/shard_map/ppermute | solution.py:64
  22.9 12.1 %collective-permute-start.9 = (f32[1024,128]{1,0:T(8,128)S(1)}, f32[1024,128]{1,0:T(8,128)S(1)}, u32[]{:S(2)}, u32[]{:S(2)}) collective-permute-start(f32[1024,128]{1,0:T(8,128)S(1)} %collective-permute-done.1), channel_id=1, source_target_pairs={{0,16},{16,0},{1,17},{17,1},{2,18},{18,2},{3,19},{19,3},{4,20},{20... | collective-permute-start | bytes 1572872 | tf_op jit(solution)/shard_map/ppermute | solution.py:67
  24.5 8.9 %collective-permute-start.2 = (f32[512,128]{1,0:T(8,128)S(1)}, f32[512,128]{1,0:T(8,128)S(1)}, u32[]{:S(2)}, u32[]{:S(2)}) collective-permute-start(f32[512,128]{1,0:T(8,128)S(1)} %get-tuple-element.20), channel_id=1, source_target_pairs={{0,2},{2,0},{4,6},{6,4},{8,10},{10,8},{12,14},{14,12},{1,3},{3,1},... | collective-permute-start | bytes 786440 | tf_op jit(solution)/shard_map/ppermute | solution.py:64
  25.1 9.9 %copy-start = (f32[1024,128]{1,0:T(8,128)S(1)}, f32[1024,128]{1,0:T(8,128)}, u32[]{:S(2)}) copy-start(f32[1024,128]{1,0:T(8,128)} %param.4) | copy-start | bytes 1572868
  25.1 10.1 %collective-permute-start.6 = (f32[512,128]{1,0:T(8,128)S(1)}, f32[512,128]{1,0:T(8,128)S(1)}, u32[]{:S(2)}, u32[]{:S(2)}) collective-permute-start(f32[512,128]{1,0:T(8,128)S(1)} %bitcast.132), channel_id=1, source_target_pairs={{0,1},{1,0},{2,3},{3,2},{4,5},{5,4},{6,7},{7,6},{8,9},{9,8},{10,11... | collective-permute-start | bytes 786440 | tf_op jit(solution)/shard_map/ppermute | solution.py:70
  28.7 6.6 %collective-permute-start.8 = (f32[512,128]{1,0:T(8,128)S(1)}, f32[512,128]{1,0:T(8,128)S(1)}, u32[]{:S(2)}, u32[]{:S(2)}) collective-permute-start(f32[512,128]{1,0:T(8,128)S(1)} %bitcast.131), channel_id=1, source_target_pairs={{0,1},{1,0},{2,3},{3,2},{4,5},{5,4},{6,7},{7,6},{8,9},{9,8},{10,11... | collective-permute-start | bytes 786440 | tf_op jit(solution)/shard_map/ppermute | solution.py:70
  33.4 6.4 %collective-permute-start.12 = (f32[512,128]{1,0:T(8,128)S(1)}, f32[512,128]{1,0:T(8,128)S(1)}, u32[]{:S(2)}, u32[]{:S(2)}) collective-permute-start(f32[512,128]{1,0:T(8,128)S(1)} %collective-permute-done.11), channel_id=1, source_target_pairs={{0,2},{2,0},{4,6},{6,4},{8,10},{10,8},{12,14},{14,12},{1,3},{3,1},... | collective-permute-start | bytes 786440 | tf_op jit(solution)/shard_map/ppermute | solution.py:64
  35.1 1.6 %collective-permute-start.10 = (f32[512,128]{1,0:T(8,128)S(1)}, f32[512,128]{1,0:T(8,128)S(1)}, u32[]{:S(2)}, u32[]{:S(2)}) collective-permute-start(f32[512,128]{1,0:T(8,128)S(1)} %bitcast.139), channel_id=1, source_target_pairs={{0,1},{1,0},{2,3},{3,2},{4,5},{5,4},{6,7},{7,6},{8,9},{9,8},{10,11... | collective-permute-start | bytes 786440 | tf_op jit(solution)/shard_map/ppermute | solution.py:70
  35.3 1.8 %collective-permute-start.5 = (f32[512,128]{1,0:T(8,128)S(1)}, f32[512,128]{1,0:T(8,128)S(1)}, u32[]{:S(2)}, u32[]{:S(2)}) collective-permute-start(f32[512,128]{1,0:T(8,128)S(1)} %bitcast.138), channel_id=1, source_target_pairs={{0,1},{1,0},{2,3},{3,2},{4,5},{5,4},{6,7},{7,6},{8,9},{9,8},{10,11... | collective-permute-start | bytes 786440 | tf_op jit(solution)/shard_map/ppermute | solution.py:70
  39.8 0.9 %copy-start.1 = (s32[4]{0:T(128)S(1)}, s32[4]{0:T(128)}, u32[]{:S(2)}) copy-start(s32[4]{0:T(128)} %param.7) | copy-start | bytes 52
  40.3 4.7 %collective-permute-start.13 = (f32[512,256]{1,0:T(8,128)S(1)}, f32[512,256]{1,0:T(8,128)S(1)}, u32[]{:S(2)}, u32[]{:S(2)}) collective-permute-start(f32[512,256]{1,0:T(8,128)S(1)} %convolution_add_fusion), channel_id=1, source_target_pairs={{0,1},{1,0},{2,3},{3,2},{4,5},{5,4},{6,7},{7,6},{8,9},{9,8},{10,11... | collective-permute-start | bytes 1572872 | tf_op jit(solution)/shard_map/ppermute | solution.py:70
  44.9 6.6 %copy-start.2 = (s32[4]{0:T(128)S(1)}, s32[4]{0:T(128)}, u32[]{:S(2)}) copy-start(s32[4]{0:T(128)} %param.6) | copy-start | bytes 52
  45.5 4.5 %collective-permute-start.15 = (f32[1,128]{1,0:T(1,128)S(1)}, f32[1,128]{1,0:T(1,128)S(1)}, u32[]{:S(2)}, u32[]{:S(2)}) collective-permute-start(f32[1,128]{1,0:T(1,128)S(1)} %bitcast.142), channel_id=1, source_target_pairs={{0,4},{2,6},{4,0},{6,2},{8,12},{10,14},{12,8},{14,10},{1,5},{3,7},... | collective-permute-start | bytes 1544 | tf_op jit(solution)/shard_map/ppermute | solution.py:61
  48.5 8.1 %collective-permute-start.14 = (f32[512,128]{1,0:T(8,128)S(1)}, f32[512,128]{1,0:T(8,128)S(1)}, u32[]{:S(2)}, u32[]{:S(2)}) collective-permute-start(f32[512,128]{1,0:T(8,128)S(1)} %get-tuple-element.18), channel_id=1, source_target_pairs={{0,4},{2,6},{4,0},{6,2},{8,12},{10,14},{12,8},{14,10},{1,5},{3,7},... | collective-permute-start | bytes 786440 | tf_op jit(solution)/shard_map/ppermute | solution.py:61
  50.0 3.5 %collective-permute-start.16 = (f32[1,128]{1,0:T(1,128)S(1)}, f32[1,128]{1,0:T(1,128)S(1)}, u32[]{:S(2)}, u32[]{:S(2)}) collective-permute-start(f32[1,128]{1,0:T(1,128)S(1)} %bitcast_add_fusion), channel_id=1, source_target_pairs={{0,16},{16,0},{1,17},{17,1},{2,18},{18,2},{3,19},{19,3},{4,20},{20... | collective-permute-start | bytes 1544 | tf_op jit(solution)/shard_map/ppermute | solution.py:67

commit v4 on v3

--- a/solution.py
+++ b/solution.py
@@ -80,6 +80,14 @@
         ]
         return jnp.stack([keep, across(give)])
 
+    def lookup(table, index):
+        picked = jnp.arange(table.shape[0])[:, None] == index
+        spread = jnp.broadcast_to(table.astype(jnp.float32)[:, None], (table.shape[0], width))
+        return jnp.sum(jnp.where(picked, spread, 0.0), axis=0, keepdims=True)
+
+    def in_order(mine, other):
+        return jnp.where(p == 0, jnp.stack([mine, other]), jnp.stack([other, mine])).reshape(rows, width)
+
     own = lax.dynamic_slice_in_dim(flow, p * half, half, 0)
     rest = lax.dynamic_slice_in_dim(flow, (1 - p) * half, half, 0)
     side_raw = along_z(flow, 1)
@@ -88,44 +96,50 @@
     own_y = along_y(own)
     three = along_z(after(rest, own_y), 3)
     two_y = along_y(two)
+    exponent, exponent_z, level = lookup(power, z), lookup(power, z ^ 1), lookup(prune_level, z) / 8.0
     far_side = along_x(after(side_raw, far))
     one = lax.dynamic_slice_in_dim(side_raw, p * half, half, 0)
     one_y = along_y(one)
-    three_y = along_y(after(three, two_y, one_y))
+    three_y = along_y(after(three, two_y, one_y, exponent, exponent_z, level))
     near = both_layers(after(flow, own_y))
     near_x = both_layers(far)
     side = both_layers(side_raw)
     side_x = both_layers(far_side)
 
-    here = jnp.stack([near, side], axis=1)
-    there = jnp.stack([near_x, side_x], axis=1)
+    here = jnp.stack([side, near], axis=1)
+    there = jnp.stack([side_x, near_x], axis=1)
     right = jnp.where(x == 0, jnp.stack([here, there], 2), jnp.stack([there, here], 2))
     right = right.reshape(2, 2, 4, 2, width, width)
-    stored = pattern[2 * x + p][None, :] * jnp.stack([pattern[:, z], pattern[:, z ^ 1]])
+    stored = pattern[2 * x + p][None, :] * jnp.stack([pattern[:, z ^ 1], pattern[:, z]])
     right = right * stored.astype(jnp.float32)[None, :, :, None, None, None]
-    kept, sent = [], []
+    blocks = []
     for i in range(4):
         chosen = lax.dynamic_index_in_dim(right, z ^ i, 2, False)
         first = lax.dynamic_index_in_dim(chosen, y, 2, False)
         second = lax.dynamic_index_in_dim(chosen, 1 - y, 2, False)
         both = jnp.concatenate([first, second], axis=2)
-        kept.append(jnp.concatenate([both[0, 0], both[0, 1]], axis=1))
-        sent.append(jnp.concatenate([both[1, 0], both[1, 1]], axis=1))
+        blocks.append([both[1, 0], both[0, 0], both[1, 1], both[0, 1]])
 
+    own = after(own, own_y)
     left = jnp.concatenate([own, own_y, one, one_y, two, two_y], axis=1)
-    early_sent = multiply(left, jnp.concatenate(sent[:3]))
-    early_kept = multiply(left, jnp.concatenate(kept[:3]))
-    last = jnp.concatenate([three, after(three_y, early_sent, early_kept)], axis=1)
-    outgoing = early_sent + multiply(last, sent[3])
-    product = early_kept + multiply(last, kept[3]) + across(outgoing)
-    mine = raise_to(product[:, :width], power[z])
-    other = raise_to(product[:, width:], power[z ^ 1])
+    wide = jnp.concatenate([jnp.concatenate(row, axis=1) for row in blocks[:3]])
+    early = multiply(left, wide)
+    last = jnp.concatenate([three, after(three_y, early)], axis=1)
+
+    def finish(i):
+        return early[:, i * width : (i + 1) * width] + multiply(last, blocks[3][i])
+
+    from_core = across(finish(0))
+    from_core_own = across(finish(2))
+    other = raise_to(finish(1) + from_core, exponent_z)
+    other_sum = jnp.sum(other, axis=0, keepdims=True)
     arrived = along_z(other, 1)
-    row_sum = jnp.sum(mine, axis=0, keepdims=True) + along_z(jnp.sum(other, axis=0, keepdims=True), 1)
-    totals = row_sum + along_x(row_sum)
-    whole = jnp.where(p == 0, jnp.stack([mine, arrived]), jnp.stack([arrived, mine])).reshape(rows, width)
-    level = prune_level[z].astype(jnp.float32) / 8.0
-    return jnp.maximum(order * whole / totals - level, 0.0)
+    mine = raise_to(finish(3) + from_core_own, exponent)
+    sums = jnp.sum(mine, axis=0, keepdims=True)
+    sums_x = along_x(sums)
+    sums_xz = lax.ppermute(other_sum, ("row", "col"), [(i, i ^ 10) for i in range(16)])
+    totals = sums + sums_x + sums_xz + jnp.sum(arrived, axis=0, keepdims=True)
+    return jnp.maximum(order * in_order(mine, arrived) / totals - level, 0.0)
 
 
 def solution(mesh):

time: 58.5 us -> 54.8 us (0.937); the launches traced: 57.5 us -> 54.6 us
  between operations: 4.62 us -> 0.35 us
  starting transfers between devices: 19.7 us -> 22.7 us
  local copies, waits for them, and re-layouts: 5.18 us -> 3.26 us
  waiting for transfers between devices: 23.6 us -> 21.8 us
  other arithmetic: 2 us -> 3.53 us
  matrix products: 2.42 us -> 3.02 us
    ppermute x4, waiting for transfers between devices: 8.95 us -> 5 us  [along_y(): return lax.ppermute(value, 'col', [(i, i ^ 1) for i in range(8)])]
    ppermute x5 -> x4, starting transfers between devices: 8.91 us -> 11.5 us  [along_z(): return lax.ppermute(value, 'col', [(i, i ^ 2 * distance) for i in range(8)])]
    unnamed x12 -> x8, local copies, waits for them, and re-layouts: 1.91 us -> 0.14 us
    ppermute x5 -> x4, waiting for transfers between devices: 12.8 us -> 14.3 us  [along_z(): return lax.ppermute(value, 'col', [(i, i ^ 2 * distance) for i in range(8)])]
    convert_element_type x0 -> x2, other arithmetic: none -> 1.32 us  [lookup(): table.astype(jnp.float32)[:, None]]
    ppermute x3, waiting for transfers between devices: 0.8 us -> 0.01 us  [along_x(): return lax.ppermute(value, 'row', [(0, 1), (1, 0)])]
    ppermute x0 -> x1, waiting for transfers between devices: none -> 0.78 us  [squared(): lax.ppermute(other_sum, ('row', 'col'), [(i, i ^ 10) for i in range(16)])]
    ppermute x5 -> x6, waiting for transfers between devices: 1.09 us -> 1.71 us  [across(): return lax.ppermute(value, 'layer', [(0, 1), (1, 0)])]
  transfers between devices with their start and end apart: 17 -> 18, of which waited for: 10 -> 12; matrix products, arithmetic and copies ran while one was open for 13% -> 15% of each run, Pallas kernels for 0% -> 0%
where the time goes in v4:
time: 54.8 us; the launch traced here: 54.6 us
  starting transfers between devices  22.7 us (41%)
  waiting for transfers between devices  21.8 us (40%)
  other arithmetic  3.53 us (6%)
  local copies, waits for them, and re-layouts  3.26 us (6%)
  matrix products  3.02 us (6%)
    ppermute x4, waiting for transfers between devices, along_z(): return lax.ppermute(value, 'col', [(i, i ^ 2 * distance) for i in range(8)])  14.3 us
    ppermute x4, starting transfers between devices, along_z(): return lax.ppermute(value, 'col', [(i, i ^ 2 * distance) for i in range(8)])  11.5 us
    ppermute x4, starting transfers between devices, along_y(): return lax.ppermute(value, 'col', [(i, i ^ 1) for i in range(8)])  5.19 us
    ppermute x4, waiting for transfers between devices, along_y(): return lax.ppermute(value, 'col', [(i, i ^ 1) for i in range(8)])  5 us
    ppermute x3, starting transfers between devices, along_x(): return lax.ppermute(value, 'row', [(0, 1), (1, 0)])  4.69 us
    dot_general x5, matrix products, multiply(): jnp.dot(left, right, precision=lax.Precision.HIGH, preferred_element_type...  3.02 us
    ppermute x6, waiting for transfers between devices, across(): return lax.ppermute(value, 'layer', [(0, 1), (1, 0)])  1.71 us
    convert_element_type x2, other arithmetic, lookup(): table.astype(jnp.float32)[:, None]  1.32 us
  transfers between devices with their start and end apart: 18, of which 12 were waited for; matrix products, arithmetic and copies ran while one was open for 15% of the time, Pallas kernels for 0%

profile of v4, /device:TPU:0, one launch (start us, length us, event | category | flops | bytes accessed | tf_op | source)
XLA Modules:
  0.0 54.6 jit_solution(6658637705490009447)
XLA Ops:
  0.0 3.0 %collective-permute-start.1 = (f32[1024,128]{1,0:T(8,128)}, f32[1024,128]{1,0:T(8,128)S(1)}, u32[]{:S(2)}, u32[]{:S(2)}) collective-permute-start(f32[1024,128]{1,0:T(8,128)} %param.4), channel_id=1, source_target_pairs={{0,4},{2,6},{4,0},{6,2},{8,12},{10,14},{12,8},{14,10},{1,5},{3,7},... | collective-permute-start | bytes 1572872 | tf_op jit(solution)/shard_map/ppermute | solution.py:61
  3.0 1.5 %collective-permute-start.7 = (f32[1024,128]{1,0:T(8,128)}, f32[1024,128]{1,0:T(8,128)S(1)}, u32[]{:S(2)}, u32[]{:S(2)}) collective-permute-start(f32[1024,128]{1,0:T(8,128)} %param.4), channel_id=1, source_target_pairs={{0,16},{16,0},{1,17},{17,1},{2,18},{18,2},{3,19},{19,3},{4,20},{20... | collective-permute-start | bytes 1572872 | tf_op jit(solution)/shard_map/ppermute | solution.py:67
  4.5 1.1 %constant_dynamic-slice_fusion = (f32[512,128]{1,0:T(8,128)S(1)}, f32[512,128]{1,0:T(8,128)S(1)}) fusion(f32[1024,128]{1,0:T(8,128)} %param.4, s32[]{:T(128)S(6)} %select_n.151, s32[]{:T(128)S(6)} %select_n.133), kind=kLoop, calls=%fused_computation.128 | loop fusion | bytes 1048584 | tf_op jit(solution)/shard_map/dynamic_slice | solution.py:92
  5.6 1.6 %collective-permute-start = (f32[512,128]{1,0:T(8,128)S(1)}, f32[512,128]{1,0:T(8,128)S(1)}, u32[]{:S(2)}, u32[]{:S(2)}) collective-permute-start(f32[512,128]{1,0:T(8,128)S(1)} %get-tuple-element.11), channel_id=1, source_target_pairs={{0,2},{2,0},{4,6},{6,4},{8,10},{10,8},{12,14},{14,12},{1,3},{3,1},... | collective-permute-start | bytes 786440 | tf_op jit(solution)/shard_map/ppermute | solution.py:64
  7.2 2.6 %collective-permute-start.3 = (f32[512,128]{1,0:T(8,128)S(1)}, f32[512,128]{1,0:T(8,128)S(1)}, u32[]{:S(2)}, u32[]{:S(2)}) collective-permute-start(f32[512,128]{1,0:T(8,128)S(1)} %get-tuple-element.11), channel_id=1, source_target_pairs={{0,8},{2,10},{4,12},{6,14},{8,0},{10,2},{12,4},{14,6},{1,9},{3,11}... | collective-permute-start | bytes 786440 | tf_op jit(solution)/shard_map/ppermute | solution.py:61
  9.8 0.7 %convert_element_type.14 = f32[4]{0:T(128)S(1)} convert(s32[4]{0:T(128)} %param.7) | non-fusion elementwise | flops 4 | bytes 32 | tf_op jit(solution)/shard_map/convert_element_type | solution.py:85
  10.4 0.7 %convert_element_type.16 = f32[4]{0:T(128)S(1)} convert(s32[4]{0:T(128)} %param.6) | non-fusion elementwise | flops 4 | bytes 32 | tf_op jit(solution)/shard_map/convert_element_type | solution.py:85
  11.1 0.7 %fusion.75 = s32[4]{0:T(128)S(1)} fusion(s32[4,4]{1,0:T(4,128)} %param.5, s32[]{:T(128)S(6)} %select_n.139), kind=kLoop, calls=%fused_computation.149 | loop fusion | bytes 36 | tf_op jit(solution)/shard_map/mul | solution.py:113
  11.8 1.0 %fusion.72 = (s32[4]{0:T(128)S(1)}, s32[4]{0:T(128)S(1)}) fusion(s32[4,4]{1,0:T(4,128)} %param.5, s32[]{:T(128)S(6)} %select_n.140, s32[]{:T(128)S(6)} %select_n.141), kind=kLoop, calls=%fused_computation.142 | loop fusion | bytes 72 | tf_op jit(solution)/shard_map/dynamic_slice | solution.py:113
  12.8 0.1 select_reduce_fusion
  12.9 0.2 collective-permute-done
  13.1 2.5 %collective-permute-start.11 = (f32[512,128]{1,0:T(8,128)S(1)}, f32[512,128]{1,0:T(8,128)S(1)}, u32[]{:S(2)}, u32[]{:S(2)}) collective-permute-start(f32[512,128]{1,0:T(8,128)S(1)} %get-tuple-element.14), channel_id=1, source_target_pairs={{0,12},{2,14},{4,8},{6,10},{8,4},{10,6},{12,0},{14,2},{1,13},{3,15... | collective-permute-start | bytes 786440 | tf_op jit(solution)/shard_map/ppermute | solution.py:61
  15.6 5.6 %collective-permute-done.3 = f32[512,128]{1,0:T(8,128)S(1)} collective-permute-done((f32[512,128]{1,0:T(8,128)S(1)}, f32[512,128]{1,0:T(8,128)S(1)}, u32[]{:S(2)}, u32[]{:S(2)}) %collective-permute-start.3) | collective-permute-done | bytes 262176 | tf_op jit(solution)/shard_map/ppermute | solution.py:61
  21.2 1.5 %collective-permute-start.4 = (f32[512,128]{1,0:T(8,128)S(1)}, f32[512,128]{1,0:T(8,128)S(1)}, u32[]{:S(2)}, u32[]{:S(2)}) collective-permute-start(f32[512,128]{1,0:T(8,128)S(1)} %collective-permute-done.3), channel_id=1, source_target_pairs={{0,2},{2,0},{4,6},{6,4},{8,10},{10,8},{12,14},{14,12},{1,3},{3,1},... | collective-permute-start | bytes 786440 | tf_op jit(solution)/shard_map/ppermute | solution.py:64
  22.8 1.6 %collective-permute-start.8 = (f32[1024,128]{1,0:T(8,128)S(1)}, f32[1024,128]{1,0:T(8,128)S(1)}, u32[]{:S(2)}, u32[]{:S(2)}) collective-permute-start(f32[1024,128]{1,0:T(8,128)S(1)} %collective-permute-done.1), channel_id=1, source_target_pairs={{0,16},{16,0},{1,17},{17,1},{2,18},{18,2},{3,19},{19,3},{4,20},{20... | collective-permute-start | bytes 1572872 | tf_op jit(solution)/shard_map/ppermute | solution.py:67
  24.4 0.6 %collective-permute-start.2 = (f32[512,128]{1,0:T(8,128)S(1)}, f32[512,128]{1,0:T(8,128)S(1)}, u32[]{:S(2)}, u32[]{:S(2)}) collective-permute-start(f32[512,128]{1,0:T(8,128)S(1)} %get-tuple-element.27), channel_id=1, source_target_pairs={{0,2},{2,0},{4,6},{6,4},{8,10},{10,8},{12,14},{14,12},{1,3},{3,1},... | collective-permute-start | bytes 786440 | tf_op jit(solution)/shard_map/ppermute | solution.py:64
  25.0 0.1 collective-permute-start.5
  25.2 3.5 %collective-permute-done.11 = f32[512,128]{1,0:T(8,128)S(1)} collective-permute-done((f32[512,128]{1,0:T(8,128)S(1)}, f32[512,128]{1,0:T(8,128)S(1)}, u32[]{:S(2)}, u32[]{:S(2)}) %collective-permute-start.11) | collective-permute-done | bytes 262176 | tf_op jit(solution)/shard_map/ppermute | solution.py:61
  28.7 1.4 %collective-permute-done.4 = f32[512,128]{1,0:T(8,128)S(1)} collective-permute-done((f32[512,128]{1,0:T(8,128)S(1)}, f32[512,128]{1,0:T(8,128)S(1)}, u32[]{:S(2)}, u32[]{:S(2)}) %collective-permute-start.4) | collective-permute-done | bytes 262176 | tf_op jit(solution)/shard_map/ppermute | solution.py:64
  30.1 3.3 %collective-permute-done.2 = f32[512,128]{1,0:T(8,128)S(1)} collective-permute-done((f32[512,128]{1,0:T(8,128)S(1)}, f32[512,128]{1,0:T(8,128)S(1)}, u32[]{:S(2)}, u32[]{:S(2)}) %collective-permute-start.2) | collective-permute-done | bytes 262176 | tf_op jit(solution)/shard_map/ppermute | solution.py:64
  33.3 1.5 %collective-permute-start.12 = (f32[512,128]{1,0:T(8,128)S(1)}, f32[512,128]{1,0:T(8,128)S(1)}, u32[]{:S(2)}, u32[]{:S(2)}) collective-permute-start(f32[512,128]{1,0:T(8,128)S(1)} %collective-permute-done.11), channel_id=1, source_target_pairs={{0,2},{2,0},{4,6},{6,4},{8,10},{10,8},{12,14},{14,12},{1,3},{3,1},... | collective-permute-start | bytes 786440 | tf_op jit(solution)/shard_map/ppermute | solution.py:64
  34.9 0.1 constant_dynamic-slice_fusion.7
  35.0 0.1 collective-permute-start.6
  35.2 0.6 %collective-permute-start.9 = (f32[512,128]{1,0:T(8,128)S(1)}, f32[512,128]{1,0:T(8,128)S(1)}, u32[]{:S(2)}, u32[]{:S(2)}) collective-permute-start(f32[512,128]{1,0:T(8,128)S(1)} %bitcast.144), channel_id=1, source_target_pairs={{0,1},{1,0},{2,3},{3,2},{4,5},{5,4},{6,7},{7,6},{8,9},{9,8},{10,11... | collective-permute-start | bytes 786440 | tf_op jit(solution)/shard_map/ppermute | solution.py:70
  35.8 0.8 %collective-permute-done.6 = f32[512,128]{1,0:T(8,128)S(1)} collective-permute-done((f32[512,128]{1,0:T(8,128)S(1)}, f32[512,128]{1,0:T(8,128)S(1)}, u32[]{:S(2)}, u32[]{:S(2)}) %collective-permute-start.6) | collective-permute-done | bytes 262176 | tf_op jit(solution)/shard_map/ppermute | solution.py:70
  36.7 0.1 maximum_bitcast_fusion
  36.7 0.2 collective-permute-done.9
  37.0 0.1 maximum_bitcast_fusion.1
  37.1 0.1 maximum_select_fusion
  37.2 0.4 broadcast_multiply_fusion
  37.6 0.2 dynamic-slice_bitcast_fusion.1
  38.0 1.5 %fusion = f32[512,512]{1,0:T(8,128)S(1)} fusion(f32[512,768]{1,0:T(8,128)S(1)} %constant_dynamic-update-slice_fusion, f32[256,128]{1,0:T(8,128)S(1)} %get-tuple-element.50, f32[256,128]{1,0:T(8,128)S(1)} %get-tuple-element.51, f32[256,128]{1,0:T(8,128)S(1)} %get-tuple-element.49, f32[256,128]{1,0:T(8,128)S(1)} %get-tuple-element.48, ...), kind=kOutput, calls=%fused_computation.1 | convolution fusion | flops 1212284928 | bytes 4194304 | tf_op jit(solution)/shard_map/dot_general | solution.py:8
  39.5 0.2 collective-permute-done.12
  39.7 0.4 slice_add_fusion
  40.1 0.4 slice_add_fusion.2
  40.5 0.2 collective-permute-start.14
  40.7 0.4 collective-permute-start.13
  41.1 0.4 fusion.33
  41.4 0.4 fusion.37
  41.8 0.3 collective-permute-done.14
  42.1 0.4 collective-permute-done.13
  42.5 0.2 fusion.82
  42.6 3.5 %collective-permute-start.15 = (f32[512,128]{1,0:T(8,128)S(1)}, f32[512,128]{1,0:T(8,128)S(1)}, u32[]{:S(2)}, u32[]{:S(2)}) collective-permute-start(f32[512,128]{1,0:T(8,128)S(1)} %get-tuple-element.37), channel_id=1, source_target_pairs={{0,4},{2,6},{4,0},{6,2},{8,12},{10,14},{12,8},{14,10},{1,5},{3,7},... | collective-permute-start | bytes 786440 | tf_op jit(solution)/shard_map/ppermute | solution.py:61
  46.1 1.6 %collective-permute-start.16 = (f32[1,128]{1,0:T(1,128)S(1)}, f32[1,128]{1,0:T(1,128)S(1)}, u32[]{:S(2)}, u32[]{:S(2)}) collective-permute-start(f32[1,128]{1,0:T(1,128)S(1)} %bitcast.148), channel_id=1, source_target_pairs={{0,16},{16,0},{1,17},{17,1},{2,18},{18,2},{3,19},{19,3},{4,20},{20... | collective-permute-start | bytes 1544 | tf_op jit(solution)/shard_map/ppermute | solution.py:67
  47.7 5.1 %collective-permute-done.15 = f32[512,128]{1,0:T(8,128)S(1)} collective-permute-done((f32[512,128]{1,0:T(8,128)S(1)}, f32[512,128]{1,0:T(8,128)S(1)}, u32[]{:S(2)}, u32[]{:S(2)}) %collective-permute-start.15) | collective-permute-done | bytes 262176 | tf_op jit(solution)/shard_map/ppermute | solution.py:61
  52.9 0.1 reduce_sum.58
  53.0 0.8 %collective-permute-done.17 = f32[1,128]{1,0:T(1,128)S(1)} collective-permute-done((f32[1,128]{1,0:T(1,128)S(1)}, f32[1,128]{1,0:T(1,128)S(1)}, u32[]{:S(2)}, u32[]{:S(2)}) %collective-permute-start.17) | collective-permute-done | bytes 544 | tf_op jit(solution)/shard_map/ppermute | solution.py:140
  53.8 0.9 %fusion.26 = f32[1024,128]{1,0:T(8,128)} fusion(f32[2,512,128]{2,1,0:T(8,128)S(1)} %fusion.24, f32[128]{0:T(128)S(1)} %broadcast_multiply_fusion.1, f32[128]{0:T(128)S(1)} %fusion.76), kind=kLoop, calls=%fused_computation.60 | loop fusion | flops 393216 | bytes 1049600 | tf_op jit(solution)/shard_map/max | solution.py:142
  (34 shorter events, 0.6 us)
Async XLA Ops:
  0.0 22.8 %collective-permute-start.1 = (f32[1024,128]{1,0:T(8,128)}, f32[1024,128]{1,0:T(8,128)S(1)}, u32[]{:S(2)}, u32[]{:S(2)}) collective-permute-start(f32[1024,128]{1,0:T(8,128)} %param.4), channel_id=1, source_target_pairs={{0,4},{2,6},{4,0},{6,2},{8,12},{10,14},{12,8},{14,10},{1,5},{3,7},... | collective-permute-start | bytes 1572872 | tf_op jit(solution)/shard_map/ppermute | solution.py:61
  3.0 19.8 %collective-permute-start.7 = (f32[1024,128]{1,0:T(8,128)}, f32[1024,128]{1,0:T(8,128)S(1)}, u32[]{:S(2)}, u32[]{:S(2)}) collective-permute-start(f32[1024,128]{1,0:T(8,128)} %param.4), channel_id=1, source_target_pairs={{0,16},{16,0},{1,17},{17,1},{2,18},{18,2},{3,19},{19,3},{4,20},{20... | collective-permute-start | bytes 1572872 | tf_op jit(solution)/shard_map/ppermute | solution.py:67
  5.6 7.6 %collective-permute-start = (f32[512,128]{1,0:T(8,128)S(1)}, f32[512,128]{1,0:T(8,128)S(1)}, u32[]{:S(2)}, u32[]{:S(2)}) collective-permute-start(f32[512,128]{1,0:T(8,128)S(1)} %get-tuple-element.11), channel_id=1, source_target_pairs={{0,2},{2,0},{4,6},{6,4},{8,10},{10,8},{12,14},{14,12},{1,3},{3,1},... | collective-permute-start | bytes 786440 | tf_op jit(solution)/shard_map/ppermute | solution.py:64
  7.2 14.1 %collective-permute-start.3 = (f32[512,128]{1,0:T(8,128)S(1)}, f32[512,128]{1,0:T(8,128)S(1)}, u32[]{:S(2)}, u32[]{:S(2)}) collective-permute-start(f32[512,128]{1,0:T(8,128)S(1)} %get-tuple-element.11), channel_id=1, source_target_pairs={{0,8},{2,10},{4,12},{6,14},{8,0},{10,2},{12,4},{14,6},{1,9},{3,11}... | collective-permute-start | bytes 786440 | tf_op jit(solution)/shard_map/ppermute | solution.py:61
  13.1 15.6 %collective-permute-start.11 = (f32[512,128]{1,0:T(8,128)S(1)}, f32[512,128]{1,0:T(8,128)S(1)}, u32[]{:S(2)}, u32[]{:S(2)}) collective-permute-start(f32[512,128]{1,0:T(8,128)S(1)} %get-tuple-element.14), channel_id=1, source_target_pairs={{0,12},{2,14},{4,8},{6,10},{8,4},{10,6},{12,0},{14,2},{1,13},{3,15... | collective-permute-start | bytes 786440 | tf_op jit(solution)/shard_map/ppermute | solution.py:61
  21.2 8.8 %collective-permute-start.4 = (f32[512,128]{1,0:T(8,128)S(1)}, f32[512,128]{1,0:T(8,128)S(1)}, u32[]{:S(2)}, u32[]{:S(2)}) collective-permute-start(f32[512,128]{1,0:T(8,128)S(1)} %collective-permute-done.3), channel_id=1, source_target_pairs={{0,2},{2,0},{4,6},{6,4},{8,10},{10,8},{12,14},{14,12},{1,3},{3,1},... | collective-permute-start | bytes 786440 | tf_op jit(solution)/shard_map/ppermute | solution.py:64
  22.8 12.1 %collective-permute-start.8 = (f32[1024,128]{1,0:T(8,128)S(1)}, f32[1024,128]{1,0:T(8,128)S(1)}, u32[]{:S(2)}, u32[]{:S(2)}) collective-permute-start(f32[1024,128]{1,0:T(8,128)S(1)} %collective-permute-done.1), channel_id=1, source_target_pairs={{0,16},{16,0},{1,17},{17,1},{2,18},{18,2},{3,19},{19,3},{4,20},{20... | collective-permute-start | bytes 1572872 | tf_op jit(solution)/shard_map/ppermute | solution.py:67
  24.4 8.9 %collective-permute-start.2 = (f32[512,128]{1,0:T(8,128)S(1)}, f32[512,128]{1,0:T(8,128)S(1)}, u32[]{:S(2)}, u32[]{:S(2)}) collective-permute-start(f32[512,128]{1,0:T(8,128)S(1)} %get-tuple-element.27), channel_id=1, source_target_pairs={{0,2},{2,0},{4,6},{6,4},{8,10},{10,8},{12,14},{14,12},{1,3},{3,1},... | collective-permute-start | bytes 786440 | tf_op jit(solution)/shard_map/ppermute | solution.py:64
  25.0 9.9 %copy-start = (f32[1024,128]{1,0:T(8,128)S(1)}, f32[1024,128]{1,0:T(8,128)}, u32[]{:S(2)}) copy-start(f32[1024,128]{1,0:T(8,128)} %param.4) | copy-start | bytes 1572868
  25.0 10.1 %collective-permute-start.5 = (f32[512,128]{1,0:T(8,128)S(1)}, f32[512,128]{1,0:T(8,128)S(1)}, u32[]{:S(2)}, u32[]{:S(2)}) collective-permute-start(f32[512,128]{1,0:T(8,128)S(1)} %bitcast.139), channel_id=1, source_target_pairs={{0,1},{1,0},{2,3},{3,2},{4,5},{5,4},{6,7},{7,6},{8,9},{9,8},{10,11... | collective-permute-start | bytes 786440 | tf_op jit(solution)/shard_map/ppermute | solution.py:70
  28.7 6.5 %collective-permute-start.10 = (f32[512,128]{1,0:T(8,128)S(1)}, f32[512,128]{1,0:T(8,128)S(1)}, u32[]{:S(2)}, u32[]{:S(2)}) collective-permute-start(f32[512,128]{1,0:T(8,128)S(1)} %bitcast.138), channel_id=1, source_target_pairs={{0,1},{1,0},{2,3},{3,2},{4,5},{5,4},{6,7},{7,6},{8,9},{9,8},{10,11... | collective-permute-start | bytes 786440 | tf_op jit(solution)/shard_map/ppermute | solution.py:70
  33.3 6.4 %collective-permute-start.12 = (f32[512,128]{1,0:T(8,128)S(1)}, f32[512,128]{1,0:T(8,128)S(1)}, u32[]{:S(2)}, u32[]{:S(2)}) collective-permute-start(f32[512,128]{1,0:T(8,128)S(1)} %collective-permute-done.11), channel_id=1, source_target_pairs={{0,2},{2,0},{4,6},{6,4},{8,10},{10,8},{12,14},{14,12},{1,3},{3,1},... | collective-permute-start | bytes 786440 | tf_op jit(solution)/shard_map/ppermute | solution.py:64
  35.0 1.6 %collective-permute-start.6 = (f32[512,128]{1,0:T(8,128)S(1)}, f32[512,128]{1,0:T(8,128)S(1)}, u32[]{:S(2)}, u32[]{:S(2)}) collective-permute-start(f32[512,128]{1,0:T(8,128)S(1)} %bitcast.145), channel_id=1, source_target_pairs={{0,1},{1,0},{2,3},{3,2},{4,5},{5,4},{6,7},{7,6},{8,9},{9,8},{10,11... | collective-permute-start | bytes 786440 | tf_op jit(solution)/shard_map/ppermute | solution.py:70
  35.2 1.8 %collective-permute-start.9 = (f32[512,128]{1,0:T(8,128)S(1)}, f32[512,128]{1,0:T(8,128)S(1)}, u32[]{:S(2)}, u32[]{:S(2)}) collective-permute-start(f32[512,128]{1,0:T(8,128)S(1)} %bitcast.144), channel_id=1, source_target_pairs={{0,1},{1,0},{2,3},{3,2},{4,5},{5,4},{6,7},{7,6},{8,9},{9,8},{10,11... | collective-permute-start | bytes 786440 | tf_op jit(solution)/shard_map/ppermute | solution.py:70
  40.5 1.6 %collective-permute-start.14 = (f32[512,128]{1,0:T(8,128)S(1)}, f32[512,128]{1,0:T(8,128)S(1)}, u32[]{:S(2)}, u32[]{:S(2)}) collective-permute-start(f32[512,128]{1,0:T(8,128)S(1)} %slice_add_fusion), channel_id=1, source_target_pairs={{0,1},{1,0},{2,3},{3,2},{4,5},{5,4},{6,7},{7,6},{8,9},{9,8},{10,11... | collective-permute-start | bytes 786440 | tf_op jit(solution)/shard_map/ppermute | solution.py:70
  40.7 1.8 %collective-permute-start.13 = (f32[512,128]{1,0:T(8,128)S(1)}, f32[512,128]{1,0:T(8,128)S(1)}, u32[]{:S(2)}, u32[]{:S(2)}) collective-permute-start(f32[512,128]{1,0:T(8,128)S(1)} %slice_add_fusion.2), channel_id=1, source_target_pairs={{0,1},{1,0},{2,3},{3,2},{4,5},{5,4},{6,7},{7,6},{8,9},{9,8},{10,11... | collective-permute-start | bytes 786440 | tf_op jit(solution)/shard_map/ppermute | solution.py:70
  42.6 10.2 %collective-permute-start.15 = (f32[512,128]{1,0:T(8,128)S(1)}, f32[512,128]{1,0:T(8,128)S(1)}, u32[]{:S(2)}, u32[]{:S(2)}) collective-permute-start(f32[512,128]{1,0:T(8,128)S(1)} %get-tuple-element.37), channel_id=1, source_target_pairs={{0,4},{2,6},{4,0},{6,2},{8,12},{10,14},{12,8},{14,10},{1,5},{3,7},... | collective-permute-start | bytes 786440 | tf_op jit(solution)/shard_map/ppermute | solution.py:61
  46.1 6.9 %collective-permute-start.16 = (f32[1,128]{1,0:T(1,128)S(1)}, f32[1,128]{1,0:T(1,128)S(1)}, u32[]{:S(2)}, u32[]{:S(2)}) collective-permute-start(f32[1,128]{1,0:T(1,128)S(1)} %bitcast.148), channel_id=1, source_target_pairs={{0,16},{16,0},{1,17},{17,1},{2,18},{18,2},{3,19},{19,3},{4,20},{20... | collective-permute-start | bytes 1544 | tf_op jit(solution)/shard_map/ppermute | solution.py:67
  47.7 6.0 %collective-permute-start.17 = (f32[1,128]{1,0:T(1,128)S(1)}, f32[1,128]{1,0:T(1,128)S(1)}, u32[]{:S(2)}, u32[]{:S(2)}) collective-permute-start(f32[1,128]{1,0:T(1,128)S(1)} %bitcast.149), channel_id=1, source_target_pairs={{0,20},{2,22},{4,16},{6,18},{8,28},{10,30},{12,24},{14,26},{16,4},... | collective-permute-start | bytes 1544 | tf_op jit(solution)/shard_map/ppermute | solution.py:140

commit v5 on v4

--- a/solution.py
+++ b/solution.py
@@ -72,12 +72,15 @@
     def after(value, *earlier):
         return lax.optimization_barrier((value, *earlier))[0]
 
-    def both_layers(value):
+    def split(value):
         grouped = value.reshape(value.shape[0] // (2 * width), 2, width, width)
-        keep, give = [
+        return [
             lax.dynamic_index_in_dim(grouped, i, 1, False).reshape(value.shape[0] // 2, width)
             for i in (l, 1 - l)
         ]
+
+    def both_layers(value):
+        keep, give = split(value)
         return jnp.stack([keep, across(give)])
 
     def lookup(table, index):
@@ -97,10 +100,10 @@
     three = along_z(after(rest, own_y), 3)
     two_y = along_y(two)
     exponent, exponent_z, level = lookup(power, z), lookup(power, z ^ 1), lookup(prune_level, z) / 8.0
-    far_side = along_x(after(side_raw, far))
     one = lax.dynamic_slice_in_dim(side_raw, p * half, half, 0)
     one_y = along_y(one)
-    three_y = along_y(after(three, two_y, one_y, exponent, exponent_z, level))
+    far_side = along_x(after(side_raw, far))
+    three_y = along_y(after(three, two_y, exponent, exponent_z, level))
     near = both_layers(after(flow, own_y))
     near_x = both_layers(far)
     side = both_layers(side_raw)
@@ -126,15 +129,14 @@
     early = multiply(left, wide)
     last = jnp.concatenate([three, after(three_y, early)], axis=1)
 
-    def finish(i):
-        return early[:, i * width : (i + 1) * width] + multiply(last, blocks[3][i])
+    def finish(i, block):
+        return early[:, i * width : (i + 1) * width] + multiply(block, blocks[3][i])
 
-    from_core = across(finish(0))
-    from_core_own = across(finish(2))
-    other = raise_to(finish(1) + from_core, exponent_z)
+    other = raise_to(finish(1, last) + across(finish(0, last)), exponent_z)
     other_sum = jnp.sum(other, axis=0, keepdims=True)
     arrived = along_z(other, 1)
-    mine = raise_to(finish(3) + from_core_own, exponent)
+    held = after(last, other)
+    mine = raise_to(finish(3, held) + across(finish(2, held)), exponent)
     sums = jnp.sum(mine, axis=0, keepdims=True)
     sums_x = along_x(sums)
     sums_xz = lax.ppermute(other_sum, ("row", "col"), [(i, i ^ 10) for i in range(16)])

time: 54.8 us -> 54.1 us (0.987)
  starting transfers between devices: 22.7 us -> 21.3 us
  waiting for transfers between devices: 21.8 us -> 22.6 us
    ppermute x4, waiting for transfers between devices: 14.3 us -> 11.5 us  [along_z(): return lax.ppermute(value, 'col', [(i, i ^ 2 * distance) for i in range(8)])]
    ppermute x3, waiting for transfers between devices: 0.01 us -> 2.16 us  [along_x(): return lax.ppermute(value, 'row', [(0, 1), (1, 0)])]
    ppermute x4, starting transfers between devices: 11.5 us -> 10 us  [along_z(): return lax.ppermute(value, 'col', [(i, i ^ 2 * distance) for i in range(8)])]
    ppermute x4, waiting for transfers between devices: 5 us -> 6.22 us  [along_y(): return lax.ppermute(value, 'col', [(i, i ^ 1) for i in range(8)])]
    ppermute x3, starting transfers between devices: 4.69 us -> 3.57 us  [along_x(): return lax.ppermute(value, 'row', [(0, 1), (1, 0)])]
    ppermute x1, starting transfers between devices: 0.01 us -> 1.02 us  [squared(): lax.ppermute(other_sum, ('row', 'col'), [(i, i ^ 10) for i in range(16)])]
  transfers between devices with their start and end apart: 18 -> 18, of which waited for: 12 -> 9; matrix products, arithmetic and copies ran while one was open for 15% -> 15% of each run, Pallas kernels for 0% -> 0%
where the time goes in v5:
time: 54.1 us; the launch traced here: 53.9 us
  waiting for transfers between devices  22.6 us (42%)
  starting transfers between devices  21.3 us (39%)
  other arithmetic  3.44 us (6%)
  local copies, waits for them, and re-layouts  3.27 us (6%)
  matrix products  3.03 us (6%)
    ppermute x4, waiting for transfers between devices, along_z(): return lax.ppermute(value, 'col', [(i, i ^ 2 * distance) for i in range(8)])  11.5 us
    ppermute x4, starting transfers between devices, along_z(): return lax.ppermute(value, 'col', [(i, i ^ 2 * distance) for i in range(8)])  10 us
    ppermute x4, waiting for transfers between devices, along_y(): return lax.ppermute(value, 'col', [(i, i ^ 1) for i in range(8)])  6.22 us
    ppermute x4, starting transfers between devices, along_y(): return lax.ppermute(value, 'col', [(i, i ^ 1) for i in range(8)])  5.2 us
    ppermute x3, starting transfers between devices, along_x(): return lax.ppermute(value, 'row', [(0, 1), (1, 0)])  3.57 us
    dot_general x5, matrix products, multiply(): jnp.dot(left, right, precision=lax.Precision.HIGH, preferred_element_type...  3.03 us
    ppermute x3, waiting for transfers between devices, along_x(): return lax.ppermute(value, 'row', [(0, 1), (1, 0)])  2.16 us
    ppermute x6, waiting for transfers between devices, across(): return lax.ppermute(value, 'layer', [(0, 1), (1, 0)])  1.91 us
  transfers between devices with their start and end apart: 18, of which 9 were waited for; matrix products, arithmetic and copies ran while one was open for 15% of the time, Pallas kernels for 0%

profile of v5, /device:TPU:0, one launch (start us, length us, event | category | flops | bytes accessed | tf_op | source)
XLA Modules:
  0.0 53.9 jit_solution(4355252250208045296)
XLA Ops:
  0.0 3.0 %collective-permute-start.1 = (f32[1024,128]{1,0:T(8,128)}, f32[1024,128]{1,0:T(8,128)S(1)}, u32[]{:S(2)}, u32[]{:S(2)}) collective-permute-start(f32[1024,128]{1,0:T(8,128)} %param.4), channel_id=1, source_target_pairs={{0,4},{2,6},{4,0},{6,2},{8,12},{10,14},{12,8},{14,10},{1,5},{3,7},... | collective-permute-start | bytes 1572872 | tf_op jit(solution)/shard_map/ppermute | solution.py:61
  3.0 1.1 %constant_dynamic-slice_fusion = (f32[512,128]{1,0:T(8,128)S(1)}, f32[512,128]{1,0:T(8,128)S(1)}) fusion(f32[1024,128]{1,0:T(8,128)} %param.4, s32[]{:T(128)S(6)} %select_n.151, s32[]{:T(128)S(6)} %select_n.133), kind=kLoop, calls=%fused_computation.128 | loop fusion | bytes 1048584 | tf_op jit(solution)/shard_map/dynamic_slice | solution.py:95
  4.1 1.6 %collective-permute-start = (f32[512,128]{1,0:T(8,128)S(1)}, f32[512,128]{1,0:T(8,128)S(1)}, u32[]{:S(2)}, u32[]{:S(2)}) collective-permute-start(f32[512,128]{1,0:T(8,128)S(1)} %get-tuple-element.12), channel_id=1, source_target_pairs={{0,2},{2,0},{4,6},{6,4},{8,10},{10,8},{12,14},{14,12},{1,3},{3,1},... | collective-permute-start | bytes 786440 | tf_op jit(solution)/shard_map/ppermute | solution.py:64
  5.7 2.6 %collective-permute-start.3 = (f32[512,128]{1,0:T(8,128)S(1)}, f32[512,128]{1,0:T(8,128)S(1)}, u32[]{:S(2)}, u32[]{:S(2)}) collective-permute-start(f32[512,128]{1,0:T(8,128)S(1)} %get-tuple-element.12), channel_id=1, source_target_pairs={{0,8},{2,10},{4,12},{6,14},{8,0},{10,2},{12,4},{14,6},{1,9},{3,11}... | collective-permute-start | bytes 786440 | tf_op jit(solution)/shard_map/ppermute | solution.py:61
  8.3 1.5 %collective-permute-start.7 = (f32[1024,128]{1,0:T(8,128)}, f32[1024,128]{1,0:T(8,128)S(1)}, u32[]{:S(2)}, u32[]{:S(2)}) collective-permute-start(f32[1024,128]{1,0:T(8,128)} %param.4), channel_id=1, source_target_pairs={{0,16},{16,0},{1,17},{17,1},{2,18},{18,2},{3,19},{19,3},{4,20},{20... | collective-permute-start | bytes 1572872 | tf_op jit(solution)/shard_map/ppermute | solution.py:67
  9.8 0.7 %fusion.77 = s32[4]{0:T(128)S(1)} fusion(s32[4,4]{1,0:T(4,128)} %param.5, s32[]{:T(128)S(6)} %select_n.139), kind=kLoop, calls=%fused_computation.149 | loop fusion | bytes 36 | tf_op jit(solution)/shard_map/mul | solution.py:116
  10.4 1.0 %fusion.74 = (s32[4]{0:T(128)S(1)}, s32[4]{0:T(128)S(1)}) fusion(s32[4,4]{1,0:T(4,128)} %param.5, s32[]{:T(128)S(6)} %select_n.140, s32[]{:T(128)S(6)} %select_n.141), kind=kLoop, calls=%fused_computation.142 | loop fusion | bytes 72 | tf_op jit(solution)/shard_map/dynamic_slice | solution.py:116
  11.5 0.7 %convert_element_type.16 = f32[4]{0:T(128)S(1)} convert(s32[4]{0:T(128)} %param.6) | non-fusion elementwise | flops 4 | bytes 32 | tf_op jit(solution)/shard_map/convert_element_type | solution.py:88
  12.2 0.7 %convert_element_type.14 = f32[4]{0:T(128)S(1)} convert(s32[4]{0:T(128)} %param.7) | non-fusion elementwise | flops 4 | bytes 32 | tf_op jit(solution)/shard_map/convert_element_type | solution.py:88
  12.8 0.1 select_reduce_fusion
  12.9 0.0 collective-permute-done
  12.9 1.5 %collective-permute-start.11 = (f32[512,128]{1,0:T(8,128)S(1)}, f32[512,128]{1,0:T(8,128)S(1)}, u32[]{:S(2)}, u32[]{:S(2)}) collective-permute-start(f32[512,128]{1,0:T(8,128)S(1)} %get-tuple-element.15), channel_id=1, source_target_pairs={{0,12},{2,14},{4,8},{6,10},{8,4},{10,6},{12,0},{14,2},{1,13},{3,15... | collective-permute-start | bytes 786440 | tf_op jit(solution)/shard_map/ppermute | solution.py:61
  14.4 6.8 %collective-permute-done.3 = f32[512,128]{1,0:T(8,128)S(1)} collective-permute-done((f32[512,128]{1,0:T(8,128)S(1)}, f32[512,128]{1,0:T(8,128)S(1)}, u32[]{:S(2)}, u32[]{:S(2)}) %collective-permute-start.3) | collective-permute-done | bytes 262176 | tf_op jit(solution)/shard_map/ppermute | solution.py:61
  21.2 1.5 %collective-permute-start.4 = (f32[512,128]{1,0:T(8,128)S(1)}, f32[512,128]{1,0:T(8,128)S(1)}, u32[]{:S(2)}, u32[]{:S(2)}) collective-permute-start(f32[512,128]{1,0:T(8,128)S(1)} %collective-permute-done.3), channel_id=1, source_target_pairs={{0,2},{2,0},{4,6},{6,4},{8,10},{10,8},{12,14},{14,12},{1,3},{3,1},... | collective-permute-start | bytes 786440 | tf_op jit(solution)/shard_map/ppermute | solution.py:64
  22.9 0.6 %collective-permute-start.2 = (f32[512,128]{1,0:T(8,128)S(1)}, f32[512,128]{1,0:T(8,128)S(1)}, u32[]{:S(2)}, u32[]{:S(2)}) collective-permute-start(f32[512,128]{1,0:T(8,128)S(1)} %get-tuple-element.27), channel_id=1, source_target_pairs={{0,2},{2,0},{4,6},{6,4},{8,10},{10,8},{12,14},{14,12},{1,3},{3,1},... | collective-permute-start | bytes 786440 | tf_op jit(solution)/shard_map/ppermute | solution.py:64
  23.4 1.5 %collective-permute-start.8 = (f32[1024,128]{1,0:T(8,128)S(1)}, f32[1024,128]{1,0:T(8,128)S(1)}, u32[]{:S(2)}, u32[]{:S(2)}) collective-permute-start(f32[1024,128]{1,0:T(8,128)S(1)} %collective-permute-done.1), channel_id=1, source_target_pairs={{0,16},{16,0},{1,17},{17,1},{2,18},{18,2},{3,19},{19,3},{4,20},{20... | collective-permute-start | bytes 1572872 | tf_op jit(solution)/shard_map/ppermute | solution.py:67
  25.0 0.0 copy-start
  25.0 0.1 collective-permute-start.10
  25.1 5.0 %collective-permute-done.4 = f32[512,128]{1,0:T(8,128)S(1)} collective-permute-done((f32[512,128]{1,0:T(8,128)S(1)}, f32[512,128]{1,0:T(8,128)S(1)}, u32[]{:S(2)}, u32[]{:S(2)}) %collective-permute-start.4) | collective-permute-done | bytes 262176 | tf_op jit(solution)/shard_map/ppermute | solution.py:64
  30.1 1.5 %collective-permute-start.12 = (f32[512,128]{1,0:T(8,128)S(1)}, f32[512,128]{1,0:T(8,128)S(1)}, u32[]{:S(2)}, u32[]{:S(2)}) collective-permute-start(f32[512,128]{1,0:T(8,128)S(1)} %collective-permute-done.11), channel_id=1, source_target_pairs={{0,2},{2,0},{4,6},{6,4},{8,10},{10,8},{12,14},{14,12},{1,3},{3,1},... | collective-permute-start | bytes 786440 | tf_op jit(solution)/shard_map/ppermute | solution.py:64
  31.6 1.3 %collective-permute-done.2 = f32[512,128]{1,0:T(8,128)S(1)} collective-permute-done((f32[512,128]{1,0:T(8,128)S(1)}, f32[512,128]{1,0:T(8,128)S(1)}, u32[]{:S(2)}, u32[]{:S(2)}) %collective-permute-start.2) | collective-permute-done | bytes 262176 | tf_op jit(solution)/shard_map/ppermute | solution.py:64
  32.9 2.2 %collective-permute-done.8 = f32[1024,128]{1,0:T(8,128)S(1)} collective-permute-done((f32[1024,128]{1,0:T(8,128)S(1)}, f32[1024,128]{1,0:T(8,128)S(1)}, u32[]{:S(2)}, u32[]{:S(2)}) %collective-permute-start.8) | collective-permute-done | bytes 524320 | tf_op jit(solution)/shard_map/ppermute | solution.py:67
  35.1 0.1 constant_dynamic-slice_fusion.7
  35.2 0.1 collective-permute-start.9
  35.4 0.6 %collective-permute-start.6 = (f32[512,128]{1,0:T(8,128)S(1)}, f32[512,128]{1,0:T(8,128)S(1)}, u32[]{:S(2)}, u32[]{:S(2)}) collective-permute-start(f32[512,128]{1,0:T(8,128)S(1)} %bitcast.148), channel_id=1, source_target_pairs={{0,1},{1,0},{2,3},{3,2},{4,5},{5,4},{6,7},{7,6},{8,9},{9,8},{10,11... | collective-permute-start | bytes 786440 | tf_op jit(solution)/shard_map/ppermute | solution.py:70
  35.9 0.8 %collective-permute-done.9 = f32[512,128]{1,0:T(8,128)S(1)} collective-permute-done((f32[512,128]{1,0:T(8,128)S(1)}, f32[512,128]{1,0:T(8,128)S(1)}, u32[]{:S(2)}, u32[]{:S(2)}) %collective-permute-start.9) | collective-permute-done | bytes 262176 | tf_op jit(solution)/shard_map/ppermute | solution.py:70
  36.8 0.1 maximum_bitcast_fusion.1
  36.9 0.3 collective-permute-done.6
  37.2 0.1 maximum_bitcast_fusion
  37.3 0.1 maximum_select_fusion
  37.4 0.4 broadcast_multiply_fusion
  37.8 0.2 dynamic-slice_bitcast_fusion
  38.2 1.5 %fusion = f32[512,512]{1,0:T(8,128)S(1)} fusion(f32[512,768]{1,0:T(8,128)S(1)} %constant_dynamic-update-slice_fusion, f32[256,128]{1,0:T(8,128)S(1)} %get-tuple-element.48, f32[256,128]{1,0:T(8,128)S(1)} %get-tuple-element.49, f32[256,128]{1,0:T(8,128)S(1)} %get-tuple-element.47, f32[256,128]{1,0:T(8,128)S(1)} %get-tuple-element.46, ...), kind=kOutput, calls=%fused_computation.1 | convolution fusion | flops 1212284928 | bytes 4194304 | tf_op jit(solution)/shard_map/dot_general | solution.py:8
  39.7 0.4 slice_add_fusion.1
  40.1 0.4 collective-permute-start.13
  40.5 0.4 fusion.39
  40.9 0.8 %collective-permute-done.13 = f32[512,128]{1,0:T(8,128)S(1)} collective-permute-done((f32[512,128]{1,0:T(8,128)S(1)}, f32[512,128]{1,0:T(8,128)S(1)}, u32[]{:S(2)}, u32[]{:S(2)}) %collective-permute-start.13) | collective-permute-done | bytes 262176 | tf_op jit(solution)/shard_map/ppermute | solution.py:70
  41.7 0.1 fusion.84
  41.8 0.4 slice_add_fusion
  42.2 0.4 collective-permute-start.14
  42.6 2.9 %collective-permute-start.15 = (f32[512,128]{1,0:T(8,128)S(1)}, f32[512,128]{1,0:T(8,128)S(1)}, u32[]{:S(2)}, u32[]{:S(2)}) collective-permute-start(f32[512,128]{1,0:T(8,128)S(1)} %get-tuple-element.25), channel_id=1, source_target_pairs={{0,4},{2,6},{4,0},{6,2},{8,12},{10,14},{12,8},{14,10},{1,5},{3,7},... | collective-permute-start | bytes 786440 | tf_op jit(solution)/shard_map/ppermute | solution.py:61
  45.5 1.0 %collective-permute-start.17 = (f32[1,128]{1,0:T(1,128)S(1)}, f32[1,128]{1,0:T(1,128)S(1)}, u32[]{:S(2)}, u32[]{:S(2)}) collective-permute-start(f32[1,128]{1,0:T(1,128)S(1)} %bitcast.153), channel_id=1, source_target_pairs={{0,20},{2,22},{4,16},{6,18},{8,28},{10,30},{12,24},{14,26},{16,4},... | collective-permute-start | bytes 1544 | tf_op jit(solution)/shard_map/ppermute | solution.py:142
  46.5 0.4 fusion.86
  46.9 0.6 %collective-permute-start.16 = (f32[1,128]{1,0:T(1,128)S(1)}, f32[1,128]{1,0:T(1,128)S(1)}, u32[]{:S(2)}, u32[]{:S(2)}) collective-permute-start(f32[1,128]{1,0:T(1,128)S(1)} %bitcast.150), channel_id=1, source_target_pairs={{0,16},{16,0},{1,17},{17,1},{2,18},{18,2},{3,19},{19,3},{4,20},{20... | collective-permute-start | bytes 1544 | tf_op jit(solution)/shard_map/ppermute | solution.py:67
  47.5 4.6 %collective-permute-done.15 = f32[512,128]{1,0:T(8,128)S(1)} collective-permute-done((f32[512,128]{1,0:T(8,128)S(1)}, f32[512,128]{1,0:T(8,128)S(1)}, u32[]{:S(2)}, u32[]{:S(2)}) %collective-permute-start.15) | collective-permute-done | bytes 262176 | tf_op jit(solution)/shard_map/ppermute | solution.py:61
  52.2 0.1 reduce_sum.58
  52.3 0.8 %collective-permute-done.17 = f32[1,128]{1,0:T(1,128)S(1)} collective-permute-done((f32[1,128]{1,0:T(1,128)S(1)}, f32[1,128]{1,0:T(1,128)S(1)}, u32[]{:S(2)}, u32[]{:S(2)}) %collective-permute-start.17) | collective-permute-done | bytes 544 | tf_op jit(solution)/shard_map/ppermute | solution.py:142
  53.1 0.9 %fusion.26 = f32[1024,128]{1,0:T(8,128)} fusion(f32[2,512,128]{2,1,0:T(8,128)S(1)} %fusion.24, f32[128]{0:T(128)S(1)} %broadcast_multiply_fusion.1, f32[128]{0:T(128)S(1)} %fusion.78), kind=kLoop, calls=%fused_computation.60 | loop fusion | flops 393216 | bytes 1049600 | tf_op jit(solution)/shard_map/max | solution.py:144
  (34 shorter events, 0.6 us)
Async XLA Ops:
  0.0 22.8 %collective-permute-start.1 = (f32[1024,128]{1,0:T(8,128)}, f32[1024,128]{1,0:T(8,128)S(1)}, u32[]{:S(2)}, u32[]{:S(2)}) collective-permute-start(f32[1024,128]{1,0:T(8,128)} %param.4), channel_id=1, source_target_pairs={{0,4},{2,6},{4,0},{6,2},{8,12},{10,14},{12,8},{14,10},{1,5},{3,7},... | collective-permute-start | bytes 1572872 | tf_op jit(solution)/shard_map/ppermute | solution.py:61
  4.1 8.8 %collective-permute-start = (f32[512,128]{1,0:T(8,128)S(1)}, f32[512,128]{1,0:T(8,128)S(1)}, u32[]{:S(2)}, u32[]{:S(2)}) collective-permute-start(f32[512,128]{1,0:T(8,128)S(1)} %get-tuple-element.12), channel_id=1, source_target_pairs={{0,2},{2,0},{4,6},{6,4},{8,10},{10,8},{12,14},{14,12},{1,3},{3,1},... | collective-permute-start | bytes 786440 | tf_op jit(solution)/shard_map/ppermute | solution.py:64
  5.7 15.6 %collective-permute-start.3 = (f32[512,128]{1,0:T(8,128)S(1)}, f32[512,128]{1,0:T(8,128)S(1)}, u32[]{:S(2)}, u32[]{:S(2)}) collective-permute-start(f32[512,128]{1,0:T(8,128)S(1)} %get-tuple-element.12), channel_id=1, source_target_pairs={{0,8},{2,10},{4,12},{6,14},{8,0},{10,2},{12,4},{14,6},{1,9},{3,11}... | collective-permute-start | bytes 786440 | tf_op jit(solution)/shard_map/ppermute | solution.py:61
  8.3 15.2 %collective-permute-start.7 = (f32[1024,128]{1,0:T(8,128)}, f32[1024,128]{1,0:T(8,128)S(1)}, u32[]{:S(2)}, u32[]{:S(2)}) collective-permute-start(f32[1024,128]{1,0:T(8,128)} %param.4), channel_id=1, source_target_pairs={{0,16},{16,0},{1,17},{17,1},{2,18},{18,2},{3,19},{19,3},{4,20},{20... | collective-permute-start | bytes 1572872 | tf_op jit(solution)/shard_map/ppermute | solution.py:67
  12.9 17.2 %collective-permute-start.11 = (f32[512,128]{1,0:T(8,128)S(1)}, f32[512,128]{1,0:T(8,128)S(1)}, u32[]{:S(2)}, u32[]{:S(2)}) collective-permute-start(f32[512,128]{1,0:T(8,128)S(1)} %get-tuple-element.15), channel_id=1, source_target_pairs={{0,12},{2,14},{4,8},{6,10},{8,4},{10,6},{12,0},{14,2},{1,13},{3,15... | collective-permute-start | bytes 786440 | tf_op jit(solution)/shard_map/ppermute | solution.py:61
  21.2 8.8 %collective-permute-start.4 = (f32[512,128]{1,0:T(8,128)S(1)}, f32[512,128]{1,0:T(8,128)S(1)}, u32[]{:S(2)}, u32[]{:S(2)}) collective-permute-start(f32[512,128]{1,0:T(8,128)S(1)} %collective-permute-done.3), channel_id=1, source_target_pairs={{0,2},{2,0},{4,6},{6,4},{8,10},{10,8},{12,14},{14,12},{1,3},{3,1},... | collective-permute-start | bytes 786440 | tf_op jit(solution)/shard_map/ppermute | solution.py:64
  22.9 10.0 %collective-permute-start.2 = (f32[512,128]{1,0:T(8,128)S(1)}, f32[512,128]{1,0:T(8,128)S(1)}, u32[]{:S(2)}, u32[]{:S(2)}) collective-permute-start(f32[512,128]{1,0:T(8,128)S(1)} %get-tuple-element.27), channel_id=1, source_target_pairs={{0,2},{2,0},{4,6},{6,4},{8,10},{10,8},{12,14},{14,12},{1,3},{3,1},... | collective-permute-start | bytes 786440 | tf_op jit(solution)/shard_map/ppermute | solution.py:64
  23.4 11.6 %collective-permute-start.8 = (f32[1024,128]{1,0:T(8,128)S(1)}, f32[1024,128]{1,0:T(8,128)S(1)}, u32[]{:S(2)}, u32[]{:S(2)}) collective-permute-start(f32[1024,128]{1,0:T(8,128)S(1)} %collective-permute-done.1), channel_id=1, source_target_pairs={{0,16},{16,0},{1,17},{17,1},{2,18},{18,2},{3,19},{19,3},{4,20},{20... | collective-permute-start | bytes 1572872 | tf_op jit(solution)/shard_map/ppermute | solution.py:67
  25.0 10.1 %copy-start = (f32[1024,128]{1,0:T(8,128)S(1)}, f32[1024,128]{1,0:T(8,128)}, u32[]{:S(2)}) copy-start(f32[1024,128]{1,0:T(8,128)} %param.4) | copy-start | bytes 1572868
  25.0 10.3 %collective-permute-start.10 = (f32[512,128]{1,0:T(8,128)S(1)}, f32[512,128]{1,0:T(8,128)S(1)}, u32[]{:S(2)}, u32[]{:S(2)}) collective-permute-start(f32[512,128]{1,0:T(8,128)S(1)} %bitcast.142), channel_id=1, source_target_pairs={{0,1},{1,0},{2,3},{3,2},{4,5},{5,4},{6,7},{7,6},{8,9},{9,8},{10,11... | collective-permute-start | bytes 786440 | tf_op jit(solution)/shard_map/ppermute | solution.py:70
  30.1 5.3 %collective-permute-start.5 = (f32[512,128]{1,0:T(8,128)S(1)}, f32[512,128]{1,0:T(8,128)S(1)}, u32[]{:S(2)}, u32[]{:S(2)}) collective-permute-start(f32[512,128]{1,0:T(8,128)S(1)} %bitcast.143), channel_id=1, source_target_pairs={{0,1},{1,0},{2,3},{3,2},{4,5},{5,4},{6,7},{7,6},{8,9},{9,8},{10,11... | collective-permute-start | bytes 786440 | tf_op jit(solution)/shard_map/ppermute | solution.py:70
  30.1 9.6 %collective-permute-start.12 = (f32[512,128]{1,0:T(8,128)S(1)}, f32[512,128]{1,0:T(8,128)S(1)}, u32[]{:S(2)}, u32[]{:S(2)}) collective-permute-start(f32[512,128]{1,0:T(8,128)S(1)} %collective-permute-done.11), channel_id=1, source_target_pairs={{0,2},{2,0},{4,6},{6,4},{8,10},{10,8},{12,14},{14,12},{1,3},{3,1},... | collective-permute-start | bytes 786440 | tf_op jit(solution)/shard_map/ppermute | solution.py:64
  35.2 1.6 %collective-permute-start.9 = (f32[512,128]{1,0:T(8,128)S(1)}, f32[512,128]{1,0:T(8,128)S(1)}, u32[]{:S(2)}, u32[]{:S(2)}) collective-permute-start(f32[512,128]{1,0:T(8,128)S(1)} %bitcast.149), channel_id=1, source_target_pairs={{0,1},{1,0},{2,3},{3,2},{4,5},{5,4},{6,7},{7,6},{8,9},{9,8},{10,11... | collective-permute-start | bytes 786440 | tf_op jit(solution)/shard_map/ppermute | solution.py:70
  35.4 1.8 %collective-permute-start.6 = (f32[512,128]{1,0:T(8,128)S(1)}, f32[512,128]{1,0:T(8,128)S(1)}, u32[]{:S(2)}, u32[]{:S(2)}) collective-permute-start(f32[512,128]{1,0:T(8,128)S(1)} %bitcast.148), channel_id=1, source_target_pairs={{0,1},{1,0},{2,3},{3,2},{4,5},{5,4},{6,7},{7,6},{8,9},{9,8},{10,11... | collective-permute-start | bytes 786440 | tf_op jit(solution)/shard_map/ppermute | solution.py:70
  40.1 1.6 %collective-permute-start.13 = (f32[512,128]{1,0:T(8,128)S(1)}, f32[512,128]{1,0:T(8,128)S(1)}, u32[]{:S(2)}, u32[]{:S(2)}) collective-permute-start(f32[512,128]{1,0:T(8,128)S(1)} %slice_add_fusion.1), channel_id=1, source_target_pairs={{0,1},{1,0},{2,3},{3,2},{4,5},{5,4},{6,7},{7,6},{8,9},{9,8},{10,11... | collective-permute-start | bytes 786440 | tf_op jit(solution)/shard_map/ppermute | solution.py:70
  42.2 4.4 %collective-permute-start.14 = (f32[512,128]{1,0:T(8,128)S(1)}, f32[512,128]{1,0:T(8,128)S(1)}, u32[]{:S(2)}, u32[]{:S(2)}) collective-permute-start(f32[512,128]{1,0:T(8,128)S(1)} %slice_add_fusion), channel_id=1, source_target_pairs={{0,1},{1,0},{2,3},{3,2},{4,5},{5,4},{6,7},{7,6},{8,9},{9,8},{10,11... | collective-permute-start | bytes 786440 | tf_op jit(solution)/shard_map/ppermute | solution.py:70
  42.6 9.6 %collective-permute-start.15 = (f32[512,128]{1,0:T(8,128)S(1)}, f32[512,128]{1,0:T(8,128)S(1)}, u32[]{:S(2)}, u32[]{:S(2)}) collective-permute-start(f32[512,128]{1,0:T(8,128)S(1)} %get-tuple-element.25), channel_id=1, source_target_pairs={{0,4},{2,6},{4,0},{6,2},{8,12},{10,14},{12,8},{14,10},{1,5},{3,7},... | collective-permute-start | bytes 786440 | tf_op jit(solution)/shard_map/ppermute | solution.py:61
  45.5 7.6 %collective-permute-start.17 = (f32[1,128]{1,0:T(1,128)S(1)}, f32[1,128]{1,0:T(1,128)S(1)}, u32[]{:S(2)}, u32[]{:S(2)}) collective-permute-start(f32[1,128]{1,0:T(1,128)S(1)} %bitcast.153), channel_id=1, source_target_pairs={{0,20},{2,22},{4,16},{6,18},{8,28},{10,30},{12,24},{14,26},{16,4},... | collective-permute-start | bytes 1544 | tf_op jit(solution)/shard_map/ppermute | solution.py:142
  46.9 6.1 %collective-permute-start.16 = (f32[1,128]{1,0:T(1,128)S(1)}, f32[1,128]{1,0:T(1,128)S(1)}, u32[]{:S(2)}, u32[]{:S(2)}) collective-permute-start(f32[1,128]{1,0:T(1,128)S(1)} %bitcast.150), channel_id=1, source_target_pairs={{0,16},{16,0},{1,17},{17,1},{2,18},{18,2},{3,19},{19,3},{4,20},{20... | collective-permute-start | bytes 1544 | tf_op jit(solution)/shard_map/ppermute | solution.py:67

commit v6 on v5

--- a/solution.py
+++ b/solution.py
@@ -102,7 +102,7 @@
     exponent, exponent_z, level = lookup(power, z), lookup(power, z ^ 1), lookup(prune_level, z) / 8.0
     one = lax.dynamic_slice_in_dim(side_raw, p * half, half, 0)
     one_y = along_y(one)
-    far_side = along_x(after(side_raw, far))
+    far_side = along_x(after(side_raw, far, two))
     three_y = along_y(after(three, two_y, exponent, exponent_z, level))
     near = both_layers(after(flow, own_y))
     near_x = both_layers(far)

time: 54.1 us -> 54.1 us (level)
  no operation moved by 1% of the time
where the time goes in v6:
time: 54.1 us; the launch traced here: 53.9 us
  waiting for transfers between devices  22.6 us (42%)
  starting transfers between devices  21.3 us (39%)
  other arithmetic  3.44 us (6%)
  local copies, waits for them, and re-layouts  3.27 us (6%)
  matrix products  3.03 us (6%)
    ppermute x4, waiting for transfers between devices, along_z(): return lax.ppermute(value, 'col', [(i, i ^ 2 * distance) for i in range(8)])  11.5 us
    ppermute x4, starting transfers between devices, along_z(): return lax.ppermute(value, 'col', [(i, i ^ 2 * distance) for i in range(8)])  10 us
    ppermute x4, waiting for transfers between devices, along_y(): return lax.ppermute(value, 'col', [(i, i ^ 1) for i in range(8)])  6.22 us
    ppermute x4, starting transfers between devices, along_y(): return lax.ppermute(value, 'col', [(i, i ^ 1) for i in range(8)])  5.2 us
    ppermute x3, starting transfers between devices, along_x(): return lax.ppermute(value, 'row', [(0, 1), (1, 0)])  3.57 us
    dot_general x5, matrix products, multiply(): jnp.dot(left, right, precision=lax.Precision.HIGH, preferred_element_type...  3.03 us
    ppermute x3, waiting for transfers between devices, along_x(): return lax.ppermute(value, 'row', [(0, 1), (1, 0)])  2.16 us
    ppermute x6, waiting for transfers between devices, across(): return lax.ppermute(value, 'layer', [(0, 1), (1, 0)])  1.91 us
  transfers between devices with their start and end apart: 18, of which 9 were waited for; matrix products, arithmetic and copies ran while one was open for 15% of the time, Pallas kernels for 0%

profile of v6, /device:TPU:0, one launch (start us, length us, event | category | flops | bytes accessed | tf_op | source)
XLA Modules:
  0.0 53.9 jit_solution(4355252250208045296)
XLA Ops:
  0.0 3.0 %collective-permute-start.1 = (f32[1024,128]{1,0:T(8,128)}, f32[1024,128]{1,0:T(8,128)S(1)}, u32[]{:S(2)}, u32[]{:S(2)}) collective-permute-start(f32[1024,128]{1,0:T(8,128)} %param.4), channel_id=1, source_target_pairs={{0,4},{2,6},{4,0},{6,2},{8,12},{10,14},{12,8},{14,10},{1,5},{3,7},... | collective-permute-start | bytes 1572872 | tf_op jit(solution)/shard_map/ppermute | solution.py:61
  3.0 1.1 %constant_dynamic-slice_fusion = (f32[512,128]{1,0:T(8,128)S(1)}, f32[512,128]{1,0:T(8,128)S(1)}) fusion(f32[1024,128]{1,0:T(8,128)} %param.4, s32[]{:T(128)S(6)} %select_n.151, s32[]{:T(128)S(6)} %select_n.133), kind=kLoop, calls=%fused_computation.128 | loop fusion | bytes 1048584 | tf_op jit(solution)/shard_map/dynamic_slice | solution.py:95
  4.1 1.6 %collective-permute-start = (f32[512,128]{1,0:T(8,128)S(1)}, f32[512,128]{1,0:T(8,128)S(1)}, u32[]{:S(2)}, u32[]{:S(2)}) collective-permute-start(f32[512,128]{1,0:T(8,128)S(1)} %get-tuple-element.12), channel_id=1, source_target_pairs={{0,2},{2,0},{4,6},{6,4},{8,10},{10,8},{12,14},{14,12},{1,3},{3,1},... | collective-permute-start | bytes 786440 | tf_op jit(solution)/shard_map/ppermute | solution.py:64
  5.7 2.6 %collective-permute-start.3 = (f32[512,128]{1,0:T(8,128)S(1)}, f32[512,128]{1,0:T(8,128)S(1)}, u32[]{:S(2)}, u32[]{:S(2)}) collective-permute-start(f32[512,128]{1,0:T(8,128)S(1)} %get-tuple-element.12), channel_id=1, source_target_pairs={{0,8},{2,10},{4,12},{6,14},{8,0},{10,2},{12,4},{14,6},{1,9},{3,11}... | collective-permute-start | bytes 786440 | tf_op jit(solution)/shard_map/ppermute | solution.py:61
  8.3 1.5 %collective-permute-start.7 = (f32[1024,128]{1,0:T(8,128)}, f32[1024,128]{1,0:T(8,128)S(1)}, u32[]{:S(2)}, u32[]{:S(2)}) collective-permute-start(f32[1024,128]{1,0:T(8,128)} %param.4), channel_id=1, source_target_pairs={{0,16},{16,0},{1,17},{17,1},{2,18},{18,2},{3,19},{19,3},{4,20},{20... | collective-permute-start | bytes 1572872 | tf_op jit(solution)/shard_map/ppermute | solution.py:67
  9.8 0.7 %fusion.77 = s32[4]{0:T(128)S(1)} fusion(s32[4,4]{1,0:T(4,128)} %param.5, s32[]{:T(128)S(6)} %select_n.139), kind=kLoop, calls=%fused_computation.149 | loop fusion | bytes 36 | tf_op jit(solution)/shard_map/mul | solution.py:116
  10.4 1.0 %fusion.74 = (s32[4]{0:T(128)S(1)}, s32[4]{0:T(128)S(1)}) fusion(s32[4,4]{1,0:T(4,128)} %param.5, s32[]{:T(128)S(6)} %select_n.140, s32[]{:T(128)S(6)} %select_n.141), kind=kLoop, calls=%fused_computation.142 | loop fusion | bytes 72 | tf_op jit(solution)/shard_map/dynamic_slice | solution.py:116
  11.5 0.7 %convert_element_type.16 = f32[4]{0:T(128)S(1)} convert(s32[4]{0:T(128)} %param.6) | non-fusion elementwise | flops 4 | bytes 32 | tf_op jit(solution)/shard_map/convert_element_type | solution.py:88
  12.2 0.7 %convert_element_type.14 = f32[4]{0:T(128)S(1)} convert(s32[4]{0:T(128)} %param.7) | non-fusion elementwise | flops 4 | bytes 32 | tf_op jit(solution)/shard_map/convert_element_type | solution.py:88
  12.8 0.1 select_reduce_fusion
  12.9 0.0 collective-permute-done
  12.9 1.5 %collective-permute-start.11 = (f32[512,128]{1,0:T(8,128)S(1)}, f32[512,128]{1,0:T(8,128)S(1)}, u32[]{:S(2)}, u32[]{:S(2)}) collective-permute-start(f32[512,128]{1,0:T(8,128)S(1)} %get-tuple-element.15), channel_id=1, source_target_pairs={{0,12},{2,14},{4,8},{6,10},{8,4},{10,6},{12,0},{14,2},{1,13},{3,15... | collective-permute-start | bytes 786440 | tf_op jit(solution)/shard_map/ppermute | solution.py:61
  14.4 6.8 %collective-permute-done.3 = f32[512,128]{1,0:T(8,128)S(1)} collective-permute-done((f32[512,128]{1,0:T(8,128)S(1)}, f32[512,128]{1,0:T(8,128)S(1)}, u32[]{:S(2)}, u32[]{:S(2)}) %collective-permute-start.3) | collective-permute-done | bytes 262176 | tf_op jit(solution)/shard_map/ppermute | solution.py:61
  21.2 1.5 %collective-permute-start.4 = (f32[512,128]{1,0:T(8,128)S(1)}, f32[512,128]{1,0:T(8,128)S(1)}, u32[]{:S(2)}, u32[]{:S(2)}) collective-permute-start(f32[512,128]{1,0:T(8,128)S(1)} %collective-permute-done.3), channel_id=1, source_target_pairs={{0,2},{2,0},{4,6},{6,4},{8,10},{10,8},{12,14},{14,12},{1,3},{3,1},... | collective-permute-start | bytes 786440 | tf_op jit(solution)/shard_map/ppermute | solution.py:64
  22.9 0.6 %collective-permute-start.2 = (f32[512,128]{1,0:T(8,128)S(1)}, f32[512,128]{1,0:T(8,128)S(1)}, u32[]{:S(2)}, u32[]{:S(2)}) collective-permute-start(f32[512,128]{1,0:T(8,128)S(1)} %get-tuple-element.27), channel_id=1, source_target_pairs={{0,2},{2,0},{4,6},{6,4},{8,10},{10,8},{12,14},{14,12},{1,3},{3,1},... | collective-permute-start | bytes 786440 | tf_op jit(solution)/shard_map/ppermute | solution.py:64
  23.4 1.5 %collective-permute-start.8 = (f32[1024,128]{1,0:T(8,128)S(1)}, f32[1024,128]{1,0:T(8,128)S(1)}, u32[]{:S(2)}, u32[]{:S(2)}) collective-permute-start(f32[1024,128]{1,0:T(8,128)S(1)} %collective-permute-done.1), channel_id=1, source_target_pairs={{0,16},{16,0},{1,17},{17,1},{2,18},{18,2},{3,19},{19,3},{4,20},{20... | collective-permute-start | bytes 1572872 | tf_op jit(solution)/shard_map/ppermute | solution.py:67
  25.0 0.0 copy-start
  25.0 0.1 collective-permute-start.10
  25.1 5.0 %collective-permute-done.4 = f32[512,128]{1,0:T(8,128)S(1)} collective-permute-done((f32[512,128]{1,0:T(8,128)S(1)}, f32[512,128]{1,0:T(8,128)S(1)}, u32[]{:S(2)}, u32[]{:S(2)}) %collective-permute-start.4) | collective-permute-done | bytes 262176 | tf_op jit(solution)/shard_map/ppermute | solution.py:64
  30.1 1.5 %collective-permute-start.12 = (f32[512,128]{1,0:T(8,128)S(1)}, f32[512,128]{1,0:T(8,128)S(1)}, u32[]{:S(2)}, u32[]{:S(2)}) collective-permute-start(f32[512,128]{1,0:T(8,128)S(1)} %collective-permute-done.11), channel_id=1, source_target_pairs={{0,2},{2,0},{4,6},{6,4},{8,10},{10,8},{12,14},{14,12},{1,3},{3,1},... | collective-permute-start | bytes 786440 | tf_op jit(solution)/shard_map/ppermute | solution.py:64
  31.6 1.3 %collective-permute-done.2 = f32[512,128]{1,0:T(8,128)S(1)} collective-permute-done((f32[512,128]{1,0:T(8,128)S(1)}, f32[512,128]{1,0:T(8,128)S(1)}, u32[]{:S(2)}, u32[]{:S(2)}) %collective-permute-start.2) | collective-permute-done | bytes 262176 | tf_op jit(solution)/shard_map/ppermute | solution.py:64
  32.9 2.2 %collective-permute-done.8 = f32[1024,128]{1,0:T(8,128)S(1)} collective-permute-done((f32[1024,128]{1,0:T(8,128)S(1)}, f32[1024,128]{1,0:T(8,128)S(1)}, u32[]{:S(2)}, u32[]{:S(2)}) %collective-permute-start.8) | collective-permute-done | bytes 524320 | tf_op jit(solution)/shard_map/ppermute | solution.py:67
  35.1 0.1 constant_dynamic-slice_fusion.7
  35.2 0.1 collective-permute-start.9
  35.4 0.6 %collective-permute-start.6 = (f32[512,128]{1,0:T(8,128)S(1)}, f32[512,128]{1,0:T(8,128)S(1)}, u32[]{:S(2)}, u32[]{:S(2)}) collective-permute-start(f32[512,128]{1,0:T(8,128)S(1)} %bitcast.148), channel_id=1, source_target_pairs={{0,1},{1,0},{2,3},{3,2},{4,5},{5,4},{6,7},{7,6},{8,9},{9,8},{10,11... | collective-permute-start | bytes 786440 | tf_op jit(solution)/shard_map/ppermute | solution.py:70
  35.9 0.8 %collective-permute-done.9 = f32[512,128]{1,0:T(8,128)S(1)} collective-permute-done((f32[512,128]{1,0:T(8,128)S(1)}, f32[512,128]{1,0:T(8,128)S(1)}, u32[]{:S(2)}, u32[]{:S(2)}) %collective-permute-start.9) | collective-permute-done | bytes 262176 | tf_op jit(solution)/shard_map/ppermute | solution.py:70
  36.8 0.1 maximum_bitcast_fusion.1
  36.9 0.3 collective-permute-done.6
  37.2 0.1 maximum_bitcast_fusion
  37.3 0.1 maximum_select_fusion
  37.4 0.4 broadcast_multiply_fusion
  37.8 0.2 dynamic-slice_bitcast_fusion
  38.2 1.5 %fusion = f32[512,512]{1,0:T(8,128)S(1)} fusion(f32[512,768]{1,0:T(8,128)S(1)} %constant_dynamic-update-slice_fusion, f32[256,128]{1,0:T(8,128)S(1)} %get-tuple-element.48, f32[256,128]{1,0:T(8,128)S(1)} %get-tuple-element.49, f32[256,128]{1,0:T(8,128)S(1)} %get-tuple-element.47, f32[256,128]{1,0:T(8,128)S(1)} %get-tuple-element.46, ...), kind=kOutput, calls=%fused_computation.1 | convolution fusion | flops 1212284928 | bytes 4194304 | tf_op jit(solution)/shard_map/dot_general | solution.py:8
  39.7 0.4 slice_add_fusion.1
  40.1 0.4 collective-permute-start.13
  40.5 0.4 fusion.39
  40.9 0.8 %collective-permute-done.13 = f32[512,128]{1,0:T(8,128)S(1)} collective-permute-done((f32[512,128]{1,0:T(8,128)S(1)}, f32[512,128]{1,0:T(8,128)S(1)}, u32[]{:S(2)}, u32[]{:S(2)}) %collective-permute-start.13) | collective-permute-done | bytes 262176 | tf_op jit(solution)/shard_map/ppermute | solution.py:70
  41.7 0.1 fusion.84
  41.8 0.4 slice_add_fusion
  42.2 0.4 collective-permute-start.14
  42.6 2.9 %collective-permute-start.15 = (f32[512,128]{1,0:T(8,128)S(1)}, f32[512,128]{1,0:T(8,128)S(1)}, u32[]{:S(2)}, u32[]{:S(2)}) collective-permute-start(f32[512,128]{1,0:T(8,128)S(1)} %get-tuple-element.25), channel_id=1, source_target_pairs={{0,4},{2,6},{4,0},{6,2},{8,12},{10,14},{12,8},{14,10},{1,5},{3,7},... | collective-permute-start | bytes 786440 | tf_op jit(solution)/shard_map/ppermute | solution.py:61
  45.5 1.0 %collective-permute-start.17 = (f32[1,128]{1,0:T(1,128)S(1)}, f32[1,128]{1,0:T(1,128)S(1)}, u32[]{:S(2)}, u32[]{:S(2)}) collective-permute-start(f32[1,128]{1,0:T(1,128)S(1)} %bitcast.153), channel_id=1, source_target_pairs={{0,20},{2,22},{4,16},{6,18},{8,28},{10,30},{12,24},{14,26},{16,4},... | collective-permute-start | bytes 1544 | tf_op jit(solution)/shard_map/ppermute | solution.py:142
  46.5 0.4 fusion.86
  46.9 0.6 %collective-permute-start.16 = (f32[1,128]{1,0:T(1,128)S(1)}, f32[1,128]{1,0:T(1,128)S(1)}, u32[]{:S(2)}, u32[]{:S(2)}) collective-permute-start(f32[1,128]{1,0:T(1,128)S(1)} %bitcast.150), channel_id=1, source_target_pairs={{0,16},{16,0},{1,17},{17,1},{2,18},{18,2},{3,19},{19,3},{4,20},{20... | collective-permute-start | bytes 1544 | tf_op jit(solution)/shard_map/ppermute | solution.py:67
  47.5 4.6 %collective-permute-done.15 = f32[512,128]{1,0:T(8,128)S(1)} collective-permute-done((f32[512,128]{1,0:T(8,128)S(1)}, f32[512,128]{1,0:T(8,128)S(1)}, u32[]{:S(2)}, u32[]{:S(2)}) %collective-permute-start.15) | collective-permute-done | bytes 262176 | tf_op jit(solution)/shard_map/ppermute | solution.py:61
  52.2 0.1 reduce_sum.58
  52.3 0.8 %collective-permute-done.17 = f32[1,128]{1,0:T(1,128)S(1)} collective-permute-done((f32[1,128]{1,0:T(1,128)S(1)}, f32[1,128]{1,0:T(1,128)S(1)}, u32[]{:S(2)}, u32[]{:S(2)}) %collective-permute-start.17) | collective-permute-done | bytes 544 | tf_op jit(solution)/shard_map/ppermute | solution.py:142
  53.1 0.9 %fusion.26 = f32[1024,128]{1,0:T(8,128)} fusion(f32[2,512,128]{2,1,0:T(8,128)S(1)} %fusion.24, f32[128]{0:T(128)S(1)} %broadcast_multiply_fusion.1, f32[128]{0:T(128)S(1)} %fusion.78), kind=kLoop, calls=%fused_computation.60 | loop fusion | flops 393216 | bytes 1049600 | tf_op jit(solution)/shard_map/max | solution.py:144
  (34 shorter events, 0.6 us)
Async XLA Ops:
  0.0 22.8 %collective-permute-start.1 = (f32[1024,128]{1,0:T(8,128)}, f32[1024,128]{1,0:T(8,128)S(1)}, u32[]{:S(2)}, u32[]{:S(2)}) collective-permute-start(f32[1024,128]{1,0:T(8,128)} %param.4), channel_id=1, source_target_pairs={{0,4},{2,6},{4,0},{6,2},{8,12},{10,14},{12,8},{14,10},{1,5},{3,7},... | collective-permute-start | bytes 1572872 | tf_op jit(solution)/shard_map/ppermute | solution.py:61
  4.1 8.8 %collective-permute-start = (f32[512,128]{1,0:T(8,128)S(1)}, f32[512,128]{1,0:T(8,128)S(1)}, u32[]{:S(2)}, u32[]{:S(2)}) collective-permute-start(f32[512,128]{1,0:T(8,128)S(1)} %get-tuple-element.12), channel_id=1, source_target_pairs={{0,2},{2,0},{4,6},{6,4},{8,10},{10,8},{12,14},{14,12},{1,3},{3,1},... | collective-permute-start | bytes 786440 | tf_op jit(solution)/shard_map/ppermute | solution.py:64
  5.7 15.6 %collective-permute-start.3 = (f32[512,128]{1,0:T(8,128)S(1)}, f32[512,128]{1,0:T(8,128)S(1)}, u32[]{:S(2)}, u32[]{:S(2)}) collective-permute-start(f32[512,128]{1,0:T(8,128)S(1)} %get-tuple-element.12), channel_id=1, source_target_pairs={{0,8},{2,10},{4,12},{6,14},{8,0},{10,2},{12,4},{14,6},{1,9},{3,11}... | collective-permute-start | bytes 786440 | tf_op jit(solution)/shard_map/ppermute | solution.py:61
  8.3 15.2 %collective-permute-start.7 = (f32[1024,128]{1,0:T(8,128)}, f32[1024,128]{1,0:T(8,128)S(1)}, u32[]{:S(2)}, u32[]{:S(2)}) collective-permute-start(f32[1024,128]{1,0:T(8,128)} %param.4), channel_id=1, source_target_pairs={{0,16},{16,0},{1,17},{17,1},{2,18},{18,2},{3,19},{19,3},{4,20},{20... | collective-permute-start | bytes 1572872 | tf_op jit(solution)/shard_map/ppermute | solution.py:67
  12.9 17.2 %collective-permute-start.11 = (f32[512,128]{1,0:T(8,128)S(1)}, f32[512,128]{1,0:T(8,128)S(1)}, u32[]{:S(2)}, u32[]{:S(2)}) collective-permute-start(f32[512,128]{1,0:T(8,128)S(1)} %get-tuple-element.15), channel_id=1, source_target_pairs={{0,12},{2,14},{4,8},{6,10},{8,4},{10,6},{12,0},{14,2},{1,13},{3,15... | collective-permute-start | bytes 786440 | tf_op jit(solution)/shard_map/ppermute | solution.py:61
  21.2 8.8 %collective-permute-start.4 = (f32[512,128]{1,0:T(8,128)S(1)}, f32[512,128]{1,0:T(8,128)S(1)}, u32[]{:S(2)}, u32[]{:S(2)}) collective-permute-start(f32[512,128]{1,0:T(8,128)S(1)} %collective-permute-done.3), channel_id=1, source_target_pairs={{0,2},{2,0},{4,6},{6,4},{8,10},{10,8},{12,14},{14,12},{1,3},{3,1},... | collective-permute-start | bytes 786440 | tf_op jit(solution)/shard_map/ppermute | solution.py:64
  22.9 10.0 %collective-permute-start.2 = (f32[512,128]{1,0:T(8,128)S(1)}, f32[512,128]{1,0:T(8,128)S(1)}, u32[]{:S(2)}, u32[]{:S(2)}) collective-permute-start(f32[512,128]{1,0:T(8,128)S(1)} %get-tuple-element.27), channel_id=1, source_target_pairs={{0,2},{2,0},{4,6},{6,4},{8,10},{10,8},{12,14},{14,12},{1,3},{3,1},... | collective-permute-start | bytes 786440 | tf_op jit(solution)/shard_map/ppermute | solution.py:64
  23.4 11.6 %collective-permute-start.8 = (f32[1024,128]{1,0:T(8,128)S(1)}, f32[1024,128]{1,0:T(8,128)S(1)}, u32[]{:S(2)}, u32[]{:S(2)}) collective-permute-start(f32[1024,128]{1,0:T(8,128)S(1)} %collective-permute-done.1), channel_id=1, source_target_pairs={{0,16},{16,0},{1,17},{17,1},{2,18},{18,2},{3,19},{19,3},{4,20},{20... | collective-permute-start | bytes 1572872 | tf_op jit(solution)/shard_map/ppermute | solution.py:67
  25.0 10.1 %copy-start = (f32[1024,128]{1,0:T(8,128)S(1)}, f32[1024,128]{1,0:T(8,128)}, u32[]{:S(2)}) copy-start(f32[1024,128]{1,0:T(8,128)} %param.4) | copy-start | bytes 1572868
  25.0 10.3 %collective-permute-start.10 = (f32[512,128]{1,0:T(8,128)S(1)}, f32[512,128]{1,0:T(8,128)S(1)}, u32[]{:S(2)}, u32[]{:S(2)}) collective-permute-start(f32[512,128]{1,0:T(8,128)S(1)} %bitcast.142), channel_id=1, source_target_pairs={{0,1},{1,0},{2,3},{3,2},{4,5},{5,4},{6,7},{7,6},{8,9},{9,8},{10,11... | collective-permute-start | bytes 786440 | tf_op jit(solution)/shard_map/ppermute | solution.py:70
  30.1 5.3 %collective-permute-start.5 = (f32[512,128]{1,0:T(8,128)S(1)}, f32[512,128]{1,0:T(8,128)S(1)}, u32[]{:S(2)}, u32[]{:S(2)}) collective-permute-start(f32[512,128]{1,0:T(8,128)S(1)} %bitcast.143), channel_id=1, source_target_pairs={{0,1},{1,0},{2,3},{3,2},{4,5},{5,4},{6,7},{7,6},{8,9},{9,8},{10,11... | collective-permute-start | bytes 786440 | tf_op jit(solution)/shard_map/ppermute | solution.py:70
  30.1 9.6 %collective-permute-start.12 = (f32[512,128]{1,0:T(8,128)S(1)}, f32[512,128]{1,0:T(8,128)S(1)}, u32[]{:S(2)}, u32[]{:S(2)}) collective-permute-start(f32[512,128]{1,0:T(8,128)S(1)} %collective-permute-done.11), channel_id=1, source_target_pairs={{0,2},{2,0},{4,6},{6,4},{8,10},{10,8},{12,14},{14,12},{1,3},{3,1},... | collective-permute-start | bytes 786440 | tf_op jit(solution)/shard_map/ppermute | solution.py:64
  35.2 1.6 %collective-permute-start.9 = (f32[512,128]{1,0:T(8,128)S(1)}, f32[512,128]{1,0:T(8,128)S(1)}, u32[]{:S(2)}, u32[]{:S(2)}) collective-permute-start(f32[512,128]{1,0:T(8,128)S(1)} %bitcast.149), channel_id=1, source_target_pairs={{0,1},{1,0},{2,3},{3,2},{4,5},{5,4},{6,7},{7,6},{8,9},{9,8},{10,11... | collective-permute-start | bytes 786440 | tf_op jit(solution)/shard_map/ppermute | solution.py:70
  35.4 1.8 %collective-permute-start.6 = (f32[512,128]{1,0:T(8,128)S(1)}, f32[512,128]{1,0:T(8,128)S(1)}, u32[]{:S(2)}, u32[]{:S(2)}) collective-permute-start(f32[512,128]{1,0:T(8,128)S(1)} %bitcast.148), channel_id=1, source_target_pairs={{0,1},{1,0},{2,3},{3,2},{4,5},{5,4},{6,7},{7,6},{8,9},{9,8},{10,11... | collective-permute-start | bytes 786440 | tf_op jit(solution)/shard_map/ppermute | solution.py:70
  40.1 1.6 %collective-permute-start.13 = (f32[512,128]{1,0:T(8,128)S(1)}, f32[512,128]{1,0:T(8,128)S(1)}, u32[]{:S(2)}, u32[]{:S(2)}) collective-permute-start(f32[512,128]{1,0:T(8,128)S(1)} %slice_add_fusion.1), channel_id=1, source_target_pairs={{0,1},{1,0},{2,3},{3,2},{4,5},{5,4},{6,7},{7,6},{8,9},{9,8},{10,11... | collective-permute-start | bytes 786440 | tf_op jit(solution)/shard_map/ppermute | solution.py:70
  42.2 4.4 %collective-permute-start.14 = (f32[512,128]{1,0:T(8,128)S(1)}, f32[512,128]{1,0:T(8,128)S(1)}, u32[]{:S(2)}, u32[]{:S(2)}) collective-permute-start(f32[512,128]{1,0:T(8,128)S(1)} %slice_add_fusion), channel_id=1, source_target_pairs={{0,1},{1,0},{2,3},{3,2},{4,5},{5,4},{6,7},{7,6},{8,9},{9,8},{10,11... | collective-permute-start | bytes 786440 | tf_op jit(solution)/shard_map/ppermute | solution.py:70
  42.6 9.6 %collective-permute-start.15 = (f32[512,128]{1,0:T(8,128)S(1)}, f32[512,128]{1,0:T(8,128)S(1)}, u32[]{:S(2)}, u32[]{:S(2)}) collective-permute-start(f32[512,128]{1,0:T(8,128)S(1)} %get-tuple-element.25), channel_id=1, source_target_pairs={{0,4},{2,6},{4,0},{6,2},{8,12},{10,14},{12,8},{14,10},{1,5},{3,7},... | collective-permute-start | bytes 786440 | tf_op jit(solution)/shard_map/ppermute | solution.py:61
  45.5 7.6 %collective-permute-start.17 = (f32[1,128]{1,0:T(1,128)S(1)}, f32[1,128]{1,0:T(1,128)S(1)}, u32[]{:S(2)}, u32[]{:S(2)}) collective-permute-start(f32[1,128]{1,0:T(1,128)S(1)} %bitcast.153), channel_id=1, source_target_pairs={{0,20},{2,22},{4,16},{6,18},{8,28},{10,30},{12,24},{14,26},{16,4},... | collective-permute-start | bytes 1544 | tf_op jit(solution)/shard_map/ppermute | solution.py:142
  46.9 6.1 %collective-permute-start.16 = (f32[1,128]{1,0:T(1,128)S(1)}, f32[1,128]{1,0:T(1,128)S(1)}, u32[]{:S(2)}, u32[]{:S(2)}) collective-permute-start(f32[1,128]{1,0:T(1,128)S(1)} %bitcast.150), channel_id=1, source_target_pairs={{0,16},{16,0},{1,17},{17,1},{2,18},{18,2},{3,19},{19,3},{4,20},{20... | collective-permute-start | bytes 1544 | tf_op jit(solution)/shard_map/ppermute | solution.py:67
